TPU v7x, 512 devices: a whole 4x8x8 slice. The times are simulated.
512 devices in a mesh: gx: 32 (over y, z_lo), gy: 16 (over z_hi, x, core).
Axes of the slice: x: 4, y: 8, z: 8 (z_hi: 2, z_lo: 4; z = z_hi * 4 + z_lo), core: 2. Of those that a mesh axis runs over, the one named last changes fastest.
Arguments:
- local_residual: float32 [512, 256, 64], P('gx', 'gy'), may hold values from -6 to 6
- lengths: float32 [3, 64, 32, 8], P(None, 'gx', 'gy'), may hold values from 0.5 to 2
- coarse_inverse: bfloat16 [32, 512, 512], P('gx', 'gy'), may hold values from -0.026516504 to 0.2265165
Outputs:
- preconditioned: float32 [512, 256, 64], P('gx', 'gy')
- mid_result: float32 [256, 128, 32], P('gx', 'gy')
- coarse_correction: float32 [64, 32, 8], P('gx', 'gy')
All inputs are finite; a program needn't handle non-finite values.
Results may differ from a plain program's by a relative error of at most 0.00315.
Values may be sent and summed in bfloat16 or wider, within the bound.
A program may use at most 128 MiB of HBM per device.

v0:
```python
import math

import jax
import jax.numpy as jnp
import numpy as np
from jax import lax
from jax.sharding import PartitionSpec as P

ORDER = 7
MID_ORDER = 3


PRECISE = lax.Precision.HIGHEST


def extended_2(cells, sides, width):
    for axis, dim in sides:
        count = lax.axis_size(axis)
        head = lax.slice_in_dim(cells, 0, width, axis=dim)
        tail = lax.slice_in_dim(cells, cells.shape[dim] - width, cells.shape[dim], axis=dim)
        cells = jnp.concatenate(
            [
                lax.ppermute(tail, axis, [(i, (i + 1) % count) for i in range(count)]),
                cells,
                lax.ppermute(head, axis, [((i + 1) % count, i) for i in range(count)]),
            ],
            axis=dim,
        )
    return cells


def from_behind(x, axis, by):
    devices = lax.axis_size(axis)
    return lax.ppermute(x, axis, [(i, (i + by) % devices) for i in range(devices)])


def from_behind_2(value, axis, steps):
    count = lax.axis_size(axis)
    initial, last = (max(0, -steps), min(count, count - steps))
    return lax.ppermute(value, axis, [(source, source + steps) for source in range(initial, last)])


def legendre_pair(order, point):
    older = 1.0
    newer = point
    for degree in range(2, order + 1):
        nexter = ((2 * degree - 1) * point * newer - (degree - 1) * older) / degree
        older = newer
        newer = nexter
    return (newer, older)


def jacobi_eigen(matrix):
    count_n = len(matrix)
    work = [list(row_items) for row_items in matrix]
    vectors = [
        [1.0 if row_at == col_at else 0.0 for col_at in range(count_n)] for row_at in range(count_n)
    ]
    for sweep_count in range(60):
        for lower_at in range(count_n):
            for upper_at in range(lower_at + 1, count_n):
                off_value = work[lower_at][upper_at]
                if abs(off_value) < 1e-18 * (
                    abs(work[lower_at][lower_at]) + abs(work[upper_at][upper_at])
                ):
                    continue
                angle_ratio = (work[upper_at][upper_at] - work[lower_at][lower_at]) / (
                    2.0 * off_value
                )
                sign_value = 1.0 if angle_ratio >= 0 else -1.0
                tangent = sign_value / (
                    abs(angle_ratio) + math.sqrt(angle_ratio * angle_ratio + 1.0)
                )
                cosine = 1.0 / math.sqrt(tangent * tangent + 1.0)
                sine_value = tangent * cosine
                for other_at in range(count_n):
                    left_value = work[other_at][lower_at]
                    right_value = work[other_at][upper_at]
                    work[other_at][lower_at] = cosine * left_value - sine_value * right_value
                    work[other_at][upper_at] = sine_value * left_value + cosine * right_value
                for other_at in range(count_n):
                    left_value = work[lower_at][other_at]
                    right_value = work[upper_at][other_at]
                    work[lower_at][other_at] = cosine * left_value - sine_value * right_value
                    work[upper_at][other_at] = sine_value * left_value + cosine * right_value
                for other_at in range(count_n):
                    left_value = vectors[other_at][lower_at]
                    right_value = vectors[other_at][upper_at]
                    vectors[other_at][lower_at] = cosine * left_value - sine_value * right_value
                    vectors[other_at][upper_at] = sine_value * left_value + cosine * right_value
    eigen_list = [work[row_at][row_at] for row_at in range(count_n)]
    ordering = sorted(range(count_n), key=lambda index_at: eigen_list[index_at])
    rates = [eigen_list[index_at] for index_at in ordering]
    basis = [[vectors[row_at][index_at] for index_at in ordering] for row_at in range(count_n)]
    return (rates, basis)


def gll_tables(order):
    point_count = order + 1
    node_list = []
    for node_at in range(point_count):
        point = math.cos(math.pi * node_at / order)
        for newton_step in range(100):
            top_value, lower_value = legendre_pair(order, point)
            point = point - (point * top_value - lower_value) / ((order + 1) * top_value)
        node_list.append(point)
    node_list = node_list[::-1]
    node_list[0] = -1.0
    node_list[-1] = 1.0
    values = [legendre_pair(order, point)[0] for point in node_list]
    weight_list = [2.0 / (order * (order + 1) * value_at**2) for value_at in values]
    derivative = [[0.0] * point_count for row_at in range(point_count)]
    for row_at in range(point_count):
        for col_at in range(point_count):
            if row_at != col_at:
                derivative[row_at][col_at] = values[row_at] / (
                    values[col_at] * (node_list[row_at] - node_list[col_at])
                )
    derivative[0][0] = -order * (order + 1) / 4.0
    derivative[order][order] = order * (order + 1) / 4.0
    stiff_list = [
        [
            sum(
                (
                    derivative[inner_at][row_at]
                    * weight_list[inner_at]
                    * derivative[inner_at][col_at]
                    for inner_at in range(point_count)
                )
            )
            for col_at in range(point_count)
        ]
        for row_at in range(point_count)
    ]
    extent = 3 * order + 1
    big_stiff = [[0.0] * extent for row_at in range(extent)]
    big_mass = [0.0] * extent
    for offset_at in (0, order, 2 * order):
        for row_at in range(point_count):
            big_mass[offset_at + row_at] += weight_list[row_at]
            for col_at in range(point_count):
                big_stiff[offset_at + row_at][offset_at + col_at] += stiff_list[row_at][col_at]
    chosen = list(range(order - 1, 2 * order + 2))
    root_mass = [1.0 / math.sqrt(big_mass[index_at]) for index_at in chosen]
    scaled = [
        [
            root_mass[row_at] * big_stiff[chosen[row_at]][chosen[col_at]] * root_mass[col_at]
            for col_at in range(len(chosen))
        ]
        for row_at in range(len(chosen))
    ]
    rates, basis = jacobi_eigen(scaled)
    eigen_basis = [
        [root_mass[row_at] * basis[row_at][col_at] for col_at in range(len(chosen))]
        for row_at in range(len(chosen))
    ]
    return (
        np.array(node_list),
        np.array(weight_list),
        np.array(stiff_list),
        np.array(eigen_basis),
        np.array(rates),
    )


def interp_table(fine_nodes, coarse_nodes):
    coarse_count = len(coarse_nodes)
    columns = []
    for column in range(coarse_count):
        factors_list = [
            (fine_nodes - coarse_nodes[other_node])
            / (coarse_nodes[column] - coarse_nodes[other_node])
            for other_node in range(coarse_count)
            if other_node != column
        ]
        columns.append(np.prod(np.stack(factors_list), axis=0))
    return np.stack(columns, axis=1)


def element_factors(lengths):
    first_len, second_len, third_len = (lengths[0], lengths[1], lengths[2])
    return jnp.stack(
        [
            second_len * third_len / (2.0 * first_len),
            first_len * third_len / (2.0 * second_len),
            first_len * second_len / (2.0 * third_len),
        ]
    ).reshape(3, -1)


def to_elements(values_in, points):
    size_x, size_y, size_z = values_in.shape
    blocks = values_in.reshape(
        size_x // points, points, size_y // points, points, size_z // points, points
    )
    return blocks.transpose(1, 3, 5, 0, 2, 4).reshape(points, points, points, -1)


def to_field(elements, counts):
    points = elements.shape[0]
    blocks = elements.reshape(points, points, points, counts[0], counts[1], counts[2])
    return blocks.transpose(3, 0, 4, 1, 5, 2).reshape(
        counts[0] * points, counts[1] * points, counts[2] * points
    )


def face_masks(extent, points, offset):
    position = (np.arange(extent) - offset) % points
    return ((position == 0).astype(np.float32), (position == points - 1).astype(np.float32))


def assemble(padded, points, offset):
    lower_mask, upper_mask = face_masks(padded.shape[0], points, offset)
    zero_slab = jnp.zeros_like(padded[:1])
    previous = jnp.concatenate([zero_slab, padded[:-1]], 0)
    following = jnp.concatenate([padded[1:], zero_slab], 0)
    summed = padded + lower_mask[:, None, None] * previous + upper_mask[:, None, None] * following
    lower_mask, upper_mask = face_masks(summed.shape[1], points, offset)
    zero_slab = jnp.zeros_like(summed[:, :1])
    previous = jnp.concatenate([zero_slab, summed[:, :-1]], 1)
    following = jnp.concatenate([summed[:, 1:], zero_slab], 1)
    summed = summed + lower_mask[None, :, None] * previous + upper_mask[None, :, None] * following
    lower_mask, upper_mask = face_masks(summed.shape[2], points, 0)
    return summed + lower_mask * jnp.roll(summed, 1, 2) + upper_mask * jnp.roll(summed, -1, 2)


def extend(assembled, points, start, counts):
    first_len, second_len, third_len = counts
    left_part = assembled[start - 2 : start - 2 + first_len * points : points]
    own_part = assembled[start : start + first_len * points].reshape(
        (first_len, points) + assembled.shape[1:]
    )
    right_part = assembled[start + points + 1 : start + points + 1 + first_len * points : points]
    section_one = jnp.concatenate([left_part[:, None], own_part, right_part[:, None]], 1)
    left_part = section_one[:, :, start - 2 : start - 2 + second_len * points : points]
    own_part = section_one[:, :, start : start + second_len * points].reshape(
        section_one.shape[:2] + (second_len, points) + section_one.shape[3:]
    )
    right_part = section_one[
        :, :, start + points + 1 : start + points + 1 + second_len * points : points
    ]
    section_two = jnp.concatenate(
        [left_part[:, :, :, None], own_part, right_part[:, :, :, None]], 3
    )
    own_part = section_two.reshape(section_two.shape[:4] + (third_len, points))
    left_part = jnp.roll(own_part[..., points - 2], 1, 4)
    right_part = jnp.roll(own_part[..., 1], -1, 4)
    section_three = jnp.concatenate([left_part[..., None], own_part, right_part[..., None]], 5)
    extent = points + 2
    return section_three.transpose(1, 3, 5, 0, 2, 4).reshape(extent, extent, extent, -1)


def fast_solve(extended, eigen_basis, eigen_rates, factors):
    basis_table = jnp.asarray(eigen_basis, jnp.float32)
    rate_table = jnp.asarray(eigen_rates, jnp.float32)
    modal = jnp.einsum("ai,abcE->ibcE", basis_table, extended, precision=PRECISE)
    modal = jnp.einsum("bj,ibcE->ijcE", basis_table, modal, precision=PRECISE)
    modal = jnp.einsum("ck,ijcE->ijkE", basis_table, modal, precision=PRECISE)
    divisor = (
        factors[0] * rate_table[:, None, None, None]
        + factors[1] * rate_table[None, :, None, None]
        + factors[2] * rate_table[None, None, :, None]
    )
    modal = modal / divisor
    inner_rows = basis_table[1:-1]
    result = jnp.einsum("ai,ijkE->ajkE", inner_rows, modal, precision=PRECISE)
    result = jnp.einsum("bj,ajkE->abkE", inner_rows, result, precision=PRECISE)
    return jnp.einsum("ck,abkE->abcE", inner_rows, result, precision=PRECISE)


def schwarz_local(padded, points, counts, tables, factors):
    assembled = assemble(padded, points, 2)
    extended = extend(assembled, points, 2, counts)
    return fast_solve(extended, tables[3], tables[4], factors)


def apply_stiffness(values, tables, factors):
    matrix = jnp.asarray(tables[2], jnp.float32)
    mass_diag = jnp.asarray(tables[1], jnp.float32)
    along_x = (
        jnp.einsum("ai,ijkE->ajkE", matrix, values, precision=PRECISE)
        * (mass_diag[None, :, None, None] * mass_diag[None, None, :, None])
        * factors[0]
    )
    along_y = (
        jnp.einsum("bj,ijkE->ibkE", matrix, values, precision=PRECISE)
        * (mass_diag[:, None, None, None] * mass_diag[None, None, :, None])
        * factors[1]
    )
    along_z = (
        jnp.einsum("ck,ijkE->ijcE", matrix, values, precision=PRECISE)
        * (mass_diag[:, None, None, None] * mass_diag[None, :, None, None])
        * factors[2]
    )
    return along_x + along_y + along_z


def restrict(values, lagrange):
    matrix = jnp.asarray(lagrange, jnp.float32)
    result = jnp.einsum("ia,ijkE->ajkE", matrix, values, precision=PRECISE)
    result = jnp.einsum("jb,ajkE->abkE", matrix, result, precision=PRECISE)
    return jnp.einsum("kc,abkE->abcE", matrix, result, precision=PRECISE)


def prolong(values, lagrange):
    matrix = jnp.asarray(lagrange, jnp.float32)
    result = jnp.einsum("ai,ijkE->ajkE", matrix, values, precision=PRECISE)
    result = jnp.einsum("bj,ajkE->abkE", matrix, result, precision=PRECISE)
    return jnp.einsum("ck,abkE->abcE", matrix, result, precision=PRECISE)


def average_weight(extent, points, at_bottom, at_top, number_type):

    def line_weight(count_in):
        position = np.arange(count_in) % points
        return np.where((position == 0) | (position == points - 1), 0.5, 1.0)

    across = jnp.asarray(line_weight(extent[1]), number_type)
    across = (
        across.at[0].set(jnp.where(at_bottom, 1.0, 0.5)).at[-1].set(jnp.where(at_top, 1.0, 0.5))
    )
    return (
        jnp.asarray(line_weight(extent[0]), number_type)[:, None, None]
        * across[None, :, None]
        * jnp.asarray(line_weight(extent[2]), number_type)[None, None, :]
    )


def corner_spread(vertex, counts):
    stacked = jnp.stack(
        [
            jnp.stack(
                [
                    jnp.stack(
                        [
                            vertex[
                                step_x : step_x + counts[0],
                                step_y : step_y + counts[1],
                                step_z : step_z + counts[2],
                            ]
                            for step_z in (0, 1)
                        ]
                    )
                    for step_y in (0, 1)
                ]
            )
            for step_x in (0, 1)
        ]
    )
    return stacked.reshape(2, 2, 2, -1)


def clear_walls(padded, rim_depth):
    row_index = jnp.arange(padded.shape[1])
    position = lax.axis_index("gy")
    final_index = lax.axis_size("gy") - 1
    blocked = (row_index < rim_depth) & (position == 0) | (
        row_index >= padded.shape[1] - rim_depth
    ) & (position == final_index)
    return jnp.where(blocked[None, :, None], jnp.zeros_like(padded), padded)


def smooth_fine(values_in, counts, factors, weight, tables):
    points = ORDER + 1
    padded = clear_walls(extended_2(values_in, (("gx", 0), ("gy", 1)), 2), 2)
    local_part = schwarz_local(padded, points, counts, tables, factors)
    copies = clear_walls(extended_2(to_field(local_part, counts), (("gx", 0), ("gy", 1)), 1), 1)
    summed = assemble(copies, points, 1)[1:-1, 1:-1]
    return summed * weight


def smooth_mid(values_in, counts, factors, weight, tables):
    points = MID_ORDER + 1
    padded = clear_walls(extended_2(values_in, (("gx", 0), ("gy", 1)), 2), 2)
    local_part = schwarz_local(padded, points, counts, tables, factors)
    copies = clear_walls(extended_2(to_field(local_part, counts), (("gx", 0), ("gy", 1)), 1), 1)
    summed = assemble(copies, points, 1)[1:-1, 1:-1]
    return summed * weight


def shards(local_residual, lengths, coarse_inverse):
    fine_points = ORDER + 1
    mid_points = MID_ORDER + 1
    fine_tables = gll_tables(ORDER)
    mid_tables = gll_tables(MID_ORDER)
    low_tables = gll_tables(1)
    down_fine = interp_table(fine_tables[0], mid_tables[0])
    down_mid = interp_table(mid_tables[0], low_tables[0])
    counts = (lengths.shape[1], lengths.shape[2], lengths.shape[3])
    factors = element_factors(lengths)
    position = lax.axis_index("gy")
    at_bottom = position == 0
    at_top = position == lax.axis_size("gy") - 1
    weight_fine = average_weight(
        local_residual.shape, fine_points, at_bottom, at_top, local_residual.dtype
    )
    weight_mid = average_weight(
        (counts[0] * mid_points, counts[1] * mid_points, counts[2] * mid_points),
        mid_points,
        at_bottom,
        at_top,
        local_residual.dtype,
    )
    first_fine = to_elements(
        smooth_fine(local_residual, counts, factors, weight_fine, fine_tables), fine_points
    )
    local_elements = to_elements(local_residual, fine_points)
    residual_fine = local_elements - apply_stiffness(first_fine, fine_tables, factors)
    residual_mid = restrict(residual_fine, down_fine)
    first_mid = to_elements(
        smooth_mid(to_field(residual_mid, counts), counts, factors, weight_mid, mid_tables),
        mid_points,
    )
    residual_low = restrict(
        residual_mid - apply_stiffness(first_mid, mid_tables, factors), down_mid
    )
    corners = residual_low.reshape(2, 2, 2, counts[0], counts[1], counts[2])
    z_summed = corners[:, :, 0] + jnp.roll(corners[:, :, 1], 1, 4)
    from_left = from_behind(z_summed[1][:, -1], "gx", 1)
    x_summed = z_summed[0] + jnp.concatenate([from_left[:, None], z_summed[1][:, :-1]], 1)
    inverse_rows = coarse_inverse[0]
    from_below = from_behind_2(x_summed[1][:, -1], "gy", 1)
    coarse_residual = x_summed[0] + jnp.concatenate([from_below[:, None], x_summed[1][:, :-1]], 1)
    shard_piece = jax.tree.map(
        lambda part: lax.all_gather(part, "gy", axis=0, tiled=True),
        coarse_residual.astype(jnp.bfloat16).reshape(-1),
    )
    columns = lax.slice_in_dim(inverse_rows, 0, shard_piece.shape[0], axis=1)
    solved = jnp.zeros((inverse_rows.shape[0],), jnp.float32) + jnp.dot(
        columns, shard_piece, preferred_element_type=jnp.float32
    )
    correction = solved.reshape(counts[0], counts[1], counts[2])
    with_x = jnp.concatenate([correction, from_behind(correction[:1], "gx", -1)], 0)
    with_y = jnp.concatenate([with_x, from_behind_2(with_x[:, :1], "gy", -1)], 1)
    with_z = jnp.concatenate([with_y, with_y[:, :, :1]], 2)
    low_values = corner_spread(with_z, counts)
    mid_update = first_mid + prolong(low_values, down_mid)
    post_mid = smooth_mid(
        to_field(residual_mid - apply_stiffness(mid_update, mid_tables, factors), counts),
        counts,
        factors,
        weight_mid,
        mid_tables,
    )
    mid_result = mid_update + to_elements(post_mid, mid_points)
    fine_update = first_fine + prolong(mid_result, down_fine)
    post_fine = smooth_fine(
        to_field(local_elements - apply_stiffness(fine_update, fine_tables, factors), counts),
        counts,
        factors,
        weight_fine,
        fine_tables,
    )
    preconditioned = to_field(fine_update, counts) + post_fine
    return (preconditioned, to_field(mid_result, counts), correction)


def solution(mesh):
    in_specs = (P("gx", "gy", None), P(None, "gx", "gy", None), P("gx", "gy", None))
    out_specs = (P("gx", "gy", None), P("gx", "gy", None), P("gx", "gy", None))
    return jax.shard_map(shards, mesh=mesh, in_specs=in_specs, out_specs=out_specs, check_vma=False)
```

profile of v0, /device:TPU:7, one launch (start us, length us, event | category | flops | bytes accessed | tf_op | source)
XLA Modules:
  0.0 402.0 jit_solution(16662646290618415520)
XLA Ops:
  1.4 4.0 collective-permute-start
  5.4 8.4 %collective-permute-start.1 = (f32[2,16,64]{2,1,0:T(8,128)S(1)}, f32[2,16,64]{2,1,0:T(8,128)S(1)}, u32[]{:S(2)}, u32[]{:S(2)}) collective-permute-start(f32[2,16,64]{2,1,0:T(8,128)S(1)} %get-tuple-element.109), channel_id=1, source_target_pairs={{16,0},{32,16},{48,32},{64,48},{80,64},{96,80},{112,96},{128,112},... | collective-permute-start | bytes 24584 | tf_op jit(solution)/shard_map/ppermute | solution.py:25
  21.8 2.9 collective-permute-start.3
  24.6 8.7 %collective-permute-start.2 = (f32[20,2,64]{2,1,0:T(2,128)S(1)}, f32[20,2,64]{2,1,0:T(2,128)S(1)}, u32[]{:S(2)}, u32[]{:S(2)}) collective-permute-start(f32[20,2,64]{2,1,0:T(2,128)S(1)} %get-tuple-element.97), channel_id=1, source_target_pairs={{0,1},{1,2},{2,3},{3,4},{4,5},{5,6},{6,7},{7,8},{8,9},{9,10},{10,1... | collective-permute-start | bytes 30728 | tf_op jit(solution)/shard_map/ppermute | solution.py:23
  36.6 2.1 fusion.121
  38.6 2.0 copy.217
  40.7 2.0 copy.219
  42.7 3.4 copy.216
  46.9 4.1 %copy.218 = f32[2,10,2,10,8,1]{5,4,3,2,1,0:T(8,128)} copy(f32[2,10,2,10,8,1]{3,4,5,2,1,0:T(8,128)} %maximum_bitcast_fusion.4) | data formatting | bytes 25600 | tf_op jit(solution)/shard_map/broadcast_in_dim | solution.py:248
  50.9 3.5 maximum_bitcast_fusion
  54.5 4.4 %copy.343 = f32[10,10,10,2,2,8]{5,4,3,0,2,1:T(2,128)S(1)} copy(f32[10,10,10,2,2,8]{2,5,1,4,0,3:T(8,128)} %maximum_bitcast_fusion) | data formatting | bytes 256000 | tf_op jit(solution)/shard_map/reshape | solution.py:250
  67.5 1.9 collective-permute-start.4
  69.5 7.3 %collective-permute-start.5 = (f32[1,16,64]{2,1,0:T(8,128)S(1)}, f32[1,16,64]{2,1,0:T(8,128)S(1)}, u32[]{:S(2)}, u32[]{:S(2)}) collective-permute-start(f32[1,16,64]{2,1,0:T(8,128)S(1)} %get-tuple-element.107), channel_id=1, source_target_pairs={{16,0},{32,16},{48,32},{64,48},{80,64},{96,80},{112,96},{128,112},... | collective-permute-start | bytes 12296 | tf_op jit(solution)/shard_map/ppermute | solution.py:25
  77.6 1.9 collective-permute-start.7
  79.5 11.4 %collective-permute-start.6 = (f32[18,1,64]{2,1,0:T(1,128)S(1)}, f32[18,1,64]{2,1,0:T(1,128)S(1)}, u32[]{:S(2)}, u32[]{:S(2)}) collective-permute-start(f32[18,1,64]{2,1,0:T(1,128)S(1)} %get-tuple-element.101), channel_id=1, source_target_pairs={{0,1},{1,2},{2,3},{3,4},{4,5},{5,6},{6,7},{7,8},{8,9},{9,10},{10,1... | collective-permute-start | bytes 13832 | tf_op jit(solution)/shard_map/ppermute | solution.py:23
  91.3 2.0 copy.229
  100.5 1.9 collective-permute-start.8
  102.5 7.8 %collective-permute-start.9 = (f32[2,8,32]{2,1,0:T(8,128)S(1)}, f32[2,8,32]{2,1,0:T(8,128)S(1)}, u32[]{:S(2)}, u32[]{:S(2)}) collective-permute-start(f32[2,8,32]{2,1,0:T(8,128)S(1)} %get-tuple-element.161), channel_id=1, source_target_pairs={{16,0},{32,16},{48,32},{64,48},{80,64},{96,80},{112,96},{128,112},... | collective-permute-start | bytes 6152 | tf_op jit(solution)/shard_map/ppermute | solution.py:25
  111.1 1.9 collective-permute-start.11
  113.1 9.7 %collective-permute-start.10 = (f32[12,2,32]{2,1,0:T(2,128)S(1)}, f32[12,2,32]{2,1,0:T(2,128)S(1)}, u32[]{:S(2)}, u32[]{:S(2)}) collective-permute-start(f32[12,2,32]{2,1,0:T(2,128)S(1)} %get-tuple-element.149), channel_id=1, source_target_pairs={{0,1},{1,2},{2,3},{3,4},{4,5},{5,6},{6,7},{7,8},{8,9},{9,10},{10,1... | collective-permute-start | bytes 9224 | tf_op jit(solution)/shard_map/ppermute | solution.py:23
  133.8 1.9 collective-permute-start.12
  135.8 7.5 %collective-permute-start.13 = (f32[1,8,32]{2,1,0:T(8,128)S(1)}, f32[1,8,32]{2,1,0:T(8,128)S(1)}, u32[]{:S(2)}, u32[]{:S(2)}) collective-permute-start(f32[1,8,32]{2,1,0:T(8,128)S(1)} %get-tuple-element.159), channel_id=1, source_target_pairs={{16,0},{32,16},{48,32},{64,48},{80,64},{96,80},{112,96},{128,112},... | collective-permute-start | bytes 3080 | tf_op jit(solution)/shard_map/ppermute | solution.py:25
  144.1 1.9 collective-permute-start.15
  146.0 11.3 %collective-permute-start.14 = (f32[10,1,32]{2,1,0:T(1,128)S(1)}, f32[10,1,32]{2,1,0:T(1,128)S(1)}, u32[]{:S(2)}, u32[]{:S(2)}) collective-permute-start(f32[10,1,32]{2,1,0:T(1,128)S(1)} %get-tuple-element.153), channel_id=1, source_target_pairs={{0,1},{1,2},{2,3},{3,4},{4,5},{5,6},{6,7},{7,8},{8,9},{9,10},{10,1... | collective-permute-start | bytes 3848 | tf_op jit(solution)/shard_map/ppermute | solution.py:23
  164.2 6.2 %collective-permute-done.16 = f32[2,2,8]{2,1,0:T(2,128)S(1)} collective-permute-done((f32[2,2,8]{2,1,0:T(2,128)S(1)}, f32[2,2,8]{2,1,0:T(2,128)S(1)}, u32[]{:S(2)}, u32[]{:S(2)}) %collective-permute-start.16) | collective-permute-done | bytes 160 | tf_op jit(solution)/shard_map/ppermute | solution.py:34
  170.4 10.3 %collective-permute-start.17 = (f32[2,8]{1,0:T(2,128)S(1)}, f32[2,8]{1,0:T(2,128)S(1)}, u32[]{:S(2)}, u32[]{:S(2)}) collective-permute-start(f32[2,8]{1,0:T(2,128)S(1)} %bitcast.423), channel_id=1, source_target_pairs={{0,1},{1,2},{2,3},{3,4},{4,5},{5,6},{6,7},{7,8},{8,9},{9,10},{10,1... | collective-permute-start | bytes 200 | tf_op jit(solution)/shard_map/ppermute | solution.py:40
  181.8 42.8 %all-reduce.32 = bf16[512]{0:T(512)(128)(2,1)S(1)} all-reduce(bf16[512]{0:T(512)(128)(2,1)S(1)} %dynamic-update-slice.28), channel_id=1, replica_groups=mesh['gx'=32,'gy'=16] {'gy'}, use_global_device_ids=true, to_apply=%add.32 | all-reduce | flops 512 | bytes 2048
  224.9 3.6 collective-permute-start.18
  229.3 2.9 collective-permute-start.19
  232.2 9.6 %collective-permute-done.19 = f32[3,1,8]{2,1,0:T(1,128)S(1)} collective-permute-done((f32[3,1,8]{2,1,0:T(1,128)S(1)}, f32[3,1,8]{2,1,0:T(1,128)S(1)}, u32[]{:S(2)}, u32[]{:S(2)}) %collective-permute-start.19) | collective-permute-done | bytes 128 | tf_op jit(solution)/shard_map/ppermute | solution.py:40
  246.8 7.6 %collective-permute-start.21 = (f32[2,8,32]{2,1,0:T(8,128)S(1)}, f32[2,8,32]{2,1,0:T(8,128)S(1)}, u32[]{:S(2)}, u32[]{:S(2)}) collective-permute-start(f32[2,8,32]{2,1,0:T(8,128)S(1)} %get-tuple-element.157), channel_id=1, source_target_pairs={{16,0},{32,16},{48,32},{64,48},{80,64},{96,80},{112,96},{128,112},... | collective-permute-start | bytes 6152 | tf_op jit(solution)/shard_map/ppermute | solution.py:25
  257.1 9.7 %collective-permute-start.22 = (f32[12,2,32]{2,1,0:T(2,128)S(1)}, f32[12,2,32]{2,1,0:T(2,128)S(1)}, u32[]{:S(2)}, u32[]{:S(2)}) collective-permute-start(f32[12,2,32]{2,1,0:T(2,128)S(1)} %get-tuple-element.147), channel_id=1, source_target_pairs={{0,1},{1,2},{2,3},{3,4},{4,5},{5,6},{6,7},{7,8},{8,9},{9,10},{10,1... | collective-permute-start | bytes 9224 | tf_op jit(solution)/shard_map/ppermute | solution.py:23
  279.7 7.5 %collective-permute-start.25 = (f32[1,8,32]{2,1,0:T(8,128)S(1)}, f32[1,8,32]{2,1,0:T(8,128)S(1)}, u32[]{:S(2)}, u32[]{:S(2)}) collective-permute-start(f32[1,8,32]{2,1,0:T(8,128)S(1)} %get-tuple-element.155), channel_id=1, source_target_pairs={{16,0},{32,16},{48,32},{64,48},{80,64},{96,80},{112,96},{128,112},... | collective-permute-start | bytes 3080 | tf_op jit(solution)/shard_map/ppermute | solution.py:25
  289.9 11.3 %collective-permute-start.26 = (f32[10,1,32]{2,1,0:T(1,128)S(1)}, f32[10,1,32]{2,1,0:T(1,128)S(1)}, u32[]{:S(2)}, u32[]{:S(2)}) collective-permute-start(f32[10,1,32]{2,1,0:T(1,128)S(1)} %get-tuple-element.151), channel_id=1, source_target_pairs={{0,1},{1,2},{2,3},{3,4},{4,5},{5,6},{6,7},{7,8},{8,9},{9,10},{10,1... | collective-permute-start | bytes 3848 | tf_op jit(solution)/shard_map/ppermute | solution.py:23
  307.9 1.9 collective-permute-start.28
  309.8 7.8 %collective-permute-start.29 = (f32[2,16,64]{2,1,0:T(8,128)S(1)}, f32[2,16,64]{2,1,0:T(8,128)S(1)}, u32[]{:S(2)}, u32[]{:S(2)}) collective-permute-start(f32[2,16,64]{2,1,0:T(8,128)S(1)} %get-tuple-element.105), channel_id=1, source_target_pairs={{16,0},{32,16},{48,32},{64,48},{80,64},{96,80},{112,96},{128,112},... | collective-permute-start | bytes 24584 | tf_op jit(solution)/shard_map/ppermute | solution.py:25
  320.4 11.1 %collective-permute-start.30 = (f32[20,2,64]{2,1,0:T(2,128)S(1)}, f32[20,2,64]{2,1,0:T(2,128)S(1)}, u32[]{:S(2)}, u32[]{:S(2)}) collective-permute-start(f32[20,2,64]{2,1,0:T(2,128)S(1)} %get-tuple-element.95), channel_id=1, source_target_pairs={{0,1},{1,2},{2,3},{3,4},{4,5},{5,6},{6,7},{7,8},{8,9},{9,10},{10,1... | collective-permute-start | bytes 30728 | tf_op jit(solution)/shard_map/ppermute | solution.py:23
  335.3 2.1 fusion.120
  337.3 2.6 copy.323
  342.6 2.9 copy.325
  345.5 4.1 %copy.322 = f32[2,10,2,10,8,1]{3,4,5,2,1,0:T(8,128)} copy(f32[2,10,2,10,8,1]{5,4,3,2,1,0:T(8,128)} %get-tuple-element.51) | data formatting | bytes 25600 | tf_op jit(solution)/shard_map/slice | solution.py:246
  352.1 4.1 %copy.324 = f32[2,10,2,10,8,1]{5,4,3,2,1,0:T(8,128)} copy(f32[2,10,2,10,8,1]{3,4,5,2,1,0:T(8,128)} %maximum_bitcast_fusion.6) | data formatting | bytes 25600 | tf_op jit(solution)/shard_map/broadcast_in_dim | solution.py:248
  356.1 3.6 maximum_bitcast_fusion.1
  359.8 4.4 %copy.346 = f32[10,10,10,2,2,8]{5,4,3,0,2,1:T(2,128)S(1)} copy(f32[10,10,10,2,2,8]{2,5,1,4,0,3:T(8,128)} %maximum_bitcast_fusion.1) | data formatting | bytes 256000 | tf_op jit(solution)/shard_map/reshape | solution.py:250
  372.8 1.9 collective-permute-start.32
  374.8 7.8 %collective-permute-start.33 = (f32[1,16,64]{2,1,0:T(8,128)S(1)}, f32[1,16,64]{2,1,0:T(8,128)S(1)}, u32[]{:S(2)}, u32[]{:S(2)}) collective-permute-start(f32[1,16,64]{2,1,0:T(8,128)S(1)} %get-tuple-element.103), channel_id=1, source_target_pairs={{16,0},{32,16},{48,32},{64,48},{80,64},{96,80},{112,96},{128,112},... | collective-permute-start | bytes 12296 | tf_op jit(solution)/shard_map/ppermute | solution.py:25
  383.4 1.9 collective-permute-start.35
  385.3 11.1 %collective-permute-start.34 = (f32[18,1,64]{2,1,0:T(1,128)S(1)}, f32[18,1,64]{2,1,0:T(1,128)S(1)}, u32[]{:S(2)}, u32[]{:S(2)}) collective-permute-start(f32[18,1,64]{2,1,0:T(1,128)S(1)} %get-tuple-element.99), channel_id=1, source_target_pairs={{0,1},{1,2},{2,3},{3,4},{4,5},{5,6},{6,7},{7,8},{8,9},{9,10},{10,1... | collective-permute-start | bytes 13832 | tf_op jit(solution)/shard_map/ppermute | solution.py:23
  (524 shorter events, 104.6 us)
Async XLA Ops:
  0.6 224.0 %copy-start = (bf16[1,32,512]{2,1,0:T(8,128)(2,1)S(1)}, bf16[1,32,512]{2,1,0:T(8,128)(2,1)}, u32[]{:S(2)}) copy-start(bf16[1,32,512]{2,1,0:T(8,128)(2,1)} %param.87) | copy-start | bytes 98308
  0.6 33.7 %copy-start.35 = (f32[20]{0:T(128)S(1)}, f32[20]{0:T(128)}, u32[]{:S(2)}) copy-start(f32[20]{0:T(128)} %constant.315) | copy-start | bytes 244
  0.7 33.7 %copy-start.37 = (f32[20]{0:T(128)S(1)}, f32[20]{0:T(128)}, u32[]{:S(2)}) copy-start(f32[20]{0:T(128)} %constant.314) | copy-start | bytes 244
  1.4 19.4 %collective-permute-start = (f32[2,16,64]{2,1,0:T(8,128)S(1)}, f32[2,16,64]{2,1,0:T(8,128)S(1)}, u32[]{:S(2)}, u32[]{:S(2)}) collective-permute-start(f32[2,16,64]{2,1,0:T(8,128)S(1)} %get-tuple-element.110), channel_id=1, source_target_pairs={{0,16},{16,32},{32,48},{48,64},{64,80},{80,96},{96,112},{112,128},... | collective-permute-start | bytes 24584 | tf_op jit(solution)/shard_map/ppermute | solution.py:23
  5.4 16.3 %collective-permute-start.1 = (f32[2,16,64]{2,1,0:T(8,128)S(1)}, f32[2,16,64]{2,1,0:T(8,128)S(1)}, u32[]{:S(2)}, u32[]{:S(2)}) collective-permute-start(f32[2,16,64]{2,1,0:T(8,128)S(1)} %get-tuple-element.109), channel_id=1, source_target_pairs={{16,0},{32,16},{48,32},{64,48},{80,64},{96,80},{112,96},{128,112},... | collective-permute-start | bytes 24584 | tf_op jit(solution)/shard_map/ppermute | solution.py:25
  21.8 11.6 %collective-permute-start.3 = (f32[20,2,64]{2,1,0:T(2,128)S(1)}, f32[20,2,64]{2,1,0:T(2,128)S(1)}, u32[]{:S(2)}, u32[]{:S(2)}) collective-permute-start(f32[20,2,64]{2,1,0:T(2,128)S(1)} %get-tuple-element.98), channel_id=1, source_target_pairs={{1,0},{2,1},{3,2},{4,3},{5,4},{6,5},{7,6},{8,7},{9,8},{10,9},{11,1... | collective-permute-start | bytes 30728 | tf_op jit(solution)/shard_map/ppermute | solution.py:25
  24.6 9.6 %collective-permute-start.2 = (f32[20,2,64]{2,1,0:T(2,128)S(1)}, f32[20,2,64]{2,1,0:T(2,128)S(1)}, u32[]{:S(2)}, u32[]{:S(2)}) collective-permute-start(f32[20,2,64]{2,1,0:T(2,128)S(1)} %get-tuple-element.97), channel_id=1, source_target_pairs={{0,1},{1,2},{2,3},{3,4},{4,5},{5,6},{6,7},{7,8},{8,9},{9,10},{10,1... | collective-permute-start | bytes 30728 | tf_op jit(solution)/shard_map/ppermute | solution.py:23
  67.5 9.3 %collective-permute-start.4 = (f32[1,16,64]{2,1,0:T(8,128)S(1)}, f32[1,16,64]{2,1,0:T(8,128)S(1)}, u32[]{:S(2)}, u32[]{:S(2)}) collective-permute-start(f32[1,16,64]{2,1,0:T(8,128)S(1)} %get-tuple-element.108), channel_id=1, source_target_pairs={{0,16},{16,32},{32,48},{48,64},{64,80},{80,96},{96,112},{112,128},... | collective-permute-start | bytes 12296 | tf_op jit(solution)/shard_map/ppermute | solution.py:23
  69.5 8.0 %collective-permute-start.5 = (f32[1,16,64]{2,1,0:T(8,128)S(1)}, f32[1,16,64]{2,1,0:T(8,128)S(1)}, u32[]{:S(2)}, u32[]{:S(2)}) collective-permute-start(f32[1,16,64]{2,1,0:T(8,128)S(1)} %get-tuple-element.107), channel_id=1, source_target_pairs={{16,0},{32,16},{48,32},{64,48},{80,64},{96,80},{112,96},{128,112},... | collective-permute-start | bytes 12296 | tf_op jit(solution)/shard_map/ppermute | solution.py:25
  77.6 16.6 %collective-permute-start.7 = (f32[18,1,64]{2,1,0:T(1,128)S(1)}, f32[18,1,64]{2,1,0:T(1,128)S(1)}, u32[]{:S(2)}, u32[]{:S(2)}) collective-permute-start(f32[18,1,64]{2,1,0:T(1,128)S(1)} %get-tuple-element.102), channel_id=1, source_target_pairs={{1,0},{2,1},{3,2},{4,3},{5,4},{6,5},{7,6},{8,7},{9,8},{10,9},{11,1... | collective-permute-start | bytes 13832 | tf_op jit(solution)/shard_map/ppermute | solution.py:25
  79.5 14.6 %collective-permute-start.6 = (f32[18,1,64]{2,1,0:T(1,128)S(1)}, f32[18,1,64]{2,1,0:T(1,128)S(1)}, u32[]{:S(2)}, u32[]{:S(2)}) collective-permute-start(f32[18,1,64]{2,1,0:T(1,128)S(1)} %get-tuple-element.101), channel_id=1, source_target_pairs={{0,1},{1,2},{2,3},{3,4},{4,5},{5,6},{6,7},{7,8},{8,9},{9,10},{10,1... | collective-permute-start | bytes 13832 | tf_op jit(solution)/shard_map/ppermute | solution.py:23
  100.5 9.8 %collective-permute-start.8 = (f32[2,8,32]{2,1,0:T(8,128)S(1)}, f32[2,8,32]{2,1,0:T(8,128)S(1)}, u32[]{:S(2)}, u32[]{:S(2)}) collective-permute-start(f32[2,8,32]{2,1,0:T(8,128)S(1)} %get-tuple-element.162), channel_id=1, source_target_pairs={{0,16},{16,32},{32,48},{48,64},{64,80},{80,96},{96,112},{112,128},... | collective-permute-start | bytes 6152 | tf_op jit(solution)/shard_map/ppermute | solution.py:23
  102.5 56.6 %copy-start.13 = (f32[8,8]{1,0:T(8,128)}, f32[8,8]{1,0:T(8,128)S(1)}, u32[]{:S(2)}) copy-start(f32[8,8]{1,0:T(8,128)S(1)} %broadcast_multiply_fusion.4) | copy-start | bytes 772
  102.5 8.6 %collective-permute-start.9 = (f32[2,8,32]{2,1,0:T(8,128)S(1)}, f32[2,8,32]{2,1,0:T(8,128)S(1)}, u32[]{:S(2)}, u32[]{:S(2)}) collective-permute-start(f32[2,8,32]{2,1,0:T(8,128)S(1)} %get-tuple-element.161), channel_id=1, source_target_pairs={{16,0},{32,16},{48,32},{64,48},{80,64},{96,80},{112,96},{128,112},... | collective-permute-start | bytes 6152 | tf_op jit(solution)/shard_map/ppermute | solution.py:25
  111.1 11.6 %collective-permute-start.11 = (f32[12,2,32]{2,1,0:T(2,128)S(1)}, f32[12,2,32]{2,1,0:T(2,128)S(1)}, u32[]{:S(2)}, u32[]{:S(2)}) collective-permute-start(f32[12,2,32]{2,1,0:T(2,128)S(1)} %get-tuple-element.150), channel_id=1, source_target_pairs={{1,0},{2,1},{3,2},{4,3},{5,4},{6,5},{7,6},{8,7},{9,8},{10,9},{11,1... | collective-permute-start | bytes 9224 | tf_op jit(solution)/shard_map/ppermute | solution.py:25
  113.1 10.5 %collective-permute-start.10 = (f32[12,2,32]{2,1,0:T(2,128)S(1)}, f32[12,2,32]{2,1,0:T(2,128)S(1)}, u32[]{:S(2)}, u32[]{:S(2)}) collective-permute-start(f32[12,2,32]{2,1,0:T(2,128)S(1)} %get-tuple-element.149), channel_id=1, source_target_pairs={{0,1},{1,2},{2,3},{3,4},{4,5},{5,6},{6,7},{7,8},{8,9},{9,10},{10,1... | collective-permute-start | bytes 9224 | tf_op jit(solution)/shard_map/ppermute | solution.py:23
  131.4 27.2 %copy-start.43 = (f32[10]{0:T(128)S(1)}, f32[10]{0:T(128)}, u32[]{:S(2)}) copy-start(f32[10]{0:T(128)} %constant.328) | copy-start | bytes 124
  131.4 27.2 %copy-start.45 = (f32[10]{0:T(128)S(1)}, f32[10]{0:T(128)}, u32[]{:S(2)}) copy-start(f32[10]{0:T(128)} %constant.327) | copy-start | bytes 124
  133.8 9.5 %collective-permute-start.12 = (f32[1,8,32]{2,1,0:T(8,128)S(1)}, f32[1,8,32]{2,1,0:T(8,128)S(1)}, u32[]{:S(2)}, u32[]{:S(2)}) collective-permute-start(f32[1,8,32]{2,1,0:T(8,128)S(1)} %get-tuple-element.160), channel_id=1, source_target_pairs={{0,16},{16,32},{32,48},{48,64},{64,80},{80,96},{96,112},{112,128},... | collective-permute-start | bytes 3080 | tf_op jit(solution)/shard_map/ppermute | solution.py:23
  135.8 8.3 %collective-permute-start.13 = (f32[1,8,32]{2,1,0:T(8,128)S(1)}, f32[1,8,32]{2,1,0:T(8,128)S(1)}, u32[]{:S(2)}, u32[]{:S(2)}) collective-permute-start(f32[1,8,32]{2,1,0:T(8,128)S(1)} %get-tuple-element.159), channel_id=1, source_target_pairs={{16,0},{32,16},{48,32},{64,48},{80,64},{96,80},{112,96},{128,112},... | collective-permute-start | bytes 3080 | tf_op jit(solution)/shard_map/ppermute | solution.py:25
  144.1 14.5 %collective-permute-start.15 = (f32[10,1,32]{2,1,0:T(1,128)S(1)}, f32[10,1,32]{2,1,0:T(1,128)S(1)}, u32[]{:S(2)}, u32[]{:S(2)}) collective-permute-start(f32[10,1,32]{2,1,0:T(1,128)S(1)} %get-tuple-element.154), channel_id=1, source_target_pairs={{1,0},{2,1},{3,2},{4,3},{5,4},{6,5},{7,6},{8,7},{9,8},{10,9},{11,1... | collective-permute-start | bytes 3848 | tf_op jit(solution)/shard_map/ppermute | solution.py:25
  146.0 12.6 %collective-permute-start.14 = (f32[10,1,32]{2,1,0:T(1,128)S(1)}, f32[10,1,32]{2,1,0:T(1,128)S(1)}, u32[]{:S(2)}, u32[]{:S(2)}) collective-permute-start(f32[10,1,32]{2,1,0:T(1,128)S(1)} %get-tuple-element.153), channel_id=1, source_target_pairs={{0,1},{1,2},{2,3},{3,4},{4,5},{5,6},{6,7},{7,8},{8,9},{9,10},{10,1... | collective-permute-start | bytes 3848 | tf_op jit(solution)/shard_map/ppermute | solution.py:23
  158.9 85.1 %copy-start.17 = (f32[32]{0:T(128)S(1)}, f32[32]{0:T(128)}, u32[]{:S(2)}) copy-start(f32[32]{0:T(128)} %copy-done.15) | copy-start | bytes 388
  158.9 85.1 %copy-start.20 = (f32[32]{0:T(128)S(1)}, f32[32]{0:T(128)}, u32[]{:S(2)}) copy-start(f32[32]{0:T(128)} %copy-done.18) | copy-start | bytes 388
  158.9 85.1 %copy-start.23 = (f32[32]{0:T(128)S(1)}, f32[32]{0:T(128)}, u32[]{:S(2)}) copy-start(f32[32]{0:T(128)} %copy-done.21) | copy-start | bytes 388
  159.4 108.2 %copy-start.54 = (pred[12]{0:T(512)(128)(4,1)S(1)}, pred[12]{0:T(512)(128)(4,1)}, u32[]{:S(2)}) copy-start(pred[12]{0:T(512)(128)(4,1)} %copy-done.53) | copy-start | bytes 40
  160.0 107.6 %copy-start.48 = (f32[12]{0:T(128)S(1)}, f32[12]{0:T(128)}, u32[]{:S(2)}) copy-start(f32[12]{0:T(128)} %constant.324) | copy-start | bytes 148
  160.0 107.6 %copy-start.50 = (f32[12]{0:T(128)S(1)}, f32[12]{0:T(128)}, u32[]{:S(2)}) copy-start(f32[12]{0:T(128)} %constant.323) | copy-start | bytes 148
  161.6 8.8 %collective-permute-start.16 = (f32[2,2,8]{2,1,0:T(2,128)S(1)}, f32[2,2,8]{2,1,0:T(2,128)S(1)}, u32[]{:S(2)}, u32[]{:S(2)}) collective-permute-start(f32[2,2,8]{2,1,0:T(2,128)S(1)} %get-tuple-element.174), channel_id=1, source_target_pairs={{0,16},{16,32},{32,48},{48,64},{64,80},{80,96},{96,112},{112,128},... | collective-permute-start | bytes 392 | tf_op jit(solution)/shard_map/ppermute | solution.py:34
  170.4 11.0 %collective-permute-start.17 = (f32[2,8]{1,0:T(2,128)S(1)}, f32[2,8]{1,0:T(2,128)S(1)}, u32[]{:S(2)}, u32[]{:S(2)}) collective-permute-start(f32[2,8]{1,0:T(2,128)S(1)} %bitcast.423), channel_id=1, source_target_pairs={{0,1},{1,2},{2,3},{3,4},{4,5},{5,6},{6,7},{7,8},{8,9},{9,10},{10,1... | collective-permute-start | bytes 200 | tf_op jit(solution)/shard_map/ppermute | solution.py:40
  224.9 4.3 %collective-permute-start.18 = (f32[1,2,8]{2,1,0:T(2,128)S(1)}, f32[1,2,8]{2,1,0:T(2,128)S(1)}, u32[]{:S(2)}, u32[]{:S(2)}) collective-permute-start(f32[1,2,8]{2,1,0:T(2,128)S(1)} %slice.729), channel_id=1, source_target_pairs={{0,496},{16,0},{32,16},{48,32},{64,48},{80,64},{96,80},{112,96},{1... | collective-permute-start | bytes 200 | tf_op jit(solution)/shard_map/ppermute | solution.py:34
  229.3 12.6 %collective-permute-start.19 = (f32[3,1,8]{2,1,0:T(1,128)S(1)}, f32[3,1,8]{2,1,0:T(1,128)S(1)}, u32[]{:S(2)}, u32[]{:S(2)}) collective-permute-start(f32[3,1,8]{2,1,0:T(1,128)S(1)} %slice.891), channel_id=1, source_target_pairs={{1,0},{2,1},{3,2},{4,3},{5,4},{6,5},{7,6},{8,7},{9,8},{10,9},{11,1... | collective-permute-start | bytes 296 | tf_op jit(solution)/shard_map/ppermute | solution.py:40
  244.9 9.5 %collective-permute-start.20 = (f32[2,8,32]{2,1,0:T(8,128)S(1)}, f32[2,8,32]{2,1,0:T(8,128)S(1)}, u32[]{:S(2)}, u32[]{:S(2)}) collective-permute-start(f32[2,8,32]{2,1,0:T(8,128)S(1)} %get-tuple-element.158), channel_id=1, source_target_pairs={{0,16},{16,32},{32,48},{48,64},{64,80},{80,96},{96,112},{112,128},... | collective-permute-start | bytes 6152 | tf_op jit(solution)/shard_map/ppermute | solution.py:23
  246.8 8.3 %collective-permute-start.21 = (f32[2,8,32]{2,1,0:T(8,128)S(1)}, f32[2,8,32]{2,1,0:T(8,128)S(1)}, u32[]{:S(2)}, u32[]{:S(2)}) collective-permute-start(f32[2,8,32]{2,1,0:T(8,128)S(1)} %get-tuple-element.157), channel_id=1, source_target_pairs={{16,0},{32,16},{48,32},{64,48},{80,64},{96,80},{112,96},{128,112},... | collective-permute-start | bytes 6152 | tf_op jit(solution)/shard_map/ppermute | solution.py:25
  255.1 11.6 %collective-permute-start.23 = (f32[12,2,32]{2,1,0:T(2,128)S(1)}, f32[12,2,32]{2,1,0:T(2,128)S(1)}, u32[]{:S(2)}, u32[]{:S(2)}) collective-permute-start(f32[12,2,32]{2,1,0:T(2,128)S(1)} %get-tuple-element.148), channel_id=1, source_target_pairs={{1,0},{2,1},{3,2},{4,3},{5,4},{6,5},{7,6},{8,7},{9,8},{10,9},{11,1... | collective-permute-start | bytes 9224 | tf_op jit(solution)/shard_map/ppermute | solution.py:25
  257.1 10.5 %collective-permute-start.22 = (f32[12,2,32]{2,1,0:T(2,128)S(1)}, f32[12,2,32]{2,1,0:T(2,128)S(1)}, u32[]{:S(2)}, u32[]{:S(2)}) collective-permute-start(f32[12,2,32]{2,1,0:T(2,128)S(1)} %get-tuple-element.147), channel_id=1, source_target_pairs={{0,1},{1,2},{2,3},{3,4},{4,5},{5,6},{6,7},{7,8},{8,9},{9,10},{10,1... | collective-permute-start | bytes 9224 | tf_op jit(solution)/shard_map/ppermute | solution.py:23
  277.8 9.5 %collective-permute-start.24 = (f32[1,8,32]{2,1,0:T(8,128)S(1)}, f32[1,8,32]{2,1,0:T(8,128)S(1)}, u32[]{:S(2)}, u32[]{:S(2)}) collective-permute-start(f32[1,8,32]{2,1,0:T(8,128)S(1)} %get-tuple-element.156), channel_id=1, source_target_pairs={{0,16},{16,32},{32,48},{48,64},{64,80},{80,96},{96,112},{112,128},... | collective-permute-start | bytes 3080 | tf_op jit(solution)/shard_map/ppermute | solution.py:23
  279.7 8.3 %collective-permute-start.25 = (f32[1,8,32]{2,1,0:T(8,128)S(1)}, f32[1,8,32]{2,1,0:T(8,128)S(1)}, u32[]{:S(2)}, u32[]{:S(2)}) collective-permute-start(f32[1,8,32]{2,1,0:T(8,128)S(1)} %get-tuple-element.155), channel_id=1, source_target_pairs={{16,0},{32,16},{48,32},{64,48},{80,64},{96,80},{112,96},{128,112},... | collective-permute-start | bytes 3080 | tf_op jit(solution)/shard_map/ppermute | solution.py:25
  288.0 13.3 %collective-permute-start.27 = (f32[10,1,32]{2,1,0:T(1,128)S(1)}, f32[10,1,32]{2,1,0:T(1,128)S(1)}, u32[]{:S(2)}, u32[]{:S(2)}) collective-permute-start(f32[10,1,32]{2,1,0:T(1,128)S(1)} %get-tuple-element.152), channel_id=1, source_target_pairs={{1,0},{2,1},{3,2},{4,3},{5,4},{6,5},{7,6},{8,7},{9,8},{10,9},{11,1... | collective-permute-start | bytes 3848 | tf_op jit(solution)/shard_map/ppermute | solution.py:25
  289.9 11.8 %collective-permute-start.26 = (f32[10,1,32]{2,1,0:T(1,128)S(1)}, f32[10,1,32]{2,1,0:T(1,128)S(1)}, u32[]{:S(2)}, u32[]{:S(2)}) collective-permute-start(f32[10,1,32]{2,1,0:T(1,128)S(1)} %get-tuple-element.151), channel_id=1, source_target_pairs={{0,1},{1,2},{2,3},{3,4},{4,5},{5,6},{6,7},{7,8},{8,9},{9,10},{10,1... | collective-permute-start | bytes 3848 | tf_op jit(solution)/shard_map/ppermute | solution.py:23
  307.9 9.7 %collective-permute-start.28 = (f32[2,16,64]{2,1,0:T(8,128)S(1)}, f32[2,16,64]{2,1,0:T(8,128)S(1)}, u32[]{:S(2)}, u32[]{:S(2)}) collective-permute-start(f32[2,16,64]{2,1,0:T(8,128)S(1)} %get-tuple-element.106), channel_id=1, source_target_pairs={{0,16},{16,32},{32,48},{48,64},{64,80},{80,96},{96,112},{112,128},... | collective-permute-start | bytes 24584 | tf_op jit(solution)/shard_map/ppermute | solution.py:23
  309.8 8.7 %collective-permute-start.29 = (f32[2,16,64]{2,1,0:T(8,128)S(1)}, f32[2,16,64]{2,1,0:T(8,128)S(1)}, u32[]{:S(2)}, u32[]{:S(2)}) collective-permute-start(f32[2,16,64]{2,1,0:T(8,128)S(1)} %get-tuple-element.105), channel_id=1, source_target_pairs={{16,0},{32,16},{48,32},{64,48},{80,64},{96,80},{112,96},{128,112},... | collective-permute-start | bytes 24584 | tf_op jit(solution)/shard_map/ppermute | solution.py:25
  318.5 13.0 %collective-permute-start.31 = (f32[20,2,64]{2,1,0:T(2,128)S(1)}, f32[20,2,64]{2,1,0:T(2,128)S(1)}, u32[]{:S(2)}, u32[]{:S(2)}) collective-permute-start(f32[20,2,64]{2,1,0:T(2,128)S(1)} %get-tuple-element.96), channel_id=1, source_target_pairs={{1,0},{2,1},{3,2},{4,3},{5,4},{6,5},{7,6},{8,7},{9,8},{10,9},{11,1... | collective-permute-start | bytes 30728 | tf_op jit(solution)/shard_map/ppermute | solution.py:25
  320.4 12.0 %collective-permute-start.30 = (f32[20,2,64]{2,1,0:T(2,128)S(1)}, f32[20,2,64]{2,1,0:T(2,128)S(1)}, u32[]{:S(2)}, u32[]{:S(2)}) collective-permute-start(f32[20,2,64]{2,1,0:T(2,128)S(1)} %get-tuple-element.95), channel_id=1, source_target_pairs={{0,1},{1,2},{2,3},{3,4},{4,5},{5,6},{6,7},{7,8},{8,9},{9,10},{10,1... | collective-permute-start | bytes 30728 | tf_op jit(solution)/shard_map/ppermute | solution.py:23
  372.8 9.8 %collective-permute-start.32 = (f32[1,16,64]{2,1,0:T(8,128)S(1)}, f32[1,16,64]{2,1,0:T(8,128)S(1)}, u32[]{:S(2)}, u32[]{:S(2)}) collective-permute-start(f32[1,16,64]{2,1,0:T(8,128)S(1)} %get-tuple-element.104), channel_id=1, source_target_pairs={{0,16},{16,32},{32,48},{48,64},{64,80},{80,96},{96,112},{112,128},... | collective-permute-start | bytes 12296 | tf_op jit(solution)/shard_map/ppermute | solution.py:23
  374.8 8.6 %collective-permute-start.33 = (f32[1,16,64]{2,1,0:T(8,128)S(1)}, f32[1,16,64]{2,1,0:T(8,128)S(1)}, u32[]{:S(2)}, u32[]{:S(2)}) collective-permute-start(f32[1,16,64]{2,1,0:T(8,128)S(1)} %get-tuple-element.103), channel_id=1, source_target_pairs={{16,0},{32,16},{48,32},{64,48},{80,64},{96,80},{112,96},{128,112},... | collective-permute-start | bytes 12296 | tf_op jit(solution)/shard_map/ppermute | solution.py:25
  383.4 16.4 %collective-permute-start.35 = (f32[18,1,64]{2,1,0:T(1,128)S(1)}, f32[18,1,64]{2,1,0:T(1,128)S(1)}, u32[]{:S(2)}, u32[]{:S(2)}) collective-permute-start(f32[18,1,64]{2,1,0:T(1,128)S(1)} %get-tuple-element.100), channel_id=1, source_target_pairs={{1,0},{2,1},{3,2},{4,3},{5,4},{6,5},{7,6},{8,7},{9,8},{10,9},{11,1... | collective-permute-start | bytes 13832 | tf_op jit(solution)/shard_map/ppermute | solution.py:25
  385.3 14.5 %collective-permute-start.34 = (f32[18,1,64]{2,1,0:T(1,128)S(1)}, f32[18,1,64]{2,1,0:T(1,128)S(1)}, u32[]{:S(2)}, u32[]{:S(2)}) collective-permute-start(f32[18,1,64]{2,1,0:T(1,128)S(1)} %get-tuple-element.99), channel_id=1, source_target_pairs={{0,1},{1,2},{2,3},{3,4},{4,5},{5,6},{6,7},{7,8},{8,9},{9,10},{10,1... | collective-permute-start | bytes 13832 | tf_op jit(solution)/shard_map/ppermute | solution.py:23
  (66 other events, 558.8 us)
where the time goes:
time: 410 us; the launch traced here: 402 us
  starting transfers between devices  198 us (48%)
  local copies, waits for them, and re-layouts  87.4 us (21%)
  blocking collectives  42.8 us (10%)
  waiting for transfers between devices  26.1 us (6%)
  other arithmetic  22.6 us (6%)
  matrix products  20 us (5%)
  between operations  4.82 us (1%)
    ppermute x16, starting transfers between devices, extended_2(): lax.ppermute(tail, axis, [(i, (i + 1) % count) for i in range(count)])  102 us
    ppermute x16, starting transfers between devices, extended_2(): lax.ppermute(head, axis, [((i + 1) % count, i) for i in range(count)])  78 us
    unnamed x1, blocking collectives  42.8 us
    slice x12, local copies, waits for them, and re-layouts, extend(): left_part = jnp.roll(own_part[..., points - 2], 1, 4)  15.4 us
    reshape x8, local copies, waits for them, and re-layouts, extend(): section_three.transpose(1, 3, 5, 0, 2, 4)  14.8 us
    ppermute x2, starting transfers between devices, from_behind_2(): lax.ppermute(value, axis, [(source, source + steps) for source in range(i...  13.3 us
    ppermute x2, waiting for transfers between devices, from_behind_2(): lax.ppermute(value, axis, [(source, source + steps) for source in range(i...  10.2 us
    broadcast_in_dim x4, local copies, waits for them, and re-layouts, extend(): left_part[..., None]  9.93 us
  transfers between devices with their start and end apart: 36, of which 16 were waited for; matrix products, arithmetic and copies ran while one was open for 4% of the time, Pallas kernels for 0%

commit v1 on v0

v1 whole, which is shorter than its diff:
```python
import functools
import math

import jax
import jax.numpy as jnp
import ml_dtypes
import numpy as np
from jax import lax
from jax.experimental import pallas as pl
from jax.experimental.pallas import tpu as pltpu
from jax.sharding import PartitionSpec as P

ORDER = 7
MID_ORDER = 3


def legendre_pair(order, point):
    older = 1.0
    newer = point
    for degree in range(2, order + 1):
        nexter = ((2 * degree - 1) * point * newer - (degree - 1) * older) / degree
        older = newer
        newer = nexter
    return (newer, older)


def jacobi_eigen(matrix):
    count_n = len(matrix)
    work = [list(row_items) for row_items in matrix]
    vectors = [
        [1.0 if row_at == col_at else 0.0 for col_at in range(count_n)] for row_at in range(count_n)
    ]
    for sweep_count in range(60):
        for lower_at in range(count_n):
            for upper_at in range(lower_at + 1, count_n):
                off_value = work[lower_at][upper_at]
                if abs(off_value) < 1e-18 * (
                    abs(work[lower_at][lower_at]) + abs(work[upper_at][upper_at])
                ):
                    continue
                angle_ratio = (work[upper_at][upper_at] - work[lower_at][lower_at]) / (
                    2.0 * off_value
                )
                sign_value = 1.0 if angle_ratio >= 0 else -1.0
                tangent = sign_value / (
                    abs(angle_ratio) + math.sqrt(angle_ratio * angle_ratio + 1.0)
                )
                cosine = 1.0 / math.sqrt(tangent * tangent + 1.0)
                sine_value = tangent * cosine
                for other_at in range(count_n):
                    left_value = work[other_at][lower_at]
                    right_value = work[other_at][upper_at]
                    work[other_at][lower_at] = cosine * left_value - sine_value * right_value
                    work[other_at][upper_at] = sine_value * left_value + cosine * right_value
                for other_at in range(count_n):
                    left_value = work[lower_at][other_at]
                    right_value = work[upper_at][other_at]
                    work[lower_at][other_at] = cosine * left_value - sine_value * right_value
                    work[upper_at][other_at] = sine_value * left_value + cosine * right_value
                for other_at in range(count_n):
                    left_value = vectors[other_at][lower_at]
                    right_value = vectors[other_at][upper_at]
                    vectors[other_at][lower_at] = cosine * left_value - sine_value * right_value
                    vectors[other_at][upper_at] = sine_value * left_value + cosine * right_value
    eigen_list = [work[row_at][row_at] for row_at in range(count_n)]
    ordering = sorted(range(count_n), key=lambda index_at: eigen_list[index_at])
    rates = [eigen_list[index_at] for index_at in ordering]
    basis = [[vectors[row_at][index_at] for index_at in ordering] for row_at in range(count_n)]
    return (rates, basis)


def gll_tables(order):
    point_count = order + 1
    node_list = []
    for node_at in range(point_count):
        point = math.cos(math.pi * node_at / order)
        for newton_step in range(100):
            top_value, lower_value = legendre_pair(order, point)
            point = point - (point * top_value - lower_value) / ((order + 1) * top_value)
        node_list.append(point)
    node_list = node_list[::-1]
    node_list[0] = -1.0
    node_list[-1] = 1.0
    values = [legendre_pair(order, point)[0] for point in node_list]
    weight_list = [2.0 / (order * (order + 1) * value_at**2) for value_at in values]
    derivative = [[0.0] * point_count for row_at in range(point_count)]
    for row_at in range(point_count):
        for col_at in range(point_count):
            if row_at != col_at:
                derivative[row_at][col_at] = values[row_at] / (
                    values[col_at] * (node_list[row_at] - node_list[col_at])
                )
    derivative[0][0] = -order * (order + 1) / 4.0
    derivative[order][order] = order * (order + 1) / 4.0
    stiff_list = [
        [
            sum(
                (
                    derivative[inner_at][row_at]
                    * weight_list[inner_at]
                    * derivative[inner_at][col_at]
                    for inner_at in range(point_count)
                )
            )
            for col_at in range(point_count)
        ]
        for row_at in range(point_count)
    ]
    extent = 3 * order + 1
    big_stiff = [[0.0] * extent for row_at in range(extent)]
    big_mass = [0.0] * extent
    for offset_at in (0, order, 2 * order):
        for row_at in range(point_count):
            big_mass[offset_at + row_at] += weight_list[row_at]
            for col_at in range(point_count):
                big_stiff[offset_at + row_at][offset_at + col_at] += stiff_list[row_at][col_at]
    chosen = list(range(order - 1, 2 * order + 2))
    root_mass = [1.0 / math.sqrt(big_mass[index_at]) for index_at in chosen]
    scaled = [
        [
            root_mass[row_at] * big_stiff[chosen[row_at]][chosen[col_at]] * root_mass[col_at]
            for col_at in range(len(chosen))
        ]
        for row_at in range(len(chosen))
    ]
    rates, basis = jacobi_eigen(scaled)
    eigen_basis = [
        [root_mass[row_at] * basis[row_at][col_at] for col_at in range(len(chosen))]
        for row_at in range(len(chosen))
    ]
    return (
        np.array(node_list),
        np.array(weight_list),
        np.array(stiff_list),
        np.array(eigen_basis),
        np.array(rates),
    )


def interp_table(fine_nodes, coarse_nodes):
    coarse_count = len(coarse_nodes)
    columns = []
    for column in range(coarse_count):
        factors_list = [
            (fine_nodes - coarse_nodes[other_node])
            / (coarse_nodes[column] - coarse_nodes[other_node])
            for other_node in range(coarse_count)
            if other_node != column
        ]
        columns.append(np.prod(np.stack(factors_list), axis=0))
    return np.stack(columns, axis=1)

BF = jnp.bfloat16
F32 = jnp.float32
RING = ((-1, 0), (1, 0), (0, -1), (-1, -1), (1, -1), (0, 1), (-1, 1), (1, 1))
GROUPS = ((0, 2), (2, 5), (5, 8))
AHEAD = (-1, 1, 2, 0)
HALO_ROWS = (32, 32, 32, 8, 8, 32, 8, 8)
FACE_ROWS = (16, 16, 16, 8, 8, 16, 8, 8)
MESH = pl.DeviceIdType.MESH


def offsets(rows):
    return tuple(int(at) for at in np.concatenate([[0], np.cumsum(rows)]))


def blocks(matrix, count):
    return np.kron(np.eye(count), matrix)


def line_extension(points, elements, periodic):
    size = elements * points
    width = size if periodic else size + 4
    table = np.zeros((elements, points + 2, width))

    def column(at):
        if periodic:
            return at % size
        if at < 0:
            return {-2: size, -1: size + 1}[at]
        if at >= size:
            return {size: size + 2, size + 1: size + 3}[at]
        return at

    for element in range(elements):
        start = element * points
        table[element, 0, column(start - 2)] += 1
        for at in range(points):
            table[element, 1 + at, start + at] += 1
        table[element, 1, column(start - 1)] += 1
        table[element, points, column(start + points)] += 1
        table[element, points + 1, column(start + points + 1)] += 1
    return table.reshape(elements * (points + 2), width)


def line_weights(points, elements):
    position = np.arange(points * elements) % points
    return np.where((position == 0) | (position == points - 1), 0.5, 1.0)


def z_back(inner, points, elements):
    table = blocks(inner, elements)
    total = np.array(table)
    size = points * elements
    for element in range(elements):
        low, high = element * points, (element * points - 1) % size
        total[low] = table[low] + table[high]
        total[high] = total[low]
    return (total * line_weights(points, elements)[:, None]).T


RIGHT = (
    "az", "bz", "bzra", "jz", "kz7", "rp", "pz", "azm", "bzm", "rb", "rj", "rk3", "rc", "rcj",
    "s64", "s32", "s256", "s80", "sl80", "s48", "sl48", "select",
)


def fitted(table, right):
    rows, columns = table.shape[-2:]
    more = ((0, -rows % 128 if right else 0), (0, -columns % 128))
    return np.pad(table, ((0, 0),) * (table.ndim - 2) + more)


def side_by_side(*parts):
    return np.concatenate([np.pad(part, ((0, 0), (0, -part.shape[1] % 128))) for part in parts], 1)


def corner_columns(inner_table, elements):
    points = inner_table.shape[0]
    table = np.zeros((elements * points, 256))
    for corner in range(2):
        for lane in range(128):
            element = (lane % elements - corner) % elements
            table[element * points : (element + 1) * points, corner * 128 + lane] = inner_table[:, corner]
    return table


def build_tables(n_gy, ez):
    p, q = ORDER + 1, MID_ORDER + 1
    fine, mid, low = gll_tables(ORDER), gll_tables(MID_ORDER), gll_tables(1)
    jf = interp_table(fine[0], mid[0])
    jm = interp_table(mid[0], low[0])
    k7, w7, s7, l7 = fine[2], np.diag(fine[1]), fine[3], fine[4]
    k3, w3, s3, l3 = mid[2], np.diag(mid[1]), mid[3], mid[4]
    pair, plain = {}, {}
    modes = p + 2
    a1 = blocks(s7.T, 2) @ line_extension(p, 2, False)
    own, sides = a1[:, : 2 * p], {-1: a1[:, 2 * p : 2 * p + 2], 1: a1[:, 2 * p + 2 :]}
    pair["wo"] = np.kron(own, own)
    parts = []
    for dx, dy in RING:
        if dy == 0:
            parts.append(np.kron(sides[dx], own))
        elif dx == 0:
            parts.append(np.concatenate([np.kron(own, sides[dy][:, at : at + 1]) for at in range(2)], 1))
        else:
            parts.append(np.pad(np.kron(sides[dx], sides[dy]), ((0, 0), (0, 4))))
    pair["wh"] = np.concatenate(parts, 1)
    pair["az"] = (blocks(s7.T, ez) @ line_extension(p, ez, True)).T
    inner = s7[1:-1]
    raw = blocks(inner, 2)
    back = np.array(raw)
    back[p - 1] = back[p] = raw[p - 1] + raw[p]
    face = {-1: raw[:1], 1: raw[-1:]}
    pair["bo"] = np.kron(back, back)
    parts, rows = [], []
    edge = {-1: 0, 1: 2 * p - 1}
    for tx, ty in RING:
        scatter = np.zeros((16, 256)) if 0 in (tx, ty) else np.zeros((8, 256))
        if ty == 0:
            parts.append(np.kron(face[tx], back))
            for at in range(16):
                scatter[at, edge[tx] * 16 + at] = 1
        elif tx == 0:
            parts.append(np.kron(back, face[ty]))
            for at in range(16):
                scatter[at, at * 16 + edge[ty]] = 1
        else:
            parts.append(np.pad(np.kron(face[tx], face[ty]), ((0, 7), (0, 0))))
            scatter[0, edge[tx] * 16 + edge[ty]] = 1
        rows.append(scatter)
    pair["bf"] = np.concatenate(parts, 0)
    scat = np.concatenate(rows, 0).T
    plain["scat"] = (scat, BF)
    bz = z_back(inner, p, ez)
    pair["bz"] = bz

    def weights(points):
        line = line_weights(points, 2)
        low_side, high_side = np.zeros(2 * points), np.zeros(2 * points)
        low_side[0], high_side[-1] = 0.5, 0.5
        return np.stack([np.kron(line, line), np.kron(line, low_side), np.kron(line, high_side)], 1)

    wt7, wt3 = weights(p), weights(q)
    columns = np.zeros((256, 128))
    columns[:, 0:3] = wt7
    columns[:96, 3:6] = scat.T @ wt7
    columns[:64, 6:9] = wt3
    columns[:, 9] = np.kron(np.tile(fine[1], 2), np.tile(fine[1], 2))
    plain["columns"] = (columns, F32)

    def three(stiff, mass, count):
        stiff, mass = blocks(stiff, count), blocks(mass, count)
        return np.kron(stiff, mass), np.kron(mass, stiff), np.kron(mass, mass)

    la = np.concatenate(three(jf.T @ k7, jf.T @ w7, 2), 0)
    ra = side_by_side(blocks(w7 @ jf, ez), blocks(k7 @ jf, ez))
    pair["la"] = la
    pair["lar"] = la @ scat
    pair["bzra"] = bz @ ra
    pair["jxy"] = np.kron(blocks(jf.T, 2), blocks(jf.T, 2))
    pair["jz"] = blocks(jf, ez)
    k7x, k7y, _ = three(k7, w7, 2)
    pair["k7"] = np.concatenate([k7x, k7y], 0)
    pair["kz7"] = blocks(k7, ez)
    plain["wz7"] = (np.tile(np.tile(fine[1], ez)[None], (8, 1)), F32)
    pair["lp"] = np.concatenate(three(k7 @ jf, w7 @ jf, 2), 0)
    pair["rp"] = side_by_side(blocks((w7 @ jf).T, ez), blocks((k7 @ jf).T, ez))
    pair["pxy"] = np.kron(blocks(jf, 2), blocks(jf, 2))
    pair["pz"] = blocks(jf.T, ez)

    def factor_rows(elements, scale):
        table = np.zeros((len(elements), 16))
        for at, (ex, ey) in enumerate(elements):
            for d in range(3):
                if scale[d] is not None:
                    table[at, d * 4 + ex * 2 + ey] = scale[d][at]
        return table

    def grid_elements(per):
        return [(x // per, y // per) for x in range(2 * per) for y in range(2 * per)]

    def direction_rows(elements):
        one = np.ones(len(elements))
        return np.concatenate([factor_rows(elements, [one if d == e else None for e in range(3)]) for d in range(3)], 0)

    spread = lambda per: np.kron(np.eye(ez), np.ones((1, per)))
    plain["e7"] = (direction_rows(grid_elements(p)), BF)
    plain["e3"] = (direction_rows(grid_elements(q)), BF)
    plain["e1"] = (direction_rows(grid_elements(2)), BF)
    plain["s64"] = (spread(p), BF)
    plain["s32"] = (spread(q), BF)
    plain["s256"] = (corner_columns(np.ones((1, 2)), ez), BF)
    grid = grid_elements(modes)
    li = np.array([l7[x % modes] for x in range(2 * modes) for y in range(2 * modes)])
    lj = np.array([l7[y % modes] for x in range(2 * modes) for y in range(2 * modes)])
    pair["ld7"] = factor_rows(grid, [li, lj, None])
    plain["le7"] = (factor_rows(grid, [None, None, np.ones(len(grid))]), BF)
    plain["s80"] = (spread(modes), BF)
    pair["sl80"] = spread(modes) * np.tile(l7, ez)[None]

    m3 = q + 2
    ext = np.zeros((4, m3, 6 * q))
    for element in range(4):
        start = q * (element + 1)
        ext[element, 0, start - 2] += 1
        for at in range(q):
            ext[element, 1 + at, start + at] += 1
        ext[element, 1, start - 1] += 1
        ext[element, q, start + q] += 1
        ext[element, q + 1, start + q + 1] += 1
    a1m = blocks(s3.T, 4) @ ext.reshape(4 * m3, 6 * q)
    order = RING + ((0, 0),)
    span = lambda d: slice((d + 1) * 2 * q, (d + 2) * 2 * q)
    wm = [np.kron(a1m[:, span(dx)], a1m[:, span(dy)]) for dx, dy in order]
    pair["wmn"] = np.concatenate(wm[:8], 1)
    pair["wmo"] = wm[8]
    pair["azm"] = (blocks(s3.T, ez) @ line_extension(q, ez, True)).T
    inner3 = s3[1:-1]
    raw3 = blocks(inner3, 4)
    back3 = np.array(raw3[q : 3 * q])
    for at in (q - 1, 2 * q - 1, 3 * q - 1):
        total = raw3[at] + raw3[at + 1]
        for row in (at, at + 1):
            if q <= row < 3 * q:
                back3[row - q] = total
    bm = np.kron(back3, back3)
    pair["bm"] = bm
    bzm = z_back(inner3, q, ez)
    pair["bzm"] = bzm
    ll = np.concatenate(three(jm.T @ k3, jm.T @ w3, 2), 0)
    pair["lb"] = np.concatenate([ll @ ((wt3[:, 0] + extra)[:, None] * bm) for extra in (0, wt3[:, 1], wt3[:, 2])], 0)
    pair["rb"] = bzm @ np.concatenate([corner_columns(w3 @ jm, ez), corner_columns(k3 @ jm, ez)], 1)
    pair["jl"] = np.kron(blocks(jm.T, 2), blocks(jm.T, 2))
    pair["rj"] = corner_columns(jm, ez)
    place = {direction: at for at, direction in enumerate(order)}

    def ring_row(ex, ey, d):
        dx, dy = ex // 2 - 1, ey // 2 - 1
        return place[(dx, dy)] * 16 + d * 4 + (ex % 2) * 2 + ey % 2

    ld3, le3 = np.zeros((576, 144)), np.zeros((576, 144))
    for x in range(24):
        for y in range(24):
            ex, ey = x // m3 + 1, y // m3 + 1
            ld3[x * 24 + y, ring_row(ex, ey, 0)] = l3[x % m3]
            ld3[x * 24 + y, ring_row(ex, ey, 1)] = l3[y % m3]
            le3[x * 24 + y, ring_row(ex, ey, 2)] = 1
    pair["ld3"] = ld3
    plain["le3"] = (le3, BF)
    plain["s48"] = (spread(m3), BF)
    pair["sl48"] = spread(m3) * np.tile(l3, ez)[None]
    er = np.zeros((3, 9, 2 * q, 2 * q, 144))
    for at in range(9):
        for x in range(2 * q):
            for y in range(2 * q):
                for d in range(3):
                    er[d, at, x, y, at * 16 + d * 4 + (x // q) * 2 + y // q] = 1
    plain["er"] = (er.reshape(3 * 576, 144), BF)
    pair["k3"] = np.concatenate(three(k3, w3, 2), 0)
    pair["rk3"] = side_by_side(blocks(w3, ez), blocks(k3, ez))
    vertex_line = lambda table: np.array(
        [[table[at % q, v - at // q] if 0 <= v - at // q <= 1 else 0.0 for v in range(8)] for at in range(6 * q)]
    )
    stiff1, mass1, plain1 = vertex_line(k3 @ jm), vertex_line(w3 @ jm), vertex_line(jm)

    def vertex_columns(left, right, dx, dy):
        table = np.zeros((64, 4, 4, 8))
        for iy in range(4):
            for ix, ahead in enumerate(AHEAD):
                for x in range(2):
                    for y in range(2):
                        table[:, iy, ix, x * 2 + y] = np.kron(
                            left[span(dx), (ahead + 1) * 2 + x], right[span(dy), iy * 2 + y]
                        )
        return table.reshape(64, 128)

    pair["lc"] = np.concatenate(
        [
            vertex_columns(left, right, dx, dy)
            for left, right in ((stiff1, mass1), (mass1, stiff1), (mass1, mass1))
            for dx, dy in order
        ],
        0,
    )
    pair["jc"] = vertex_columns(plain1, plain1, 0, 0)

    def z_vertices(table):
        result = np.zeros((ez, ez * q))
        for element in range(ez):
            for at in range(q):
                result[element, element * q + at] += table[at, 0]
                result[(element + 1) % ez, element * q + at] += table[at, 1]
        return np.tile(result, (4, 1))

    pair["rc"] = side_by_side(z_vertices(w3 @ jm), z_vertices(k3 @ jm))
    pair["rcj"] = z_vertices(jm)
    mask, left = np.zeros((n_gy, 16, 128)), np.zeros((n_gy, 16, 16))
    for gy in range(n_gy):
        for row in range(16):
            vx, vy = row // 8 + row // 4 % 2, row // 2 % 2 + row % 2
            owner = gy + vy // 2
            if owner < n_gy:
                first = owner * 32 + (vx % 2) * 16 + (vy % 2) * 8
                mask[gy, row, first % 128 : first % 128 + 8] = 1
                left[gy, first // 128 + 4 * (vx // 2), row] = 1
    plain["mask"] = (mask.reshape(-1, 128), F32)
    plain["left"] = (left.reshape(-1, 16), BF)
    chosen = np.zeros((8, 32))
    select = np.zeros((32, 8))
    for lane in range(32):
        chosen[lane // 8, lane] = 1
        select[lane, lane % 8] = 1
    plain["chosen"] = (chosen, F32)
    plain["select"] = (select, BF)
    tables = {}
    for name, table in pair.items():
        table = fitted(np.asarray(table, np.float64), name in RIGHT)
        high = table.astype(ml_dtypes.bfloat16)
        tables[name] = np.stack([high, (table - high.astype(np.float64)).astype(ml_dtypes.bfloat16)])
    for name, (table, kind) in plain.items():
        table = fitted(np.asarray(table), name in RIGHT)
        tables[name] = table.astype(ml_dtypes.bfloat16 if kind is BF else np.float32)[None]
    return tables


STAGES = (
    (
        "columns", "wo", "jxy", "jz", "s80", "sl80", "ld7", "le7", "e7", "e3", "e1", "s64", "s32", "s256",
        "wz7", "chosen", "mask",
    ),
    ("wh", "az", "bf", "bo", "la", "bzra", "ld3", "le3", "s48", "sl48", "er", "lar"),
    (
        "wmo", "jl", "rj", "scat", "bz", "k7", "kz7", "wmn", "azm", "lb", "rb", "left", "bm", "bzm", "select",
        "rk3", "k3", "lc", "rc", "jc", "rcj", "rp", "lp", "pxy", "pz",
    ),
)


def pack(tables):
    stacks, places = {}, {}
    for stage, names in enumerate(STAGES):
        for name in names:
            table = tables[name]
            key = (stage, table.dtype.name, table.shape[-1])
            parts = stacks.setdefault(key, [])
            at = sum(part.shape[0] for part in parts)
            height = -(-table.shape[1] // 16) * 16
            for part in table:
                parts.append(np.pad(part, ((0, height - part.shape[0]), (0, 0))))
            places[name] = (key, at, height, table.shape[1])
    keys = tuple(stacks)
    return keys, [np.concatenate(stacks[key], 0) for key in keys], places


class Table:
    def __init__(self, ref, place):
        _, self.at, self.height, self.rows = place
        self.ref = ref
        self.shape = (2, self.rows, ref.shape[-1])

    def __getitem__(self, part):
        part = 0 if part is Ellipsis else part
        return self.ref[self.at + part * self.height : self.at + part * self.height + self.rows, :]

    def piece(self, part, start, rows):
        return self.ref[pl.ds(self.at + part * self.height + start, rows), :]


def dot(a, b):
    return jnp.dot(a, b, preferred_element_type=F32)


def split(x):
    high = x.astype(BF)
    return high, (x - high.astype(F32)).astype(BF)


def wide(x, lanes=128):
    if x.shape[1] == lanes:
        return x
    return jnp.concatenate([x, jnp.zeros((x.shape[0], lanes - x.shape[1]), x.dtype)], 1)


def tall(x, rows):
    if x.shape[0] == rows:
        return x
    return jnp.concatenate([x, jnp.zeros((rows - x.shape[0], x.shape[1]), x.dtype)], 0)


def left3(table, x):
    high, rest = split(tall(x, table.shape[-1]))
    return dot(table[0], high) + dot(table[0], rest) + dot(table[1], high)


def terms3(table, x):
    high, rest = split(tall(x, table.shape[-1]))
    rows = table.shape[1] // 3
    results = []
    for term in range(3):
        lanes = slice(128, 256) if term == 2 else slice(0, 128)
        main, small = table.piece(0, term * rows, rows), table.piece(1, term * rows, rows)
        results.append(dot(main, high[:, lanes]) + dot(main, rest[:, lanes]) + dot(small, high[:, lanes]))
    return results


def right3(x, table):
    high, rest = split(wide(x, table.shape[-2]))
    return dot(high, table[0]) + dot(rest, table[0]) + dot(high, table[1])


def left2(table, x):
    high, rest = split(tall(x, table.shape[-1]))
    return dot(table[...], high) + dot(table[...], rest)


def right2(x, table):
    high, rest = split(wide(x, table.shape[-2]))
    return dot(high, table[...]) + dot(rest, table[...])


KEPT = {
    "fine_f": (768, 128), "mid_f": (192, 128), "low_f": (48, 256), "ring_f": (1728, 128), "inverse7": (400, 128),
    "inverse3": (576, 128), "wt7": (256, 128), "wr7": (96, 128), "wt3": (64, 128), "base_mid": (64, 128),
    "base_low": (16, 256), "local": (256, 128), "first_fine": (256, 128), "base_fine": (256, 128),
    "first_mid": (64, 128), "modal": (400, 128), "modal3": (576, 128), "own_part": (192, 128), "base_ring": (576, 128),
    "ww7": (256, 128),
}


def cycle_kernel(keys, places, n_gx, n_gy, *refs):
    r_hbm, len_hbm, inv_hbm = refs[:3]
    count = len(keys)
    packed = refs[3 : 3 + count]
    out_fine, out_mid, out_low = refs[3 + count : 6 + count]
    stores = refs[6 + count : 6 + 2 * count]
    (
        r_ref, len_ref, inv_ref, rs, fs, hb1, fb1, rm, fm, hb2, fb2, hs1, hs2, st1, st2, held, gs, gb, cb,
        send_sem, recv_sem, gsend, grecv, csend, crecv, in_sem, table_sem,
    ) = refs[6 + 2 * count : -len(KEPT)]
    inputs = [
        pltpu.make_async_copy(source, target, in_sem.at[at])
        for at, (source, target) in enumerate(((len_hbm, len_ref), (r_hbm, r_ref), (inv_hbm, inv_ref)))
    ]
    loads = [pltpu.make_async_copy(packed[at], stores[at], table_sem.at[at]) for at in range(count)]
    for load in inputs + loads:
        load.start()

    def ready(stage):
        for key, load in zip(keys, loads):
            if key[0] == stage:
                load.wait()

    kept = dict(zip(KEPT, refs[-len(KEPT) :]))

    def keep(name, value):
        kept[name][...] = value
        return kept[name]

    t = {name: Table(stores[keys.index(place[0])], place) for name, place in places.items()}
    gx, gy = lax.axis_index("gx"), lax.axis_index("gy")
    last = n_gy - 1
    at_bottom, at_top = gy == 0, gy == last
    not_bottom, not_top = gy > 0, gy < last
    sent = {0: None, 1: not_bottom, 2: not_top}

    def guarded(condition, action):
        if condition is None:
            action()
        else:
            pl.when(condition)(action)

    def exchange(phase, source, buffer, rows):
        at = offsets(rows)

        def group(number):
            def action():
                for index in range(*GROUPS[number]):
                    tx, ty = RING[index]
                    slot = RING.index((-tx, -ty))
                    landing = (0, 2, 1)[number]
                    pltpu.make_async_remote_copy(
                        src_ref=source(index),
                        dst_ref=buffer.at[pl.ds(at[slot], rows[slot])],
                        send_sem=send_sem.at[phase, number],
                        recv_sem=recv_sem.at[phase, landing],
                        device_id=(lax.rem(gx + (tx + n_gx), n_gx), gy + ty),
                        device_id_type=MESH,
                    ).start()

            return action

        for number in range(3):
            guarded(sent[number], group(number))

    def settle(phase, sems, buffer, rows):
        at = offsets(rows)
        for number in range(3):
            first, end = GROUPS[number]
            piece = buffer.at[pl.ds(at[first], at[end] - at[first])]
            guarded(sent[number], lambda: pltpu.make_async_copy(piece, piece, sems.at[phase, number]).wait())

    def clear(number):
        first, end = GROUPS[number]
        for buffer, rows in (
            (fs, (16,) * 8), (hb1, HALO_ROWS), (fb1, FACE_ROWS), (rm, (64,) * 8),
            (fm, (64,) * 8), (hb2, HALO_ROWS), (fb2, FACE_ROWS),
        ):
            at = offsets(rows)
            buffer[at[first] : at[end], :] = jnp.zeros((at[end] - at[first], buffer.shape[1]), F32)

    @pl.when(at_bottom)
    def _():
        clear(1)
        cb[0:32, :] = jnp.zeros((32, 32), F32)

    @pl.when(at_top)
    def _():
        clear(2)
        cb[64:96, :] = jnp.zeros((32, 32), F32)

    @pl.when(gy >= last - 1)
    def _():
        cb[96:128, :] = jnp.zeros((32, 32), F32)

    def halo(field, stage):
        at = offsets(HALO_ROWS)
        for index, (tx, ty) in enumerate(RING):
            xs, ys = (14, 0)[tx < 0], (14, 0)[ty < 0]
            if ty == 0:
                stage[at[index] : at[index] + 32, :] = field[xs : xs + 2, :, :].reshape(32, 64)
            elif tx == 0:
                stage[at[index] : at[index] + 16, :] = field[:, ys, :]
                stage[at[index] + 16 : at[index] + 32, :] = field[:, ys + 1, :]
            else:
                stage[at[index] : at[index] + 2, :] = field[xs, ys : ys + 2, :]
                stage[at[index] + 2 : at[index] + 4, :] = field[xs + 1, ys : ys + 2, :]
                stage[at[index] + 4 : at[index] + 8, :] = jnp.zeros((4, 64), F32)

    at_halo, at_face = offsets(HALO_ROWS), offsets(FACE_ROWS)

    inputs[0].wait()
    own_f = 8 * 16
    for ex in range(2):
        a, b, c = len_ref[0, ex], len_ref[1, ex], len_ref[2, ex]
        fs[own_f + ex * 2 : own_f + ex * 2 + 2, :] = b * c / (2.0 * a)
        fs[own_f + 4 + ex * 2 : own_f + 6 + ex * 2, :] = a * c / (2.0 * b)
        fs[own_f + 8 + ex * 2 : own_f + 10 + ex * 2, :] = a * b / (2.0 * c)
    fs[own_f + 12 : own_f + 16, :] = jnp.zeros((4, 8), F32)
    inputs[1].wait()
    halo(r_ref, hs1)
    exchange(1, lambda index: hs1.at[pl.ds(at_halo[index], HALO_ROWS[index])], hb1, HALO_ROWS)
    exchange(0, lambda index: fs.at[pl.ds(own_f, 16)], fs, (16,) * 8)

    bottom_on = jnp.where(at_bottom, 1.0, 0.0)
    top_on = jnp.where(at_top, 1.0, 0.0)

    ready(0)
    columns = t["columns"][...]

    def wall_weight(rows, at):
        piece = columns[0:rows]
        return piece[:, at : at + 1] + bottom_on * piece[:, at + 1 : at + 2] + top_on * piece[:, at + 2 : at + 3]

    wt7 = keep("wt7", jnp.broadcast_to(wall_weight(256, 0), (256, 128)))
    wr7 = keep("wr7", jnp.broadcast_to(wall_weight(96, 3), (96, 128)))
    wt3 = keep("wt3", jnp.broadcast_to(wall_weight(64, 6), (64, 128)))
    ww7 = keep("ww7", jnp.broadcast_to(columns[:, 9:10], (256, 128)))
    r = wide(r_ref[...].reshape(256, 64))
    f_own = wide(fs[own_f : own_f + 16, :])
    d7 = left3(t["ld7"], right2(f_own, t["s80"])) + left2(t["le7"], right3(f_own, t["sl80"]))
    inverse7 = keep("inverse7", jnp.where(d7 > 0.0, 1.0 / jnp.where(d7 > 0.0, d7, 1.0), 0.0))
    modal = keep("modal", left3(t["wo"], r))
    base_mid = keep("base_mid", right3(left3(t["jxy"], r), t["jz"]))
    fine_f = keep("fine_f", left2(t["e7"], right2(f_own, t["s64"])))
    mid_f = keep("mid_f", left2(t["e3"], right2(f_own, t["s32"])))
    low_f = keep("low_f", left2(t["e1"], right2(f_own, t["s256"])))

    def fine_back(modal, buffer, stage, phase):
        modal = right3(modal, t["az"]) * inverse7[...]
        stage[...] = left3(t["bf"], modal)[:, : stage.shape[1]]
        exchange(phase, lambda index: stage.at[pl.ds(at_face[index], FACE_ROWS[index])], buffer, FACE_ROWS)
        return left3(t["bo"], modal)

    ready(1)
    settle(1, recv_sem, hb1, HALO_ROWS)
    modal = modal[...] + left3(t["wh"], wide(hb1[...]))
    local = keep("local", fine_back(modal, fb1, st1, 2) * wt7[...])
    own_part = keep("own_part", jnp.concatenate(terms3(t["la"], right3(local[...], t["bzra"])), 0))
    settle(0, recv_sem, fs, (16,) * 8)
    ring_f = wide(fs[...])
    d3 = left3(t["ld3"], right2(ring_f, t["s48"])) + left2(t["le3"], right3(ring_f, t["sl48"]))
    inverse3 = keep("inverse3", jnp.where(d3 > 0.0, 1.0 / jnp.where(d3 > 0.0, d3, 1.0), 0.0))
    ring_f = keep("ring_f", left2(t["er"], right2(ring_f, t["s32"])))

    settle(2, recv_sem, fb1, FACE_ROWS)
    faces = wide(fb1[...]) * wr7[...]
    face_part = terms3(t["lar"], right3(faces, t["bzra"]))
    residual_mid = base_mid[...] - (
        mid_f[0:64] * (own_part[0:64] + face_part[0])
        + mid_f[64:128] * (own_part[64:128] + face_part[1])
        + mid_f[128:192] * (own_part[128:192] + face_part[2])
    )
    rm[512:576, :] = residual_mid[:, 0:32]
    exchange(3, lambda index: rm.at[pl.ds(512, 64)], rm, (64,) * 8)

    ready(2)
    own_modal = keep("modal3", left3(t["wmo"], residual_mid))
    base_low = keep("base_low", right3(left3(t["jl"], residual_mid), t["rj"]))
    first_fine = keep("first_fine", right3(local[...] + left2(t["scat"], faces), t["bz"]))
    massed = left3(t["k7"], first_fine[...] * t["wz7"][...][0:1])
    along_z = right3(first_fine[...], t["kz7"]) * ww7[...]
    base_fine = keep(
        "base_fine",
        wide(r_ref[...].reshape(256, 64))
        - (fine_f[0:256] * massed[0:256] + fine_f[256:512] * massed[256:512] + fine_f[512:768] * along_z),
    )

    settle(3, recv_sem, rm, (64,) * 8)
    modal3 = own_modal[...] + left3(t["wmn"], wide(rm[0:512, :]))
    modal3 = right3(modal3, t["azm"]) * inverse3[...]
    variant = jnp.where(at_bottom, 1, jnp.where(at_top, 2, 0))
    rows = pl.multiple_of(variant * 48, 16)
    high, rest = split(tall(modal3, t["lb"].shape[-1]))
    lb_high, lb_rest = t["lb"].piece(0, rows, 48), t["lb"].piece(1, rows, 48)
    low = dot(lb_high, high) + dot(lb_high, rest) + dot(lb_rest, high)
    low = right3(low, t["rb"])
    low = base_low[...] - (
        low_f[0:16] * low[0:16, 0:256] + low_f[16:32] * low[16:32, 0:256] + low_f[32:48] * low[32:48, 256:512]
    )
    wall = pl.multiple_of(gy * 16, 16)
    high, rest = split(tall((low[:, 0:128] + low[:, 128:256]) * t["mask"].piece(0, wall, 16), 128))
    lefts = t["left"].piece(0, wall, 16)
    message = (dot(lefts, high) + dot(lefts, rest))[0:8]
    gs[...] = message

    def send_slab(step, ahead):
        slot = step + jnp.where(ahead == 0, -1, n_gy - 1)
        pltpu.make_async_remote_copy(
            src_ref=gs,
            dst_ref=gb.at[slot],
            send_sem=gsend,
            recv_sem=grecv,
            device_id=(lax.rem(gx + ahead, n_gx), lax.rem(gy + step, n_gy)),
            device_id_type=MESH,
        ).start()

    for step in range(1, n_gy):
        send_slab(step, 0)
    for step in range(n_gy):
        send_slab(step, 1)

    first_mid = keep("first_mid", right3(left3(t["bm"], modal3) * wt3[...], t["bzm"]))
    fm[512:576, :] = first_mid[:, 0:32]
    exchange(4, lambda index: fm.at[pl.ds(512, 64)], fm, (64,) * 8)

    pltpu.make_async_copy(gb, gb, grecv).wait()
    here = gs[...] + jnp.sum(gb[0 : n_gy - 1], axis=0)
    behind = jnp.sum(gb[n_gy - 1 :], axis=0)
    inputs[2].wait()
    chunks = inv_ref.shape[2] // 128
    vector = here + pltpu.roll(behind, 4, 0)
    row = lax.broadcasted_iota(jnp.int32, (8, 128), 0)
    vector = jnp.concatenate([jnp.where(row == chunk, vector, 0.0) for chunk in range(chunks)], 1)
    vector = tall(vector, 16).astype(BF)
    inverse = tall(inv_ref[0], 128)
    solved = lax.dot_general(vector, inverse, (((1,), (1,)), ((), ())), preferred_element_type=F32)
    solved = jnp.sum(solved, axis=0, keepdims=True)
    solved = jnp.broadcast_to(solved, (8, 128)) * t["chosen"][...]
    own_c = (4 + 3) * 8
    cb[own_c : own_c + 8, :] = solved[:, 0:32]

    def send_correction(iy):
        def action():
            for ix, ahead in enumerate(AHEAD):
                if (ahead, iy - 1) != (0, 0):
                    pltpu.make_async_remote_copy(
                        src_ref=cb.at[pl.ds(own_c, 8)],
                        dst_ref=cb.at[pl.ds((iy * 4 + ix) * 8, 8)],
                        send_sem=csend.at[iy],
                        recv_sem=crecv.at[iy],
                        device_id=(lax.rem(gx - ahead + n_gx, n_gx), gy - (iy - 1)),
                        device_id_type=MESH,
                    ).start()

        return action

    to_group = (not_top, None, not_bottom, gy > 1)
    from_group = (not_bottom, None, not_top, gy < last - 1)
    for iy in range(4):
        guarded(to_group[iy], send_correction(iy))

    def settle_corrections(sems, conditions):
        for iy in range(4):
            piece = cb.at[pl.ds(iy * 32, 24 if iy == 1 else 32)]
            guarded(conditions[iy], lambda: pltpu.make_async_copy(piece, piece, sems.at[iy]).wait())

    low_out = right2(tall(solved, 16), t["select"])
    out_low[0] = low_out[0:2, 0:8]
    out_low[1] = low_out[2:4, 0:8]
    settle(4, recv_sem, fm, (64,) * 8)
    turned = right3(wide(fm[...]), t["rk3"])
    parts = []
    for at in range(9):
        piece = terms3(t["k3"], turned[at * 64 : (at + 1) * 64])
        parts.append(
            wide(rm[at * 64 : (at + 1) * 64, :])
            - (
                ring_f[at * 64 : (at + 1) * 64] * piece[0]
                + ring_f[576 + at * 64 : 576 + (at + 1) * 64] * piece[1]
                + ring_f[1152 + at * 64 : 1152 + (at + 1) * 64] * piece[2]
            )
        )
    base_ring = keep("base_ring", jnp.concatenate(parts, 0))
    modal3 = keep("modal3", left3(t["wmn"], base_ring[0:512]) + left3(t["wmo"], base_ring[512:576]))

    settle_corrections(crecv, from_group)
    corrections = wide(cb[...])
    change = terms3(t["lc"], right3(corrections, t["rc"]))
    change = (
        ring_f[0:576] * change[0]
        + ring_f[576:1152] * change[1]
        + ring_f[1152:1728] * change[2]
    )
    modal3 = modal3[...] - left3(t["wmn"], change[0:512]) - left3(t["wmo"], change[512:576])
    modal3 = right3(modal3, t["azm"]) * inverse3[...]
    held[0:64, :] = first_mid[...] + right3(left3(t["jc"], corrections), t["rcj"])
    mid_result = held[0:64, :] + right3(left3(t["bm"], modal3) * wt3[...], t["bzm"])

    turned = right3(mid_result, t["rp"])
    turned = terms3(t["lp"], turned)
    residual = base_fine[...] - (
        fine_f[0:256] * turned[0]
        + fine_f[256:512] * turned[1]
        + fine_f[512:768] * turned[2]
    )
    rs[...] = residual[:, 0:64].reshape(16, 16, 64)
    halo(rs, hs2)
    exchange(5, lambda index: hs2.at[pl.ds(at_halo[index], HALO_ROWS[index])], hb2, HALO_ROWS)
    out_mid[...] = mid_result[:, 0:32].reshape(8, 8, 32)
    modal = keep("modal", left3(t["wo"], residual))
    held[...] = first_fine[...] + right3(left3(t["pxy"], mid_result), t["pz"])
    settle(5, recv_sem, hb2, HALO_ROWS)
    modal = modal[...] + left3(t["wh"], wide(hb2[...]))
    local = fine_back(modal, fb2, st2, 6) * wt7[...]
    held[...] = held[...] + right3(local, t["bz"])
    settle(6, recv_sem, fb2, FACE_ROWS)
    result = held[...] + left2(t["scat"], right3(wide(fb2[...]) * wr7[...], t["bz"]))
    out_fine[...] = result[:, 0:64].reshape(16, 16, 64)

    for phase, buffer, rows in (
        (0, fs, (16,) * 8), (1, hb1, HALO_ROWS), (2, fb1, FACE_ROWS), (3, rm, (64,) * 8),
        (4, fm, (64,) * 8), (5, hb2, HALO_ROWS), (6, fb2, FACE_ROWS),
    ):
        settle(phase, send_sem, buffer, rows)
    pltpu.make_async_copy(gb, gb, gsend).wait()
    settle_corrections(csend, to_group)


def shards(n_gx, n_gy, local_residual, lengths, coarse_inverse):
    keys, packed, places = pack(build_tables(n_gy, lengths.shape[3]))
    vmem = pl.BlockSpec(memory_space=pltpu.VMEM)
    modes = lengths.shape[3] * (ORDER + 3)
    scratch = [pltpu.VMEM(table.shape, BF if key[1] == "bfloat16" else F32) for key, table in zip(keys, packed)]
    scratch += [
        pltpu.VMEM(local_residual.shape, F32),
        pltpu.VMEM(lengths.shape, F32),
        pltpu.VMEM(coarse_inverse.shape, BF),
        pltpu.VMEM((16, 16, 64), F32),
        pltpu.VMEM((144, 8), F32),
        pltpu.VMEM((160, 64), F32),
        pltpu.VMEM((96, modes), F32),
        pltpu.VMEM((576, 32), F32),
        pltpu.VMEM((576, 32), F32),
        pltpu.VMEM((160, 64), F32),
        pltpu.VMEM((96, modes), F32),
        pltpu.VMEM((160, 64), F32),
        pltpu.VMEM((160, 64), F32),
        pltpu.VMEM((96, modes), F32),
        pltpu.VMEM((96, modes), F32),
        pltpu.VMEM((256, 128), F32),
        pltpu.VMEM((8, 128), F32),
        pltpu.VMEM((2 * n_gy - 1, 8, 128), F32),
        pltpu.VMEM((128, 32), F32),
        pltpu.SemaphoreType.DMA((7, 3)),
        pltpu.SemaphoreType.DMA((7, 3)),
        pltpu.SemaphoreType.DMA,
        pltpu.SemaphoreType.DMA,
        pltpu.SemaphoreType.DMA((4,)),
        pltpu.SemaphoreType.DMA((4,)),
        pltpu.SemaphoreType.DMA((3,)),
        pltpu.SemaphoreType.DMA((len(keys),)),
    ]
    scratch += [pltpu.VMEM(shape, F32) for shape in KEPT.values()]
    return pl.pallas_call(
        functools.partial(cycle_kernel, keys, places, n_gx, n_gy),
        out_shape=(
            jax.ShapeDtypeStruct((16, 16, 64), F32),
            jax.ShapeDtypeStruct((8, 8, 32), F32),
            jax.ShapeDtypeStruct((2, 2, 8), F32),
        ),
        in_specs=[pl.BlockSpec(memory_space=pl.ANY)] * (3 + len(keys)),
        out_specs=(vmem, vmem, vmem),
        scratch_shapes=scratch,
        compiler_params=pltpu.CompilerParams(has_side_effects=True, vmem_limit_bytes=60 * 1024 * 1024),
    )(local_residual, lengths, coarse_inverse, *[jnp.asarray(table) for table in packed])


def solution(mesh):
    in_specs = (P("gx", "gy", None), P(None, "gx", "gy", None), P("gx", "gy", None))
    out_specs = (P("gx", "gy", None), P("gx", "gy", None), P("gx", "gy", None))
    return jax.shard_map(
        functools.partial(shards, mesh.shape["gx"], mesh.shape["gy"]),
        mesh=mesh,
        in_specs=in_specs,
        out_specs=out_specs,
        check_vma=False,
    )
```

time: 410 us -> 84.4 us (0.21); the launches traced: 402 us -> 84.2 us
  starting transfers between devices: 198 us -> 0 us
  local copies, waits for them, and re-layouts: 87.4 us -> 4.19 us
  Pallas kernels: 0 us -> 79.4 us
  blocking collectives: 42.8 us -> 0 us
  waiting for transfers between devices: 26.1 us -> 0 us
  other arithmetic: 22.6 us -> 0 us
  matrix products: 20 us -> 0 us
  between operations: 4.82 us -> 0.64 us
    ppermute x36 -> x0, starting transfers between devices: 198 us -> none  [the longest x16 102 us: extended_2(): lax.ppermute(tail, axis, [(i, (i + 1) % count) for i in range(count)])]
    pallas_call x0 -> x1, Pallas kernels: none -> 79.4 us  [shards(): pl.pallas_call(functools.partial(cycle_kernel, keys, places, n_gx, n_gy),...]
    unnamed x1 -> x0, blocking collectives: 42.8 us -> none
    reshape x43 -> x0, local copies, waits for them, and re-layouts: 29.4 us -> none  [the longest x8 14.8 us: extend(): section_three.transpose(1, 3, 5, 0, 2, 4)]
    slice x91 -> x0, local copies, waits for them, and re-layouts: 28.1 us -> none  [the longest x12 15.4 us: extend(): left_part = jnp.roll(own_part[..., points - 2], 1, 4)]
    ppermute x36 -> x0, waiting for transfers between devices: 26.1 us -> none  [the longest x2 10.2 us: from_behind_2(): lax.ppermute(value, axis, [(source, source + steps) for source in range(i...]
    dot_general x49 -> x0, matrix products: 20 us -> none  [the longest x4 2.95 us: fast_solve(): modal = jnp.einsum('bj,ibcE->ijcE', basis_table, modal, precision=PRECISE)]
    broadcast_in_dim x12 -> x0, local copies, waits for them, and re-layouts: 16.6 us -> none  [the longest x4 9.93 us: extend(): left_part[..., None]]
  transfers between devices with their start and end apart: 36 -> 0, of which waited for: 16 -> 0; matrix products, arithmetic and copies ran while one was open for 4% -> 0% of each run, Pallas kernels for 0% -> 0%
where the time goes in v1:
time: 84.4 us; the launch traced here: 84.2 us
  Pallas kernels  79.4 us (94%)
  local copies, waits for them, and re-layouts  4.19 us (5%)
    pallas_call x1, Pallas kernels, shards(): pl.pallas_call(functools.partial(cycle_kernel, keys, places, n_gx, n_gy),...  79.4 us
    unnamed x3, local copies, waits for them, and re-layouts  4.19 us

profile of v1, /device:TPU:7, one launch (start us, length us, event | category | flops | bytes accessed | tf_op | source)
XLA Modules:
  0.0 84.2 jit_solution(10838456136850061137)
XLA Ops:
  0.6 79.4 %shard_map.148 = (f32[16,16,64]{2,1,0:T(8,128)}, f32[8,8,32]{2,1,0:T(8,128)}, f32[2,2,8]{2,1,0:T(2,128)}) custom-call(f32[16,16,64]{2,1,0:T(8,128)} %refs_0_.1, f32[3,2,2,8]{3,2,1,0:T(2,128)} %refs_1_.1, bf16[1,32,512]{2,1,0:T(8,128)(2,1)} %refs_2_.1, f32[544,128]{1,0:T(8,128)} %constant.20.clone.refs_3_, bf16[1056,256]{1,0:T(8,128)(2,1)} %constant.21.clone.refs_4_, ...), custom_call_target="tpu_custom_call" | custom-call | tf_op jit(solution)/shard_map/pallas_call | solution.py:945
  80.0 1.6 %copy.19 = f32[16,16,64]{2,1,0:T(8,128)} copy(f32[16,16,64]{2,1,0:T(8,128)} %get-tuple-element.6) | data formatting | bytes 131072
  81.6 1.4 %copy.20 = f32[8,8,32]{2,1,0:T(8,128)} copy(f32[8,8,32]{2,1,0:T(8,128)} %get-tuple-element.7) | data formatting | bytes 16384
  83.0 1.2 %copy.21 = f32[2,2,8]{2,1,0:T(2,128)} copy(f32[2,2,8]{2,1,0:T(2,128)} %get-tuple-element.8) | data formatting | bytes 256

commit v2 on v1

--- a/solution.py
+++ b/solution.py
@@ -155,8 +155,8 @@
 RING = ((-1, 0), (1, 0), (0, -1), (-1, -1), (1, -1), (0, 1), (-1, 1), (1, 1))
 GROUPS = ((0, 2), (2, 5), (5, 8))
 AHEAD = (-1, 1, 2, 0)
-HALO_ROWS = (32, 32, 32, 8, 8, 32, 8, 8)
 FACE_ROWS = (16, 16, 16, 8, 8, 16, 8, 8)
+BLOCK_ROWS = (16,) * 8
 MESH = pl.DeviceIdType.MESH
 
 
@@ -247,15 +247,19 @@
     a1 = blocks(s7.T, 2) @ line_extension(p, 2, False)
     own, sides = a1[:, : 2 * p], {-1: a1[:, 2 * p : 2 * p + 2], 1: a1[:, 2 * p + 2 :]}
     pair["wo"] = np.kron(own, own)
-    parts = []
-    for dx, dy in RING:
-        if dy == 0:
-            parts.append(np.kron(sides[dx], own))
-        elif dx == 0:
-            parts.append(np.concatenate([np.kron(own, sides[dy][:, at : at + 1]) for at in range(2)], 1))
-        else:
-            parts.append(np.pad(np.kron(sides[dx], sides[dy]), ((0, 0), (0, 4))))
-    pair["wh"] = np.concatenate(parts, 1)
+    halves = []
+    for half in range(2):
+        layer = slice(half, half + 1)
+        parts = []
+        for dx, dy in RING:
+            if dy == 0:
+                parts.append(np.kron(sides[dx][:, layer], own))
+            elif dx == 0:
+                parts.append(np.kron(own, sides[dy][:, layer]))
+            else:
+                parts.append(np.pad(np.kron(sides[dx], sides[dy][:, layer]), ((0, 0), (0, 6))))
+        halves.append(np.concatenate(parts, 1))
+    pair["wh"] = side_by_side(*halves)
     pair["az"] = (blocks(s7.T, ez) @ line_extension(p, ez, True)).T
     inner = s7[1:-1]
     raw = blocks(inner, 2)
@@ -467,9 +471,14 @@
     for name, table in pair.items():
         table = fitted(np.asarray(table, np.float64), name in RIGHT)
         high = table.astype(ml_dtypes.bfloat16)
-        tables[name] = np.stack([high, (table - high.astype(np.float64)).astype(ml_dtypes.bfloat16)])
+        rest = (table - high.astype(np.float64)).astype(ml_dtypes.bfloat16)
+        if name in RIGHT:
+            tables[name] = np.block([[high, rest], [high, np.zeros_like(rest)]])[None]
+        else:
+            tables[name] = np.stack([high, rest])
     for name, (table, kind) in plain.items():
         table = fitted(np.asarray(table), name in RIGHT)
+        table = np.concatenate([table, table], 0) if name in RIGHT else table
         tables[name] = table.astype(ml_dtypes.bfloat16 if kind is BF else np.float32)[None]
     return tables
 
@@ -538,35 +547,38 @@
     return jnp.concatenate([x, jnp.zeros((rows - x.shape[0], x.shape[1]), x.dtype)], 0)
 
 
+def halves(x):
+    middle = x.shape[1] // 2
+    return x[:, :middle] + x[:, middle:]
+
+
+def exactly(main, small, x):
+    high, rest = split(x)
+    return halves(dot(main, jnp.concatenate([high, rest], 1))) + dot(small, high)
+
+
 def left3(table, x):
-    high, rest = split(tall(x, table.shape[-1]))
-    return dot(table[0], high) + dot(table[0], rest) + dot(table[1], high)
+    return exactly(table[0], table[1], tall(x, table.shape[-1]))
+
+
+def left2(table, x):
+    return halves(dot(table[...], jnp.concatenate(split(tall(x, table.shape[-1])), 1)))
 
 
 def terms3(table, x):
-    high, rest = split(tall(x, table.shape[-1]))
+    x = tall(x, table.shape[-1])
     rows = table.shape[1] // 3
-    results = []
-    for term in range(3):
-        lanes = slice(128, 256) if term == 2 else slice(0, 128)
-        main, small = table.piece(0, term * rows, rows), table.piece(1, term * rows, rows)
-        results.append(dot(main, high[:, lanes]) + dot(main, rest[:, lanes]) + dot(small, high[:, lanes]))
-    return results
+    first = exactly(table.piece(0, 0, 2 * rows), table.piece(1, 0, 2 * rows), x[:, 0:128])
+    third = exactly(table.piece(0, 2 * rows, rows), table.piece(1, 2 * rows, rows), x[:, 128:256])
+    return first[0:rows], first[rows:], third
 
 
 def right3(x, table):
-    high, rest = split(wide(x, table.shape[-2]))
-    return dot(high, table[0]) + dot(rest, table[0]) + dot(high, table[1])
-
-
-def left2(table, x):
-    high, rest = split(tall(x, table.shape[-1]))
-    return dot(table[...], high) + dot(table[...], rest)
+    return halves(right2(x, table))
 
 
 def right2(x, table):
-    high, rest = split(wide(x, table.shape[-2]))
-    return dot(high, table[...]) + dot(rest, table[...])
+    return dot(jnp.concatenate(split(wide(x)), 1), table[...])
 
 
 KEPT = {
@@ -585,9 +597,30 @@
     out_fine, out_mid, out_low = refs[3 + count : 6 + count]
     stores = refs[6 + count : 6 + 2 * count]
     (
-        r_ref, len_ref, inv_ref, rs, fs, hb1, fb1, rm, fm, hb2, fb2, hs1, hs2, st1, st2, held, gs, gb, cb,
+        r_ref, len_ref, inv_ref, rs, fs, hb1, fb1, rm, fm, rp, fp, hb2, fb2, hs1, hs2, st1, st2, held, gs, gb, cb,
         send_sem, recv_sem, gsend, grecv, csend, crecv, in_sem, table_sem,
     ) = refs[6 + 2 * count : -len(KEPT)]
+    gx, gy = lax.axis_index("gx"), lax.axis_index("gy")
+    last = n_gy - 1
+    barrier = pltpu.get_barrier_semaphore()
+
+    def greet(ahead, row):
+        pl.semaphore_signal(
+            barrier, inc=1, device_id=(lax.rem(gx + (ahead + n_gx), n_gx), row), device_id_type=MESH
+        )
+
+    def greet_if(row):
+        @pl.when((row >= 0) & (row <= last))
+        def _():
+            greet(1, row)
+            greet(2, row)
+
+    for step in range(-1, 3):
+        greet_if(gy + step)
+    for step in range(1, n_gy):
+        greet(0, lax.rem(gy + step, n_gy))
+    for step in range(n_gy):
+        greet(-1, lax.rem(gy + step, n_gy))
     inputs = [
         pltpu.make_async_copy(source, target, in_sem.at[at])
         for at, (source, target) in enumerate(((len_hbm, len_ref), (r_hbm, r_ref), (inv_hbm, inv_ref)))
@@ -608,8 +641,6 @@
         return kept[name]
 
     t = {name: Table(stores[keys.index(place[0])], place) for name, place in places.items()}
-    gx, gy = lax.axis_index("gx"), lax.axis_index("gy")
-    last = n_gy - 1
     at_bottom, at_top = gy == 0, gy == last
     not_bottom, not_top = gy > 0, gy < last
     sent = {0: None, 1: not_bottom, 2: not_top}
@@ -640,7 +671,7 @@
 
             return action
 
-        for number in range(3):
+        for number in (1, 2, 0):
             guarded(sent[number], group(number))
 
     def settle(phase, sems, buffer, rows):
@@ -653,8 +684,8 @@
     def clear(number):
         first, end = GROUPS[number]
         for buffer, rows in (
-            (fs, (16,) * 8), (hb1, HALO_ROWS), (fb1, FACE_ROWS), (rm, (64,) * 8),
-            (fm, (64,) * 8), (hb2, HALO_ROWS), (fb2, FACE_ROWS),
+            (fs, BLOCK_ROWS), (hb1, FACE_ROWS), (fb1, FACE_ROWS), (rp, BLOCK_ROWS),
+            (fp, BLOCK_ROWS), (hb2, FACE_ROWS), (fb2, FACE_ROWS),
         ):
             at = offsets(rows)
             buffer[at[first] : at[end], :] = jnp.zeros((at[end] - at[first], buffer.shape[1]), F32)
@@ -662,45 +693,63 @@
     @pl.when(at_bottom)
     def _():
         clear(1)
-        cb[0:32, :] = jnp.zeros((32, 32), F32)
+        cb[0:32, :] = jnp.zeros((32, 128), F32)
 
     @pl.when(at_top)
     def _():
         clear(2)
-        cb[64:96, :] = jnp.zeros((32, 32), F32)
+        cb[64:96, :] = jnp.zeros((32, 128), F32)
 
     @pl.when(gy >= last - 1)
     def _():
-        cb[96:128, :] = jnp.zeros((32, 32), F32)
+        cb[96:128, :] = jnp.zeros((32, 128), F32)
 
     def halo(field, stage):
-        at = offsets(HALO_ROWS)
+        at = offsets(FACE_ROWS)
         for index, (tx, ty) in enumerate(RING):
             xs, ys = (14, 0)[tx < 0], (14, 0)[ty < 0]
             if ty == 0:
-                stage[at[index] : at[index] + 32, :] = field[xs : xs + 2, :, :].reshape(32, 64)
+                layers = field[xs, :, :], field[xs + 1, :, :]
             elif tx == 0:
-                stage[at[index] : at[index] + 16, :] = field[:, ys, :]
-                stage[at[index] + 16 : at[index] + 32, :] = field[:, ys + 1, :]
+                layers = field[:, ys, :], field[:, ys + 1, :]
             else:
-                stage[at[index] : at[index] + 2, :] = field[xs, ys : ys + 2, :]
-                stage[at[index] + 2 : at[index] + 4, :] = field[xs + 1, ys : ys + 2, :]
-                stage[at[index] + 4 : at[index] + 8, :] = jnp.zeros((4, 64), F32)
-
-    at_halo, at_face = offsets(HALO_ROWS), offsets(FACE_ROWS)
+                layers = field[xs : xs + 2, ys, :], field[xs : xs + 2, ys + 1, :]
+            stage[at[index] : at[index + 1], :] = tall(jnp.concatenate(layers, 1), at[index + 1] - at[index])
+
+    def unfold(buffer):
+        packed_rows = tall(buffer[...], 128)
+        return jnp.concatenate([packed_rows, pltpu.roll(packed_rows, 64, 1)], 0)
+
+    def fold(block):
+        result = block[0:16]
+        for part in range(1, 4):
+            result = result + pltpu.roll(block[part * 16 : part * 16 + 16], part * 32, 1)
+        return result
+
+    def spread_blocks(folded, blocks_ref):
+        for part in range(4):
+            turned_back = pltpu.roll(folded[0:128, :], (128 - part * 32) % 128, 1) if part else folded[0:128, :]
+            for slot in range(8):
+                blocks_ref[slot * 64 + part * 16 : slot * 64 + part * 16 + 16, :] = turned_back[
+                    slot * 16 : slot * 16 + 16
+                ]
+
+    at_face = offsets(FACE_ROWS)
 
     inputs[0].wait()
     own_f = 8 * 16
     for ex in range(2):
         a, b, c = len_ref[0, ex], len_ref[1, ex], len_ref[2, ex]
-        fs[own_f + ex * 2 : own_f + ex * 2 + 2, :] = b * c / (2.0 * a)
-        fs[own_f + 4 + ex * 2 : own_f + 6 + ex * 2, :] = a * c / (2.0 * b)
-        fs[own_f + 8 + ex * 2 : own_f + 10 + ex * 2, :] = a * b / (2.0 * c)
-    fs[own_f + 12 : own_f + 16, :] = jnp.zeros((4, 8), F32)
+        fs[own_f + ex * 2 : own_f + ex * 2 + 2, :] = wide(b * c / (2.0 * a))
+        fs[own_f + 4 + ex * 2 : own_f + 6 + ex * 2, :] = wide(a * c / (2.0 * b))
+        fs[own_f + 8 + ex * 2 : own_f + 10 + ex * 2, :] = wide(a * b / (2.0 * c))
+    fs[own_f + 12 : own_f + 16, :] = jnp.zeros((4, 128), F32)
     inputs[1].wait()
     halo(r_ref, hs1)
-    exchange(1, lambda index: hs1.at[pl.ds(at_halo[index], HALO_ROWS[index])], hb1, HALO_ROWS)
-    exchange(0, lambda index: fs.at[pl.ds(own_f, 16)], fs, (16,) * 8)
+    near = jnp.minimum(gy + 1, last) - jnp.maximum(gy - 2, 0) + 1
+    pl.semaphore_wait(barrier, 2 * n_gy - 1 + 2 * near)
+    exchange(1, lambda index: hs1.at[pl.ds(at_face[index], FACE_ROWS[index])], hb1, FACE_ROWS)
+    exchange(0, lambda index: fs.at[pl.ds(own_f, 16)], fs, BLOCK_ROWS)
 
     bottom_on = jnp.where(at_bottom, 1.0, 0.0)
     top_on = jnp.where(at_top, 1.0, 0.0)
@@ -728,16 +777,16 @@
 
     def fine_back(modal, buffer, stage, phase):
         modal = right3(modal, t["az"]) * inverse7[...]
-        stage[...] = left3(t["bf"], modal)[:, : stage.shape[1]]
+        stage[...] = left3(t["bf"], modal)
         exchange(phase, lambda index: stage.at[pl.ds(at_face[index], FACE_ROWS[index])], buffer, FACE_ROWS)
         return left3(t["bo"], modal)
 
     ready(1)
-    settle(1, recv_sem, hb1, HALO_ROWS)
-    modal = modal[...] + left3(t["wh"], wide(hb1[...]))
+    settle(1, recv_sem, hb1, FACE_ROWS)
+    modal = modal[...] + left3(t["wh"], unfold(hb1))
     local = keep("local", fine_back(modal, fb1, st1, 2) * wt7[...])
     own_part = keep("own_part", jnp.concatenate(terms3(t["la"], right3(local[...], t["bzra"])), 0))
-    settle(0, recv_sem, fs, (16,) * 8)
+    settle(0, recv_sem, fs, BLOCK_ROWS)
     ring_f = wide(fs[...])
     d3 = left3(t["ld3"], right2(ring_f, t["s48"])) + left2(t["le3"], right3(ring_f, t["sl48"]))
     inverse3 = keep("inverse3", jnp.where(d3 > 0.0, 1.0 / jnp.where(d3 > 0.0, d3, 1.0), 0.0))
@@ -751,8 +800,9 @@
         + mid_f[64:128] * (own_part[64:128] + face_part[1])
         + mid_f[128:192] * (own_part[128:192] + face_part[2])
     )
-    rm[512:576, :] = residual_mid[:, 0:32]
-    exchange(3, lambda index: rm.at[pl.ds(512, 64)], rm, (64,) * 8)
+    rp[128:144, :] = fold(residual_mid)
+    exchange(3, lambda index: rp.at[pl.ds(128, 16)], rp, BLOCK_ROWS)
+    rm[512:576, :] = residual_mid
 
     ready(2)
     own_modal = keep("modal3", left3(t["wmo"], residual_mid))
@@ -766,22 +816,20 @@
         - (fine_f[0:256] * massed[0:256] + fine_f[256:512] * massed[256:512] + fine_f[512:768] * along_z),
     )
 
-    settle(3, recv_sem, rm, (64,) * 8)
-    modal3 = own_modal[...] + left3(t["wmn"], wide(rm[0:512, :]))
+    settle(3, recv_sem, rp, BLOCK_ROWS)
+    spread_blocks(rp, rm)
+    modal3 = own_modal[...] + left3(t["wmn"], rm[0:512, :])
     modal3 = right3(modal3, t["azm"]) * inverse3[...]
     variant = jnp.where(at_bottom, 1, jnp.where(at_top, 2, 0))
     rows = pl.multiple_of(variant * 48, 16)
-    high, rest = split(tall(modal3, t["lb"].shape[-1]))
-    lb_high, lb_rest = t["lb"].piece(0, rows, 48), t["lb"].piece(1, rows, 48)
-    low = dot(lb_high, high) + dot(lb_high, rest) + dot(lb_rest, high)
+    low = exactly(t["lb"].piece(0, rows, 48), t["lb"].piece(1, rows, 48), tall(modal3, t["lb"].shape[-1]))
     low = right3(low, t["rb"])
     low = base_low[...] - (
         low_f[0:16] * low[0:16, 0:256] + low_f[16:32] * low[16:32, 0:256] + low_f[32:48] * low[32:48, 256:512]
     )
     wall = pl.multiple_of(gy * 16, 16)
-    high, rest = split(tall((low[:, 0:128] + low[:, 128:256]) * t["mask"].piece(0, wall, 16), 128))
-    lefts = t["left"].piece(0, wall, 16)
-    message = (dot(lefts, high) + dot(lefts, rest))[0:8]
+    low = tall(halves(low) * t["mask"].piece(0, wall, 16), 128)
+    message = halves(dot(t["left"].piece(0, wall, 16), jnp.concatenate(split(low), 1)))[0:8]
     gs[...] = message
 
     def send_slab(step, ahead):
@@ -801,8 +849,9 @@
         send_slab(step, 1)
 
     first_mid = keep("first_mid", right3(left3(t["bm"], modal3) * wt3[...], t["bzm"]))
-    fm[512:576, :] = first_mid[:, 0:32]
-    exchange(4, lambda index: fm.at[pl.ds(512, 64)], fm, (64,) * 8)
+    fm[512:576, :] = first_mid[...]
+    fp[128:144, :] = fold(first_mid[...])
+    exchange(4, lambda index: fp.at[pl.ds(128, 16)], fp, BLOCK_ROWS)
 
     pltpu.make_async_copy(gb, gb, grecv).wait()
     here = gs[...] + jnp.sum(gb[0 : n_gy - 1], axis=0)
@@ -818,7 +867,7 @@
     solved = jnp.sum(solved, axis=0, keepdims=True)
     solved = jnp.broadcast_to(solved, (8, 128)) * t["chosen"][...]
     own_c = (4 + 3) * 8
-    cb[own_c : own_c + 8, :] = solved[:, 0:32]
+    cb[own_c : own_c + 8, :] = solved
 
     def send_correction(iy):
         def action():
@@ -848,13 +897,14 @@
     low_out = right2(tall(solved, 16), t["select"])
     out_low[0] = low_out[0:2, 0:8]
     out_low[1] = low_out[2:4, 0:8]
-    settle(4, recv_sem, fm, (64,) * 8)
-    turned = right3(wide(fm[...]), t["rk3"])
+    settle(4, recv_sem, fp, BLOCK_ROWS)
+    spread_blocks(fp, fm)
+    turned = right3(fm[...], t["rk3"])
     parts = []
     for at in range(9):
         piece = terms3(t["k3"], turned[at * 64 : (at + 1) * 64])
         parts.append(
-            wide(rm[at * 64 : (at + 1) * 64, :])
+            rm[at * 64 : (at + 1) * 64, :]
             - (
                 ring_f[at * 64 : (at + 1) * 64] * piece[0]
                 + ring_f[576 + at * 64 : 576 + (at + 1) * 64] * piece[1]
@@ -886,12 +936,12 @@
     )
     rs[...] = residual[:, 0:64].reshape(16, 16, 64)
     halo(rs, hs2)
-    exchange(5, lambda index: hs2.at[pl.ds(at_halo[index], HALO_ROWS[index])], hb2, HALO_ROWS)
+    exchange(5, lambda index: hs2.at[pl.ds(at_face[index], FACE_ROWS[index])], hb2, FACE_ROWS)
     out_mid[...] = mid_result[:, 0:32].reshape(8, 8, 32)
     modal = keep("modal", left3(t["wo"], residual))
     held[...] = first_fine[...] + right3(left3(t["pxy"], mid_result), t["pz"])
-    settle(5, recv_sem, hb2, HALO_ROWS)
-    modal = modal[...] + left3(t["wh"], wide(hb2[...]))
+    settle(5, recv_sem, hb2, FACE_ROWS)
+    modal = modal[...] + left3(t["wh"], unfold(hb2))
     local = fine_back(modal, fb2, st2, 6) * wt7[...]
     held[...] = held[...] + right3(local, t["bz"])
     settle(6, recv_sem, fb2, FACE_ROWS)
@@ -899,39 +949,48 @@
     out_fine[...] = result[:, 0:64].reshape(16, 16, 64)
 
     for phase, buffer, rows in (
-        (0, fs, (16,) * 8), (1, hb1, HALO_ROWS), (2, fb1, FACE_ROWS), (3, rm, (64,) * 8),
-        (4, fm, (64,) * 8), (5, hb2, HALO_ROWS), (6, fb2, FACE_ROWS),
+        (0, fs, BLOCK_ROWS), (1, hb1, FACE_ROWS), (2, fb1, FACE_ROWS), (3, rp, BLOCK_ROWS),
+        (4, fp, BLOCK_ROWS), (5, hb2, FACE_ROWS), (6, fb2, FACE_ROWS),
     ):
         settle(phase, send_sem, buffer, rows)
     pltpu.make_async_copy(gb, gb, gsend).wait()
     settle_corrections(csend, to_group)
 
 
+def hand_over(*refs):
+    copies = [pltpu.make_async_copy(refs[at], refs[3 + at], refs[6].at[at]) for at in range(3)]
+    for copy in copies:
+        copy.start()
+    for copy in copies:
+        copy.wait()
+
+
 def shards(n_gx, n_gy, local_residual, lengths, coarse_inverse):
     keys, packed, places = pack(build_tables(n_gy, lengths.shape[3]))
     vmem = pl.BlockSpec(memory_space=pltpu.VMEM)
-    modes = lengths.shape[3] * (ORDER + 3)
     scratch = [pltpu.VMEM(table.shape, BF if key[1] == "bfloat16" else F32) for key, table in zip(keys, packed)]
     scratch += [
         pltpu.VMEM(local_residual.shape, F32),
         pltpu.VMEM(lengths.shape, F32),
         pltpu.VMEM(coarse_inverse.shape, BF),
         pltpu.VMEM((16, 16, 64), F32),
-        pltpu.VMEM((144, 8), F32),
-        pltpu.VMEM((160, 64), F32),
-        pltpu.VMEM((96, modes), F32),
-        pltpu.VMEM((576, 32), F32),
-        pltpu.VMEM((576, 32), F32),
-        pltpu.VMEM((160, 64), F32),
-        pltpu.VMEM((96, modes), F32),
-        pltpu.VMEM((160, 64), F32),
-        pltpu.VMEM((160, 64), F32),
-        pltpu.VMEM((96, modes), F32),
-        pltpu.VMEM((96, modes), F32),
+        pltpu.VMEM((144, 128), F32),
+        pltpu.VMEM((96, 128), F32),
+        pltpu.VMEM((96, 128), F32),
+        pltpu.VMEM((576, 128), F32),
+        pltpu.VMEM((576, 128), F32),
+        pltpu.VMEM((144, 128), F32),
+        pltpu.VMEM((144, 128), F32),
+        pltpu.VMEM((96, 128), F32),
+        pltpu.VMEM((96, 128), F32),
+        pltpu.VMEM((96, 128), F32),
+        pltpu.VMEM((96, 128), F32),
+        pltpu.VMEM((96, 128), F32),
+        pltpu.VMEM((96, 128), F32),
         pltpu.VMEM((256, 128), F32),
         pltpu.VMEM((8, 128), F32),
         pltpu.VMEM((2 * n_gy - 1, 8, 128), F32),
-        pltpu.VMEM((128, 32), F32),
+        pltpu.VMEM((128, 128), F32),
         pltpu.SemaphoreType.DMA((7, 3)),
         pltpu.SemaphoreType.DMA((7, 3)),
         pltpu.SemaphoreType.DMA,
@@ -942,7 +1001,7 @@
         pltpu.SemaphoreType.DMA((len(keys),)),
     ]
     scratch += [pltpu.VMEM(shape, F32) for shape in KEPT.values()]
-    return pl.pallas_call(
+    outs = pl.pallas_call(
         functools.partial(cycle_kernel, keys, places, n_gx, n_gy),
         out_shape=(
             jax.ShapeDtypeStruct((16, 16, 64), F32),
@@ -952,8 +1011,15 @@
         in_specs=[pl.BlockSpec(memory_space=pl.ANY)] * (3 + len(keys)),
         out_specs=(vmem, vmem, vmem),
         scratch_shapes=scratch,
-        compiler_params=pltpu.CompilerParams(has_side_effects=True, vmem_limit_bytes=60 * 1024 * 1024),
+        compiler_params=pltpu.CompilerParams(collective_id=0, has_side_effects=True, vmem_limit_bytes=60 * 1024 * 1024),
     )(local_residual, lengths, coarse_inverse, *[jnp.asarray(table) for table in packed])
+    return pl.pallas_call(
+        hand_over,
+        out_shape=tuple(jax.ShapeDtypeStruct(out.shape, out.dtype) for out in outs),
+        in_specs=[vmem] * 3,
+        out_specs=[pl.BlockSpec(memory_space=pl.ANY)] * 3,
+        scratch_shapes=[pltpu.SemaphoreType.DMA((3,))],
+    )(*outs)
 
 
 def solution(mesh):

time: 84.4 us -> 61.8 us (0.73)
  the two profiles are of different devices: /device:TPU:7 before, /device:TPU:1 now
where the time goes in v2:
time: 61.8 us; the launch traced here: 61.7 us
  Pallas kernels  61 us (99%)
  between operations  0.64 us (1%)
    pallas_call x1, Pallas kernels, shards(): pl.pallas_call(functools.partial(cycle_kernel, keys, places, n_gx, n_gy),...  59.4 us
    pallas_call x1, Pallas kernels, shards(): pl.pallas_call(hand_over, out_shape=tuple((jax.ShapeDtypeStruct(out.shape...  1.61 us

profile of v2, /device:TPU:1, one launch (start us, length us, event | category | flops | bytes accessed | tf_op | source)
XLA Modules:
  0.0 61.7 jit_solution(8418998414830467124)
XLA Ops:
  0.6 59.4 %shard_map.157 = (f32[16,16,64]{2,1,0:T(8,128)}, f32[8,8,32]{2,1,0:T(8,128)}, f32[2,2,8]{2,1,0:T(2,128)}) custom-call(f32[16,16,64]{2,1,0:T(8,128)} %refs_0_.1, f32[3,2,2,8]{3,2,1,0:T(2,128)} %refs_1_.1, bf16[1,32,512]{2,1,0:T(8,128)(2,1)} %refs_2_.1, f32[544,128]{1,0:T(8,128)} %constant.22.clone.refs_3_, bf16[1696,256]{1,0:T(8,128)(2,1)} %constant.23.clone.refs_4_, ...), custom_call_target="tpu_custom_call" | custom-call | tf_op jit(solution)/shard_map/pallas_call | solution.py:1004
  60.1 1.6 %shard_map.158 = (f32[16,16,64]{2,1,0:T(8,128)}, f32[8,8,32]{2,1,0:T(8,128)}, f32[2,2,8]{2,1,0:T(2,128)}) custom-call(f32[16,16,64]{2,1,0:T(8,128)} %get-tuple-element.6.refs_0_, f32[8,8,32]{2,1,0:T(8,128)} %get-tuple-element.7.refs_1_, f32[2,2,8]{2,1,0:T(2,128)} %get-tuple-element.8.refs_2_), custom_call_target="tpu_custom_call" | custom-call | tf_op jit(solution)/shard_map/pallas_call | solution.py:1016

commit v3 on v2

--- a/solution.py
+++ b/solution.py
@@ -157,6 +157,9 @@
 AHEAD = (-1, 1, 2, 0)
 FACE_ROWS = (16, 16, 16, 8, 8, 16, 8, 8)
 BLOCK_ROWS = (16,) * 8
+WIDE_ROWS = (80, 80, 80, 64, 64, 80, 64, 64)
+LOW_SIDE = ((-1, 0), (-1, -1), (-1, 1), (0, -1), (0, 1))
+HIGH_SIDE = ((1, 0), (1, -1), (1, 1), (0, -1), (0, 1))
 MESH = pl.DeviceIdType.MESH
 
 
@@ -210,7 +213,7 @@
 
 
 RIGHT = (
-    "az", "bz", "bzra", "jz", "kz7", "rp", "pz", "azm", "bzm", "rb", "rj", "rk3", "rc", "rcj",
+    "az", "bz", "bzra", "jz", "kz7", "rp", "pz", "azm", "bzm", "rb", "rj", "rk3", "ra3", "cz", "s16", "rcj",
     "s64", "s32", "s256", "s80", "sl80", "s48", "sl48", "select",
 )
 
@@ -289,6 +292,43 @@
     bz = z_back(inner, p, ez)
     pair["bz"] = bz
 
+    count = 4 * modes
+    ext = np.zeros((4, modes, 36))
+    for element in range(4):
+        start = 2 + p * element
+        ext[element, 0, start - 2] += 1
+        for at in range(p):
+            ext[element, 1 + at, start + at] += 1
+        ext[element, 1, start - 1] += 1
+        ext[element, p, start + p] += 1
+        ext[element, p + 1, start + p + 1] += 1
+    a1w = blocks(s7.T, 4) @ ext.reshape(count, 36)
+    middle = a1w[:, 10:26]
+    beside = {-1: a1w[:, 0:10], 1: a1w[:, 26:36]}
+    for name, group, rows in (("vl", LOW_SIDE, slice(0, 2 * modes)), ("vr", HIGH_SIDE, slice(2 * modes, None))):
+        parts = []
+        for half in range(2):
+            for dx, dy in group:
+                pieces = []
+                for at in range(half, 10, 2):
+                    if dy == 0:
+                        pieces.append(np.kron(beside[dx][rows, at : at + 1], middle))
+                    elif dx == 0:
+                        pieces.append(np.kron(middle[rows], beside[dy][:, at : at + 1]))
+                    else:
+                        pieces.append(np.kron(beside[dx][rows], beside[dy][:, at : at + 1]))
+                piece = np.concatenate(pieces, 1)
+                parts.append(np.pad(piece, ((0, 0), (0, -piece.shape[1] % 16))))
+        plain[name] = (np.concatenate(parts, 1), BF)
+    plain["vo"] = (np.kron(middle, middle), BF)
+    raw = blocks(inner, 4)
+    around = np.array(raw[p : 3 * p])
+    for at in (p - 1, 2 * p - 1, 3 * p - 1):
+        for row in (at, at + 1):
+            if p <= row < 3 * p:
+                around[row - p] = raw[at] + raw[at + 1]
+    plain["vb"] = (np.kron(around, around), BF)
+
     def weights(points):
         line = line_weights(points, 2)
         low_side, high_side = np.zeros(2 * points), np.zeros(2 * points)
@@ -400,6 +440,15 @@
             ld3[x * 24 + y, ring_row(ex, ey, 0)] = l3[x % m3]
             ld3[x * 24 + y, ring_row(ex, ey, 1)] = l3[y % m3]
             le3[x * 24 + y, ring_row(ex, ey, 2)] = 1
+    ld9, le9 = np.zeros((count * count, 144)), np.zeros((count * count, 144))
+    for x in range(count):
+        for y in range(count):
+            ex, ey = x // modes + 1, y // modes + 1
+            ld9[x * count + y, ring_row(ex, ey, 0)] = l7[x % modes]
+            ld9[x * count + y, ring_row(ex, ey, 1)] = l7[y % modes]
+            le9[x * count + y, ring_row(ex, ey, 2)] = 1
+    pair["ld9"] = ld9
+    plain["le9"] = (le9, BF)
     pair["ld3"] = ld3
     plain["le3"] = (le3, BF)
     plain["s48"] = (spread(m3), BF)
@@ -413,10 +462,35 @@
     plain["er"] = (er.reshape(3 * 576, 144), BF)
     pair["k3"] = np.concatenate(three(k3, w3, 2), 0)
     pair["rk3"] = side_by_side(blocks(w3, ez), blocks(k3, ez))
+    corner_line = lambda table: np.kron(np.eye(6), table)
+    modes_of = [a1m @ corner_line(table) for table in (k3 @ jm, w3 @ jm)]
+    pair["wl"] = np.concatenate(
+        [np.kron(modes_of[left], modes_of[right]) for left, right in ((0, 1), (1, 0), (1, 1))], 1
+    )
+    pair["ra3"] = side_by_side(
+        blocks((w3 @ jm).T, ez) @ pair["azm"], blocks((k3 @ jm).T, ez) @ pair["azm"]
+    )
+    spread_vertices, spread_factors = np.zeros((144, 128)), np.zeros((3, 144, 144))
+    for row in range(144):
+        (ex, cx), (ey, cy) = divmod(row // 12, 2), divmod(row % 12, 2)
+        vx, vy = ex + cx, ey + cy
+        column = ((vy // 2) * 4 + AHEAD.index(vx // 2 - 1)) * 8 + (vx % 2) * 2 + vy % 2
+        spread_vertices[row, column] = 1
+        for d in range(3):
+            at = order.index((ex // 2 - 1, ey // 2 - 1))
+            spread_factors[d, row, at * 16 + d * 4 + (ex % 2) * 2 + ey % 2] = 1
+    plain["ev"] = (spread_vertices, BF)
+    plain["ef"] = (spread_factors.reshape(432, 144), BF)
+    corner_z = np.zeros((ez, 2 * ez))
+    for element in range(ez):
+        for at in range(2):
+            corner_z[(element + at) % ez, 2 * element + at] = 1
+    plain["cz"] = (np.tile(corner_z, (4, 1)), BF)
+    plain["s16"] = (spread(2), BF)
     vertex_line = lambda table: np.array(
         [[table[at % q, v - at // q] if 0 <= v - at // q <= 1 else 0.0 for v in range(8)] for at in range(6 * q)]
     )
-    stiff1, mass1, plain1 = vertex_line(k3 @ jm), vertex_line(w3 @ jm), vertex_line(jm)
+    plain1 = vertex_line(jm)
 
     def vertex_columns(left, right, dx, dy):
         table = np.zeros((64, 4, 4, 8))
@@ -429,14 +503,6 @@
                         )
         return table.reshape(64, 128)
 
-    pair["lc"] = np.concatenate(
-        [
-            vertex_columns(left, right, dx, dy)
-            for left, right in ((stiff1, mass1), (mass1, stiff1), (mass1, mass1))
-            for dx, dy in order
-        ],
-        0,
-    )
     pair["jc"] = vertex_columns(plain1, plain1, 0, 0)
 
     def z_vertices(table):
@@ -447,7 +513,6 @@
                 result[(element + 1) % ez, element * q + at] += table[at, 1]
         return np.tile(result, (4, 1))
 
-    pair["rc"] = side_by_side(z_vertices(w3 @ jm), z_vertices(k3 @ jm))
     pair["rcj"] = z_vertices(jm)
     mask, left = np.zeros((n_gy, 16, 128)), np.zeros((n_gy, 16, 16))
     for gy in range(n_gy):
@@ -491,8 +556,9 @@
     ("wh", "az", "bf", "bo", "la", "bzra", "ld3", "le3", "s48", "sl48", "er", "lar"),
     (
         "wmo", "jl", "rj", "scat", "bz", "k7", "kz7", "wmn", "azm", "lb", "rb", "left", "bm", "bzm", "select",
-        "rk3", "k3", "lc", "rc", "jc", "rcj", "rp", "lp", "pxy", "pz",
+        "rk3", "k3", "wl", "ra3", "ev", "ef", "cz", "s16", "jc", "rcj", "rp", "lp", "pxy", "pz",
     ),
+    ("ld9", "le9", "vo", "vl", "vr", "vb"),
 )
 
 
@@ -586,7 +652,7 @@
     "inverse3": (576, 128), "wt7": (256, 128), "wr7": (96, 128), "wt3": (64, 128), "base_mid": (64, 128),
     "base_low": (16, 256), "local": (256, 128), "first_fine": (256, 128), "base_fine": (256, 128),
     "first_mid": (64, 128), "modal": (400, 128), "modal3": (576, 128), "own_part": (192, 128), "base_ring": (576, 128),
-    "ww7": (256, 128),
+    "ww7": (256, 128), "inverse9": (1600, 128), "corner_f": (432, 128), "modal9": (1600, 128),
 }
 
 
@@ -597,7 +663,7 @@
     out_fine, out_mid, out_low = refs[3 + count : 6 + count]
     stores = refs[6 + count : 6 + 2 * count]
     (
-        r_ref, len_ref, inv_ref, rs, fs, hb1, fb1, rm, fm, rp, fp, hb2, fb2, hs1, hs2, st1, st2, held, gs, gb, cb,
+        r_ref, len_ref, inv_ref, rs, fs, hb1, fb1, rm, fm, rp, fp, hb2, hs1, hs2, st1, corner, held, gs, gb, cb,
         send_sem, recv_sem, gsend, grecv, csend, crecv, in_sem, table_sem,
     ) = refs[6 + 2 * count : -len(KEPT)]
     gx, gy = lax.axis_index("gx"), lax.axis_index("gy")
@@ -609,25 +675,39 @@
             barrier, inc=1, device_id=(lax.rem(gx + (ahead + n_gx), n_gx), row), device_id_type=MESH
         )
 
-    def greet_if(row):
+    def greet_if(row, *columns):
         @pl.when((row >= 0) & (row <= last))
         def _():
-            greet(1, row)
-            greet(2, row)
-
-    for step in range(-1, 3):
-        greet_if(gy + step)
-    for step in range(1, n_gy):
-        greet(0, lax.rem(gy + step, n_gy))
-    for step in range(n_gy):
-        greet(-1, lax.rem(gy + step, n_gy))
+            for ahead in columns:
+                greet(ahead, row)
+
+    greet_if(gy + 1, 0, 1, -1)
+    greet_if(gy - 1, 0, 1, -1)
+    greet(1, gy)
+    greet(-1, gy)
+    greet(2, gy)
+    greet_if(gy + 1, 2)
+    greet_if(gy - 1, 2)
+    greet_if(gy + 2, 1, 2)
+    for row in range(n_gy):
+        @pl.when((row < gy - 1) | (row > gy + 1))
+        def _():
+            greet(0, row)
+            greet(-1, row)
     inputs = [
         pltpu.make_async_copy(source, target, in_sem.at[at])
         for at, (source, target) in enumerate(((len_hbm, len_ref), (r_hbm, r_ref), (inv_hbm, inv_ref)))
     ]
     loads = [pltpu.make_async_copy(packed[at], stores[at], table_sem.at[at]) for at in range(count)]
-    for load in inputs + loads:
+    for load in inputs:
         load.start()
+
+    def fetch(*stages):
+        for key, load in zip(keys, loads):
+            if key[0] in stages:
+                load.start()
+
+    fetch(0)
 
     def ready(stage):
         for key, load in zip(keys, loads):
@@ -685,10 +765,10 @@
         first, end = GROUPS[number]
         for buffer, rows in (
             (fs, BLOCK_ROWS), (hb1, FACE_ROWS), (fb1, FACE_ROWS), (rp, BLOCK_ROWS),
-            (fp, BLOCK_ROWS), (hb2, FACE_ROWS), (fb2, FACE_ROWS),
+            (fp, BLOCK_ROWS), (hb2, WIDE_ROWS),
         ):
             at = offsets(rows)
-            buffer[at[first] : at[end], :] = jnp.zeros((at[end] - at[first], buffer.shape[1]), F32)
+            buffer[at[first] : at[end], :] = jnp.zeros((at[end] - at[first], buffer.shape[1]), buffer.dtype)
 
     @pl.when(at_bottom)
     def _():
@@ -715,6 +795,36 @@
             else:
                 layers = field[xs : xs + 2, ys, :], field[xs : xs + 2, ys + 1, :]
             stage[at[index] : at[index + 1], :] = tall(jnp.concatenate(layers, 1), at[index + 1] - at[index])
+
+    at_wide = offsets(WIDE_ROWS)
+
+    def wide_halo(field, stage):
+        for index, (tx, ty) in enumerate(RING):
+            xs, ys = (6, 0)[tx < 0], (6, 0)[ty < 0]
+            if 0 not in (tx, ty):
+                corner[48:64, :] = jnp.zeros((16, 128), F32)
+            for pair in range(5):
+                xa, ya = xs + 2 * pair, ys + 2 * pair
+                at = at_wide[index] + pair * 16
+                if ty == 0:
+                    layers = field[xa, :, :], field[xa + 1, :, :]
+                    stage[at : at + 16, :] = jnp.concatenate(layers, 1).astype(stage.dtype)
+                elif tx == 0:
+                    layers = field[:, ya, :], field[:, ya + 1, :]
+                    stage[at : at + 16, :] = jnp.concatenate(layers, 1).astype(stage.dtype)
+                else:
+                    layers = field[xs : xs + 10, ya, :], field[xs : xs + 10, ya + 1, :]
+                    corner[pair * 10 : pair * 10 + 10, :] = jnp.concatenate(layers, 1)
+            if 0 not in (tx, ty):
+                stage[at_wide[index] : at_wide[index + 1], :] = corner[...].astype(stage.dtype)
+
+    def side_values(buffer, group):
+        pieces = []
+        for direction in group:
+            index = RING.index(direction)
+            pieces.append(buffer[at_wide[index] : at_wide[index + 1], :])
+        turned_back = [pltpu.roll(piece.astype(F32), 64, 1).astype(BF) for piece in pieces]
+        return tall(jnp.concatenate(pieces + turned_back, 0), 768)
 
     def unfold(buffer):
         packed_rows = tall(buffer[...], 128)
@@ -750,6 +860,7 @@
     pl.semaphore_wait(barrier, 2 * n_gy - 1 + 2 * near)
     exchange(1, lambda index: hs1.at[pl.ds(at_face[index], FACE_ROWS[index])], hb1, FACE_ROWS)
     exchange(0, lambda index: fs.at[pl.ds(own_f, 16)], fs, BLOCK_ROWS)
+    fetch(1, 2)
 
     bottom_on = jnp.where(at_bottom, 1.0, 0.0)
     top_on = jnp.where(at_top, 1.0, 0.0)
@@ -784,6 +895,7 @@
     ready(1)
     settle(1, recv_sem, hb1, FACE_ROWS)
     modal = modal[...] + left3(t["wh"], unfold(hb1))
+    fetch(3)
     local = keep("local", fine_back(modal, fb1, st1, 2) * wt7[...])
     own_part = keep("own_part", jnp.concatenate(terms3(t["la"], right3(local[...], t["bzra"])), 0))
     settle(0, recv_sem, fs, BLOCK_ROWS)
@@ -894,6 +1006,11 @@
             piece = cb.at[pl.ds(iy * 32, 24 if iy == 1 else 32)]
             guarded(conditions[iy], lambda: pltpu.make_async_copy(piece, piece, sems.at[iy]).wait())
 
+    ready(3)
+    ring_l = wide(fs[...])
+    d9 = left3(t["ld9"], right2(ring_l, t["s80"])) + left2(t["le9"], right3(ring_l, t["sl80"]))
+    inverse9 = keep("inverse9", jnp.where(d9 > 0.0, 1.0 / jnp.where(d9 > 0.0, d9, 1.0), 0.0))
+    corner_f = keep("corner_f", left2(t["ef"], right2(ring_l, t["s16"])))
     low_out = right2(tall(solved, 16), t["select"])
     out_low[0] = low_out[0:2, 0:8]
     out_low[1] = low_out[2:4, 0:8]
@@ -912,18 +1029,15 @@
             )
         )
     base_ring = keep("base_ring", jnp.concatenate(parts, 0))
-    modal3 = keep("modal3", left3(t["wmn"], base_ring[0:512]) + left3(t["wmo"], base_ring[512:576]))
+    modal3 = left3(t["wmn"], base_ring[0:512]) + left3(t["wmo"], base_ring[512:576])
+    modal3 = keep("modal3", right3(modal3, t["azm"]))
 
     settle_corrections(crecv, from_group)
     corrections = wide(cb[...])
-    change = terms3(t["lc"], right3(corrections, t["rc"]))
-    change = (
-        ring_f[0:576] * change[0]
-        + ring_f[576:1152] * change[1]
-        + ring_f[1152:1728] * change[2]
-    )
-    modal3 = modal3[...] - left3(t["wmn"], change[0:512]) - left3(t["wmo"], change[512:576])
-    modal3 = right3(modal3, t["azm"]) * inverse3[...]
+    change = left2(t["ev"], right2(corrections, t["cz"]))
+    change = right3(jnp.concatenate([change * corner_f[at * 144 : at * 144 + 144] for at in range(3)], 0), t["ra3"])
+    change = jnp.concatenate([change[0:288, 0:128], change[288:432, 128:256]], 0)
+    modal3 = (modal3[...] - left3(t["wl"], change)) * inverse3[...]
     held[0:64, :] = first_mid[...] + right3(left3(t["jc"], corrections), t["rcj"])
     mid_result = held[0:64, :] + right3(left3(t["bm"], modal3) * wt3[...], t["bzm"])
 
@@ -935,22 +1049,27 @@
         + fine_f[512:768] * turned[2]
     )
     rs[...] = residual[:, 0:64].reshape(16, 16, 64)
-    halo(rs, hs2)
-    exchange(5, lambda index: hs2.at[pl.ds(at_face[index], FACE_ROWS[index])], hb2, FACE_ROWS)
+    wide_halo(rs, hs2)
+    exchange(5, lambda index: hs2.at[pl.ds(at_wide[index], WIDE_ROWS[index])], hb2, WIDE_ROWS)
     out_mid[...] = mid_result[:, 0:32].reshape(8, 8, 32)
-    modal = keep("modal", left3(t["wo"], residual))
+    modal9 = keep("modal9", dot(t["vo"][...], residual.astype(BF)))
     held[...] = first_fine[...] + right3(left3(t["pxy"], mid_result), t["pz"])
-    settle(5, recv_sem, hb2, FACE_ROWS)
-    modal = modal[...] + left3(t["wh"], unfold(hb2))
-    local = fine_back(modal, fb2, st2, 6) * wt7[...]
-    held[...] = held[...] + right3(local, t["bz"])
-    settle(6, recv_sem, fb2, FACE_ROWS)
-    result = held[...] + left2(t["scat"], right3(wide(fb2[...]) * wr7[...], t["bz"]))
+    settle(5, recv_sem, hb2, WIDE_ROWS)
+    modal = jnp.concatenate(
+        [
+            modal9[0:800] + dot(t["vl"][...], side_values(hb2, LOW_SIDE)),
+            modal9[800:1600] + dot(t["vr"][...], side_values(hb2, HIGH_SIDE)),
+        ],
+        0,
+    )
+    modal = right3(modal, t["az"]) * inverse9[...]
+    local = dot(t["vb"][...], tall(modal, 1664).astype(BF)) * wt7[...]
+    result = held[...] + right3(local, t["bz"])
     out_fine[...] = result[:, 0:64].reshape(16, 16, 64)
 
     for phase, buffer, rows in (
         (0, fs, BLOCK_ROWS), (1, hb1, FACE_ROWS), (2, fb1, FACE_ROWS), (3, rp, BLOCK_ROWS),
-        (4, fp, BLOCK_ROWS), (5, hb2, FACE_ROWS), (6, fb2, FACE_ROWS),
+        (4, fp, BLOCK_ROWS), (5, hb2, WIDE_ROWS),
     ):
         settle(phase, send_sem, buffer, rows)
     pltpu.make_async_copy(gb, gb, gsend).wait()
@@ -981,18 +1100,17 @@
         pltpu.VMEM((576, 128), F32),
         pltpu.VMEM((144, 128), F32),
         pltpu.VMEM((144, 128), F32),
+        pltpu.VMEM((576, 128), BF),
         pltpu.VMEM((96, 128), F32),
+        pltpu.VMEM((576, 128), BF),
         pltpu.VMEM((96, 128), F32),
-        pltpu.VMEM((96, 128), F32),
-        pltpu.VMEM((96, 128), F32),
-        pltpu.VMEM((96, 128), F32),
-        pltpu.VMEM((96, 128), F32),
+        pltpu.VMEM((64, 128), F32),
         pltpu.VMEM((256, 128), F32),
         pltpu.VMEM((8, 128), F32),
         pltpu.VMEM((2 * n_gy - 1, 8, 128), F32),
         pltpu.VMEM((128, 128), F32),
-        pltpu.SemaphoreType.DMA((7, 3)),
-        pltpu.SemaphoreType.DMA((7, 3)),
+        pltpu.SemaphoreType.DMA((6, 3)),
+        pltpu.SemaphoreType.DMA((6, 3)),
         pltpu.SemaphoreType.DMA,
         pltpu.SemaphoreType.DMA,
         pltpu.SemaphoreType.DMA((4,)),

time: 61.8 us -> 58.3 us (0.943)
  Pallas kernels: 61 us -> 57.5 us
    pallas_call x1, Pallas kernels: 59.4 us -> 55.9 us  [shards(): pl.pallas_call(functools.partial(cycle_kernel, keys, places, n_gx, n_gy),...]
where the time goes in v3:
time: 58.3 us; the launch traced here: 58.2 us
  Pallas kernels  57.5 us (99%)
  between operations  0.64 us (1%)
    pallas_call x1, Pallas kernels, shards(): pl.pallas_call(functools.partial(cycle_kernel, keys, places, n_gx, n_gy),...  55.9 us
    pallas_call x1, Pallas kernels, shards(): pl.pallas_call(hand_over, out_shape=tuple((jax.ShapeDtypeStruct(out.shape...  1.61 us

profile of v3, /device:TPU:1, one launch (start us, length us, event | category | flops | bytes accessed | tf_op | source)
XLA Modules:
  0.0 58.2 jit_solution(9908821879360647313)
XLA Ops:
  0.6 55.9 %shard_map.184 = (f32[16,16,64]{2,1,0:T(8,128)}, f32[8,8,32]{2,1,0:T(8,128)}, f32[2,2,8]{2,1,0:T(2,128)}) custom-call(f32[16,16,64]{2,1,0:T(8,128)} %refs_0_.1, f32[3,2,2,8]{3,2,1,0:T(2,128)} %refs_1_.1, bf16[1,32,512]{2,1,0:T(8,128)(2,1)} %refs_2_.1, f32[544,128]{1,0:T(8,128)} %constant.28.clone.refs_3_, bf16[1696,256]{1,0:T(8,128)(2,1)} %constant.29.clone.refs_4_, ...), custom_call_target="tpu_custom_call" | custom-call | tf_op jit(solution)/shard_map/pallas_call | solution.py:1122
  56.6 1.6 %shard_map.185 = (f32[16,16,64]{2,1,0:T(8,128)}, f32[8,8,32]{2,1,0:T(8,128)}, f32[2,2,8]{2,1,0:T(2,128)}) custom-call(f32[16,16,64]{2,1,0:T(8,128)} %get-tuple-element.6.refs_0_, f32[8,8,32]{2,1,0:T(8,128)} %get-tuple-element.7.refs_1_, f32[2,2,8]{2,1,0:T(2,128)} %get-tuple-element.8.refs_2_), custom_call_target="tpu_custom_call" | custom-call | tf_op jit(solution)/shard_map/pallas_call | solution.py:1134

commit v4 on v3

--- a/solution.py
+++ b/solution.py
@@ -155,7 +155,6 @@
 RING = ((-1, 0), (1, 0), (0, -1), (-1, -1), (1, -1), (0, 1), (-1, 1), (1, 1))
 GROUPS = ((0, 2), (2, 5), (5, 8))
 AHEAD = (-1, 1, 2, 0)
-FACE_ROWS = (16, 16, 16, 8, 8, 16, 8, 8)
 BLOCK_ROWS = (16,) * 8
 WIDE_ROWS = (80, 80, 80, 64, 64, 80, 64, 64)
 LOW_SIDE = ((-1, 0), (-1, -1), (-1, 1), (0, -1), (0, 1))
@@ -213,7 +212,7 @@
 
 
 RIGHT = (
-    "az", "bz", "bzra", "jz", "kz7", "rp", "pz", "azm", "bzm", "rb", "rj", "rk3", "ra3", "cz", "s16", "rcj",
+    "az", "bz", "bzra", "jz", "kz7", "rp", "pz", "azm", "bzm", "rb", "rj", "rk3", "ra3", "bzrp", "cz", "s16", "rcj",
     "s64", "s32", "s256", "s80", "sl80", "s48", "sl48", "select",
 )
 
@@ -247,48 +246,8 @@
     k3, w3, s3, l3 = mid[2], np.diag(mid[1]), mid[3], mid[4]
     pair, plain = {}, {}
     modes = p + 2
-    a1 = blocks(s7.T, 2) @ line_extension(p, 2, False)
-    own, sides = a1[:, : 2 * p], {-1: a1[:, 2 * p : 2 * p + 2], 1: a1[:, 2 * p + 2 :]}
-    pair["wo"] = np.kron(own, own)
-    halves = []
-    for half in range(2):
-        layer = slice(half, half + 1)
-        parts = []
-        for dx, dy in RING:
-            if dy == 0:
-                parts.append(np.kron(sides[dx][:, layer], own))
-            elif dx == 0:
-                parts.append(np.kron(own, sides[dy][:, layer]))
-            else:
-                parts.append(np.pad(np.kron(sides[dx], sides[dy][:, layer]), ((0, 0), (0, 6))))
-        halves.append(np.concatenate(parts, 1))
-    pair["wh"] = side_by_side(*halves)
     pair["az"] = (blocks(s7.T, ez) @ line_extension(p, ez, True)).T
     inner = s7[1:-1]
-    raw = blocks(inner, 2)
-    back = np.array(raw)
-    back[p - 1] = back[p] = raw[p - 1] + raw[p]
-    face = {-1: raw[:1], 1: raw[-1:]}
-    pair["bo"] = np.kron(back, back)
-    parts, rows = [], []
-    edge = {-1: 0, 1: 2 * p - 1}
-    for tx, ty in RING:
-        scatter = np.zeros((16, 256)) if 0 in (tx, ty) else np.zeros((8, 256))
-        if ty == 0:
-            parts.append(np.kron(face[tx], back))
-            for at in range(16):
-                scatter[at, edge[tx] * 16 + at] = 1
-        elif tx == 0:
-            parts.append(np.kron(back, face[ty]))
-            for at in range(16):
-                scatter[at, at * 16 + edge[ty]] = 1
-        else:
-            parts.append(np.pad(np.kron(face[tx], face[ty]), ((0, 7), (0, 0))))
-            scatter[0, edge[tx] * 16 + edge[ty]] = 1
-        rows.append(scatter)
-    pair["bf"] = np.concatenate(parts, 0)
-    scat = np.concatenate(rows, 0).T
-    plain["scat"] = (scat, BF)
     bz = z_back(inner, p, ez)
     pair["bz"] = bz
 
@@ -320,14 +279,14 @@
                 piece = np.concatenate(pieces, 1)
                 parts.append(np.pad(piece, ((0, 0), (0, -piece.shape[1] % 16))))
         plain[name] = (np.concatenate(parts, 1), BF)
-    plain["vo"] = (np.kron(middle, middle), BF)
+    pair["vo"] = np.kron(middle, middle)
     raw = blocks(inner, 4)
     around = np.array(raw[p : 3 * p])
     for at in (p - 1, 2 * p - 1, 3 * p - 1):
         for row in (at, at + 1):
             if p <= row < 3 * p:
                 around[row - p] = raw[at] + raw[at + 1]
-    plain["vb"] = (np.kron(around, around), BF)
+    pair["vb"] = np.kron(around, around)
 
     def weights(points):
         line = line_weights(points, 2)
@@ -338,7 +297,6 @@
     wt7, wt3 = weights(p), weights(q)
     columns = np.zeros((256, 128))
     columns[:, 0:3] = wt7
-    columns[:96, 3:6] = scat.T @ wt7
     columns[:64, 6:9] = wt3
     columns[:, 9] = np.kron(np.tile(fine[1], 2), np.tile(fine[1], 2))
     plain["columns"] = (columns, F32)
@@ -350,7 +308,6 @@
     la = np.concatenate(three(jf.T @ k7, jf.T @ w7, 2), 0)
     ra = side_by_side(blocks(w7 @ jf, ez), blocks(k7 @ jf, ez))
     pair["la"] = la
-    pair["lar"] = la @ scat
     pair["bzra"] = bz @ ra
     pair["jxy"] = np.kron(blocks(jf.T, 2), blocks(jf.T, 2))
     pair["jz"] = blocks(jf, ez)
@@ -360,6 +317,7 @@
     plain["wz7"] = (np.tile(np.tile(fine[1], ez)[None], (8, 1)), F32)
     pair["lp"] = np.concatenate(three(k7 @ jf, w7 @ jf, 2), 0)
     pair["rp"] = side_by_side(blocks((w7 @ jf).T, ez), blocks((k7 @ jf).T, ez))
+    pair["bzrp"] = z_back(s3[1:-1], q, ez) @ pair["rp"]
     pair["pxy"] = np.kron(blocks(jf, 2), blocks(jf, 2))
     pair["pz"] = blocks(jf.T, ez)
 
@@ -385,11 +343,6 @@
     plain["s64"] = (spread(p), BF)
     plain["s32"] = (spread(q), BF)
     plain["s256"] = (corner_columns(np.ones((1, 2)), ez), BF)
-    grid = grid_elements(modes)
-    li = np.array([l7[x % modes] for x in range(2 * modes) for y in range(2 * modes)])
-    lj = np.array([l7[y % modes] for x in range(2 * modes) for y in range(2 * modes)])
-    pair["ld7"] = factor_rows(grid, [li, lj, None])
-    plain["le7"] = (factor_rows(grid, [None, None, np.ones(len(grid))]), BF)
     plain["s80"] = (spread(modes), BF)
     pair["sl80"] = spread(modes) * np.tile(l7, ez)[None]
 
@@ -474,7 +427,7 @@
     for row in range(144):
         (ex, cx), (ey, cy) = divmod(row // 12, 2), divmod(row % 12, 2)
         vx, vy = ex + cx, ey + cy
-        column = ((vy // 2) * 4 + AHEAD.index(vx // 2 - 1)) * 8 + (vx % 2) * 2 + vy % 2
+        column = (AHEAD.index(vx // 2 - 1) * 4 + vy // 2) * 8 + (vx % 2) * 2 + vy % 2
         spread_vertices[row, column] = 1
         for d in range(3):
             at = order.index((ex // 2 - 1, ey // 2 - 1))
@@ -498,7 +451,7 @@
             for ix, ahead in enumerate(AHEAD):
                 for x in range(2):
                     for y in range(2):
-                        table[:, iy, ix, x * 2 + y] = np.kron(
+                        table[:, ix, iy, x * 2 + y] = np.kron(
                             left[span(dx), (ahead + 1) * 2 + x], right[span(dy), iy * 2 + y]
                         )
         return table.reshape(64, 128)
@@ -549,16 +502,13 @@
 
 
 STAGES = (
+    ("columns", "vo", "jxy", "jz", "s80", "sl80", "e7", "e3", "e1", "s64", "s32", "s256", "wz7", "chosen", "mask"),
+    ("ld9", "le9", "vl", "vr", "az", "vb", "la", "bzra"),
+    ("ld3", "le3", "s48", "sl48", "er"),
     (
-        "columns", "wo", "jxy", "jz", "s80", "sl80", "ld7", "le7", "e7", "e3", "e1", "s64", "s32", "s256",
-        "wz7", "chosen", "mask",
+        "wmo", "jl", "rj", "bz", "k7", "kz7", "wmn", "azm", "lb", "rb", "left", "bm", "bzm", "select",
+        "rk3", "k3", "wl", "ra3", "ev", "ef", "cz", "s16", "jc", "rcj", "rp", "bzrp", "lp", "pxy", "pz",
     ),
-    ("wh", "az", "bf", "bo", "la", "bzra", "ld3", "le3", "s48", "sl48", "er", "lar"),
-    (
-        "wmo", "jl", "rj", "scat", "bz", "k7", "kz7", "wmn", "azm", "lb", "rb", "left", "bm", "bzm", "select",
-        "rk3", "k3", "wl", "ra3", "ev", "ef", "cz", "s16", "jc", "rcj", "rp", "lp", "pxy", "pz",
-    ),
-    ("ld9", "le9", "vo", "vl", "vr", "vb"),
 )
 
 
@@ -648,10 +598,9 @@
 
 
 KEPT = {
-    "fine_f": (768, 128), "mid_f": (192, 128), "low_f": (48, 256), "ring_f": (1728, 128), "inverse7": (400, 128),
-    "inverse3": (576, 128), "wt7": (256, 128), "wr7": (96, 128), "wt3": (64, 128), "base_mid": (64, 128),
-    "base_low": (16, 256), "local": (256, 128), "first_fine": (256, 128), "base_fine": (256, 128),
-    "first_mid": (64, 128), "modal": (400, 128), "modal3": (576, 128), "own_part": (192, 128), "base_ring": (576, 128),
+    "fine_f": (768, 128), "mid_f": (192, 128), "low_f": (48, 256), "ring_f": (1728, 128), "inverse3": (576, 128), "wt7": (256, 128), "wt3": (64, 128), "base_mid": (64, 128),
+    "base_low": (16, 256), "first_fine": (256, 128), "base_fine": (256, 128),
+    "first_mid": (64, 128), "modal3": (576, 128), "base_ring": (576, 128),
     "ww7": (256, 128), "inverse9": (1600, 128), "corner_f": (432, 128), "modal9": (1600, 128),
 }
 
@@ -663,8 +612,8 @@
     out_fine, out_mid, out_low = refs[3 + count : 6 + count]
     stores = refs[6 + count : 6 + 2 * count]
     (
-        r_ref, len_ref, inv_ref, rs, fs, hb1, fb1, rm, fm, rp, fp, hb2, hs1, hs2, st1, corner, held, gs, gb, cb,
-        send_sem, recv_sem, gsend, grecv, csend, crecv, in_sem, table_sem,
+        r_ref, len_ref, inv_ref, rs, fs, hb1, rm, fm, rp, fp, hb2, hs1, hs2, corner, held, gs, gb, cb, invs,
+        send_sem, recv_sem, gsend, grecv, csend, crecv, isend, irecv, in_sem, table_sem,
     ) = refs[6 + 2 * count : -len(KEPT)]
     gx, gy = lax.axis_index("gx"), lax.axis_index("gy")
     last = n_gy - 1
@@ -686,9 +635,6 @@
     greet(1, gy)
     greet(-1, gy)
     greet(2, gy)
-    greet_if(gy + 1, 2)
-    greet_if(gy - 1, 2)
-    greet_if(gy + 2, 1, 2)
     for row in range(n_gy):
         @pl.when((row < gy - 1) | (row > gy + 1))
         def _():
@@ -764,8 +710,7 @@
     def clear(number):
         first, end = GROUPS[number]
         for buffer, rows in (
-            (fs, BLOCK_ROWS), (hb1, FACE_ROWS), (fb1, FACE_ROWS), (rp, BLOCK_ROWS),
-            (fp, BLOCK_ROWS), (hb2, WIDE_ROWS),
+            (fs, BLOCK_ROWS), (hb1, WIDE_ROWS), (rp, BLOCK_ROWS), (fp, BLOCK_ROWS), (hb2, WIDE_ROWS),
         ):
             at = offsets(rows)
             buffer[at[first] : at[end], :] = jnp.zeros((at[end] - at[first], buffer.shape[1]), buffer.dtype)
@@ -773,28 +718,16 @@
     @pl.when(at_bottom)
     def _():
         clear(1)
-        cb[0:32, :] = jnp.zeros((32, 128), F32)
+        invs[0:32, :] = jnp.zeros((32, invs.shape[1]), BF)
 
     @pl.when(at_top)
     def _():
         clear(2)
-        cb[64:96, :] = jnp.zeros((32, 128), F32)
+        invs[64:96, :] = jnp.zeros((32, invs.shape[1]), BF)
 
     @pl.when(gy >= last - 1)
     def _():
-        cb[96:128, :] = jnp.zeros((32, 128), F32)
-
-    def halo(field, stage):
-        at = offsets(FACE_ROWS)
-        for index, (tx, ty) in enumerate(RING):
-            xs, ys = (14, 0)[tx < 0], (14, 0)[ty < 0]
-            if ty == 0:
-                layers = field[xs, :, :], field[xs + 1, :, :]
-            elif tx == 0:
-                layers = field[:, ys, :], field[:, ys + 1, :]
-            else:
-                layers = field[xs : xs + 2, ys, :], field[xs : xs + 2, ys + 1, :]
-            stage[at[index] : at[index + 1], :] = tall(jnp.concatenate(layers, 1), at[index + 1] - at[index])
+        invs[96:128, :] = jnp.zeros((32, invs.shape[1]), BF)
 
     at_wide = offsets(WIDE_ROWS)
 
@@ -826,10 +759,6 @@
         turned_back = [pltpu.roll(piece.astype(F32), 64, 1).astype(BF) for piece in pieces]
         return tall(jnp.concatenate(pieces + turned_back, 0), 768)
 
-    def unfold(buffer):
-        packed_rows = tall(buffer[...], 128)
-        return jnp.concatenate([packed_rows, pltpu.roll(packed_rows, 64, 1)], 0)
-
     def fold(block):
         result = block[0:16]
         for part in range(1, 4):
@@ -844,7 +773,6 @@
                     slot * 16 : slot * 16 + 16
                 ]
 
-    at_face = offsets(FACE_ROWS)
 
     inputs[0].wait()
     own_f = 8 * 16
@@ -855,12 +783,29 @@
         fs[own_f + 8 + ex * 2 : own_f + 10 + ex * 2, :] = wide(a * b / (2.0 * c))
     fs[own_f + 12 : own_f + 16, :] = jnp.zeros((4, 128), F32)
     inputs[1].wait()
-    halo(r_ref, hs1)
-    near = jnp.minimum(gy + 1, last) - jnp.maximum(gy - 2, 0) + 1
-    pl.semaphore_wait(barrier, 2 * n_gy - 1 + 2 * near)
-    exchange(1, lambda index: hs1.at[pl.ds(at_face[index], FACE_ROWS[index])], hb1, FACE_ROWS)
+    wide_halo(r_ref, hs1)
+    near = jnp.minimum(gy + 1, last) - jnp.maximum(gy - 1, 0) + 1
+    pl.semaphore_wait(barrier, 2 * n_gy + near)
     exchange(0, lambda index: fs.at[pl.ds(own_f, 16)], fs, BLOCK_ROWS)
+    exchange(1, lambda index: hs1.at[pl.ds(at_wide[index], WIDE_ROWS[index])], hb1, WIDE_ROWS)
     fetch(1, 2)
+    inputs[2].wait()
+    invs[32:64, :] = inv_ref[0]
+    reach = ((1, 0, not_top, not_bottom), (-1, 2, not_bottom, not_top), (-2, 3, gy > 1, gy < last - 1))
+
+    def inverse_copy(at):
+        step, slot, _, _ = reach[at]
+        return pltpu.make_async_remote_copy(
+            src_ref=invs.at[pl.ds(32, 32)],
+            dst_ref=invs.at[pl.ds(slot * 32, 32)],
+            send_sem=isend.at[at],
+            recv_sem=irecv.at[at],
+            device_id=(gx, gy + step),
+            device_id_type=MESH,
+        )
+
+    for at in range(3):
+        pl.when(reach[at][2])(lambda: inverse_copy(at).start())
 
     bottom_on = jnp.where(at_bottom, 1.0, 0.0)
     top_on = jnp.where(at_top, 1.0, 0.0)
@@ -873,53 +818,48 @@
         return piece[:, at : at + 1] + bottom_on * piece[:, at + 1 : at + 2] + top_on * piece[:, at + 2 : at + 3]
 
     wt7 = keep("wt7", jnp.broadcast_to(wall_weight(256, 0), (256, 128)))
-    wr7 = keep("wr7", jnp.broadcast_to(wall_weight(96, 3), (96, 128)))
     wt3 = keep("wt3", jnp.broadcast_to(wall_weight(64, 6), (64, 128)))
     ww7 = keep("ww7", jnp.broadcast_to(columns[:, 9:10], (256, 128)))
     r = wide(r_ref[...].reshape(256, 64))
     f_own = wide(fs[own_f : own_f + 16, :])
-    d7 = left3(t["ld7"], right2(f_own, t["s80"])) + left2(t["le7"], right3(f_own, t["sl80"]))
-    inverse7 = keep("inverse7", jnp.where(d7 > 0.0, 1.0 / jnp.where(d7 > 0.0, d7, 1.0), 0.0))
-    modal = keep("modal", left3(t["wo"], r))
+    modal9 = keep("modal9", left3(t["vo"], r))
     base_mid = keep("base_mid", right3(left3(t["jxy"], r), t["jz"]))
     fine_f = keep("fine_f", left2(t["e7"], right2(f_own, t["s64"])))
     mid_f = keep("mid_f", left2(t["e3"], right2(f_own, t["s32"])))
     low_f = keep("low_f", left2(t["e1"], right2(f_own, t["s256"])))
 
-    def fine_back(modal, buffer, stage, phase):
-        modal = right3(modal, t["az"]) * inverse7[...]
-        stage[...] = left3(t["bf"], modal)
-        exchange(phase, lambda index: stage.at[pl.ds(at_face[index], FACE_ROWS[index])], buffer, FACE_ROWS)
-        return left3(t["bo"], modal)
+    def ring_modes(buffer):
+        modal = jnp.concatenate(
+            [
+                modal9[0:800] + dot(t["vl"][...], side_values(buffer, LOW_SIDE)),
+                modal9[800:1600] + dot(t["vr"][...], side_values(buffer, HIGH_SIDE)),
+            ],
+            0,
+        )
+        return right3(modal, t["az"]) * inverse9[...]
 
     ready(1)
-    settle(1, recv_sem, hb1, FACE_ROWS)
-    modal = modal[...] + left3(t["wh"], unfold(hb1))
     fetch(3)
-    local = keep("local", fine_back(modal, fb1, st1, 2) * wt7[...])
-    own_part = keep("own_part", jnp.concatenate(terms3(t["la"], right3(local[...], t["bzra"])), 0))
     settle(0, recv_sem, fs, BLOCK_ROWS)
-    ring_f = wide(fs[...])
-    d3 = left3(t["ld3"], right2(ring_f, t["s48"])) + left2(t["le3"], right3(ring_f, t["sl48"]))
-    inverse3 = keep("inverse3", jnp.where(d3 > 0.0, 1.0 / jnp.where(d3 > 0.0, d3, 1.0), 0.0))
-    ring_f = keep("ring_f", left2(t["er"], right2(ring_f, t["s32"])))
-
-    settle(2, recv_sem, fb1, FACE_ROWS)
-    faces = wide(fb1[...]) * wr7[...]
-    face_part = terms3(t["lar"], right3(faces, t["bzra"]))
-    residual_mid = base_mid[...] - (
-        mid_f[0:64] * (own_part[0:64] + face_part[0])
-        + mid_f[64:128] * (own_part[64:128] + face_part[1])
-        + mid_f[128:192] * (own_part[128:192] + face_part[2])
-    )
+    ring_l = wide(fs[...])
+    d9 = left3(t["ld9"], right2(ring_l, t["s80"])) + left2(t["le9"], right3(ring_l, t["sl80"]))
+    inverse9 = keep("inverse9", jnp.where(d9 > 0.0, 1.0 / d9, 0.0))
+    settle(1, recv_sem, hb1, WIDE_ROWS)
+    local = left3(t["vb"], ring_modes(hb1)) * wt7[...]
+    terms = terms3(t["la"], right3(local, t["bzra"]))
+    residual_mid = base_mid[...] - (mid_f[0:64] * terms[0] + mid_f[64:128] * terms[1] + mid_f[128:192] * terms[2])
     rp[128:144, :] = fold(residual_mid)
     exchange(3, lambda index: rp.at[pl.ds(128, 16)], rp, BLOCK_ROWS)
     rm[512:576, :] = residual_mid
 
     ready(2)
+    ready(3)
+    ring_l = wide(fs[...])
+    d3 = left3(t["ld3"], right2(ring_l, t["s48"])) + left2(t["le3"], right3(ring_l, t["sl48"]))
+    inverse3 = keep("inverse3", jnp.where(d3 > 0.0, 1.0 / d3, 0.0))
     own_modal = keep("modal3", left3(t["wmo"], residual_mid))
     base_low = keep("base_low", right3(left3(t["jl"], residual_mid), t["rj"]))
-    first_fine = keep("first_fine", right3(local[...] + left2(t["scat"], faces), t["bz"]))
+    first_fine = keep("first_fine", right3(local, t["bz"]))
     massed = left3(t["k7"], first_fine[...] * t["wz7"][...][0:1])
     along_z = right3(first_fine[...], t["kz7"]) * ww7[...]
     base_fine = keep(
@@ -944,74 +884,62 @@
     message = halves(dot(t["left"].piece(0, wall, 16), jnp.concatenate(split(low), 1)))[0:8]
     gs[...] = message
 
-    def send_slab(step, ahead):
-        slot = step + jnp.where(ahead == 0, -1, n_gy - 1)
+    def send_slab(flips, ahead):
+        row = gy
+        for bit in (8, 4, 2, 1):
+            if flips & bit:
+                row = row + bit * (1 - 2 * (gy // bit % 2))
         pltpu.make_async_remote_copy(
             src_ref=gs,
-            dst_ref=gb.at[slot],
+            dst_ref=gb.at[flips + (n_gy - 1 if ahead else -1)],
             send_sem=gsend,
             recv_sem=grecv,
-            device_id=(lax.rem(gx + ahead, n_gx), lax.rem(gy + step, n_gy)),
+            device_id=(lax.rem(gx + ahead, n_gx), row),
             device_id_type=MESH,
         ).start()
 
-    for step in range(1, n_gy):
-        send_slab(step, 0)
-    for step in range(n_gy):
-        send_slab(step, 1)
+    for flips in (12, 13, 10, 11, 14, 15, 8, 9, 4, 5, 2, 3, 6, 7, 1, 0):
+        if flips < n_gy:
+            send_slab(flips, 1)
+            if flips:
+                send_slab(flips, 0)
 
     first_mid = keep("first_mid", right3(left3(t["bm"], modal3) * wt3[...], t["bzm"]))
     fm[512:576, :] = first_mid[...]
     fp[128:144, :] = fold(first_mid[...])
     exchange(4, lambda index: fp.at[pl.ds(128, 16)], fp, BLOCK_ROWS)
 
+    for at in range(3):
+        pl.when(reach[at][3])(lambda: inverse_copy(at).wait_recv())
     pltpu.make_async_copy(gb, gb, grecv).wait()
     here = gs[...] + jnp.sum(gb[0 : n_gy - 1], axis=0)
     behind = jnp.sum(gb[n_gy - 1 :], axis=0)
-    inputs[2].wait()
     chunks = inv_ref.shape[2] // 128
     vector = here + pltpu.roll(behind, 4, 0)
     row = lax.broadcasted_iota(jnp.int32, (8, 128), 0)
     vector = jnp.concatenate([jnp.where(row == chunk, vector, 0.0) for chunk in range(chunks)], 1)
     vector = tall(vector, 16).astype(BF)
-    inverse = tall(inv_ref[0], 128)
-    solved = lax.dot_general(vector, inverse, (((1,), (1,)), ((), ())), preferred_element_type=F32)
-    solved = jnp.sum(solved, axis=0, keepdims=True)
-    solved = jnp.broadcast_to(solved, (8, 128)) * t["chosen"][...]
-    own_c = (4 + 3) * 8
-    cb[own_c : own_c + 8, :] = solved
-
-    def send_correction(iy):
-        def action():
-            for ix, ahead in enumerate(AHEAD):
-                if (ahead, iy - 1) != (0, 0):
-                    pltpu.make_async_remote_copy(
-                        src_ref=cb.at[pl.ds(own_c, 8)],
-                        dst_ref=cb.at[pl.ds((iy * 4 + ix) * 8, 8)],
-                        send_sem=csend.at[iy],
-                        recv_sem=crecv.at[iy],
-                        device_id=(lax.rem(gx - ahead + n_gx, n_gx), gy - (iy - 1)),
-                        device_id_type=MESH,
-                    ).start()
-
-        return action
-
-    to_group = (not_top, None, not_bottom, gy > 1)
-    from_group = (not_bottom, None, not_top, gy < last - 1)
+    solved = lax.dot_general(vector, invs[...], (((1,), (1,)), ((), ())), preferred_element_type=F32)
+    solved = jnp.broadcast_to(jnp.sum(solved, axis=0, keepdims=True), (8, 128))
+    chosen = t["chosen"][...]
     for iy in range(4):
-        guarded(to_group[iy], send_correction(iy))
-
-    def settle_corrections(sems, conditions):
-        for iy in range(4):
-            piece = cb.at[pl.ds(iy * 32, 24 if iy == 1 else 32)]
-            guarded(conditions[iy], lambda: pltpu.make_async_copy(piece, piece, sems.at[iy]).wait())
-
-    ready(3)
+        cb[96 + iy * 8 : 104 + iy * 8, :] = (pltpu.roll(solved, 128 - iy * 32, 1) if iy else solved) * chosen
+    for ix in (2, 1, 0):
+        pltpu.make_async_remote_copy(
+            src_ref=cb.at[pl.ds(96, 32)],
+            dst_ref=cb.at[pl.ds(ix * 32, 32)],
+            send_sem=csend,
+            recv_sem=crecv,
+            device_id=(lax.rem(gx - AHEAD[ix] + n_gx, n_gx), gy),
+            device_id_type=MESH,
+        ).start()
+
+    others = cb.at[pl.ds(0, 96)]
+
     ring_l = wide(fs[...])
-    d9 = left3(t["ld9"], right2(ring_l, t["s80"])) + left2(t["le9"], right3(ring_l, t["sl80"]))
-    inverse9 = keep("inverse9", jnp.where(d9 > 0.0, 1.0 / jnp.where(d9 > 0.0, d9, 1.0), 0.0))
+    ring_f = keep("ring_f", left2(t["er"], right2(ring_l, t["s32"])))
     corner_f = keep("corner_f", left2(t["ef"], right2(ring_l, t["s16"])))
-    low_out = right2(tall(solved, 16), t["select"])
+    low_out = right2(tall(cb[104:112, :], 16), t["select"])
     out_low[0] = low_out[0:2, 0:8]
     out_low[1] = low_out[2:4, 0:8]
     settle(4, recv_sem, fp, BLOCK_ROWS)
@@ -1032,17 +960,16 @@
     modal3 = left3(t["wmn"], base_ring[0:512]) + left3(t["wmo"], base_ring[512:576])
     modal3 = keep("modal3", right3(modal3, t["azm"]))
 
-    settle_corrections(crecv, from_group)
+    pltpu.make_async_copy(others, others, crecv).wait()
     corrections = wide(cb[...])
     change = left2(t["ev"], right2(corrections, t["cz"]))
     change = right3(jnp.concatenate([change * corner_f[at * 144 : at * 144 + 144] for at in range(3)], 0), t["ra3"])
     change = jnp.concatenate([change[0:288, 0:128], change[288:432, 128:256]], 0)
     modal3 = (modal3[...] - left3(t["wl"], change)) * inverse3[...]
     held[0:64, :] = first_mid[...] + right3(left3(t["jc"], corrections), t["rcj"])
-    mid_result = held[0:64, :] + right3(left3(t["bm"], modal3) * wt3[...], t["bzm"])
-
-    turned = right3(mid_result, t["rp"])
-    turned = terms3(t["lp"], turned)
+    smoothed = left3(t["bm"], modal3) * wt3[...]
+
+    turned = terms3(t["lp"], right3(smoothed, t["bzrp"]) + right3(held[0:64, :], t["rp"]))
     residual = base_fine[...] - (
         fine_f[0:256] * turned[0]
         + fine_f[256:512] * turned[1]
@@ -1051,29 +978,23 @@
     rs[...] = residual[:, 0:64].reshape(16, 16, 64)
     wide_halo(rs, hs2)
     exchange(5, lambda index: hs2.at[pl.ds(at_wide[index], WIDE_ROWS[index])], hb2, WIDE_ROWS)
+    mid_result = held[0:64, :] + right3(smoothed, t["bzm"])
     out_mid[...] = mid_result[:, 0:32].reshape(8, 8, 32)
-    modal9 = keep("modal9", dot(t["vo"][...], residual.astype(BF)))
+    modal9 = keep("modal9", dot(t["vo"][0], residual.astype(BF)))
     held[...] = first_fine[...] + right3(left3(t["pxy"], mid_result), t["pz"])
     settle(5, recv_sem, hb2, WIDE_ROWS)
-    modal = jnp.concatenate(
-        [
-            modal9[0:800] + dot(t["vl"][...], side_values(hb2, LOW_SIDE)),
-            modal9[800:1600] + dot(t["vr"][...], side_values(hb2, HIGH_SIDE)),
-        ],
-        0,
-    )
-    modal = right3(modal, t["az"]) * inverse9[...]
-    local = dot(t["vb"][...], tall(modal, 1664).astype(BF)) * wt7[...]
+    local = dot(t["vb"][0], tall(ring_modes(hb2), 1664).astype(BF)) * wt7[...]
     result = held[...] + right3(local, t["bz"])
     out_fine[...] = result[:, 0:64].reshape(16, 16, 64)
 
     for phase, buffer, rows in (
-        (0, fs, BLOCK_ROWS), (1, hb1, FACE_ROWS), (2, fb1, FACE_ROWS), (3, rp, BLOCK_ROWS),
-        (4, fp, BLOCK_ROWS), (5, hb2, WIDE_ROWS),
+        (0, fs, BLOCK_ROWS), (1, hb1, WIDE_ROWS), (3, rp, BLOCK_ROWS), (4, fp, BLOCK_ROWS), (5, hb2, WIDE_ROWS),
     ):
         settle(phase, send_sem, buffer, rows)
     pltpu.make_async_copy(gb, gb, gsend).wait()
-    settle_corrections(csend, to_group)
+    pltpu.make_async_copy(others, others, csend).wait()
+    for at in range(3):
+        pl.when(reach[at][2])(lambda: inverse_copy(at).wait_send())
 
 
 def hand_over(*refs):
@@ -1094,27 +1015,28 @@
         pltpu.VMEM(coarse_inverse.shape, BF),
         pltpu.VMEM((16, 16, 64), F32),
         pltpu.VMEM((144, 128), F32),
-        pltpu.VMEM((96, 128), F32),
-        pltpu.VMEM((96, 128), F32),
+        pltpu.VMEM((576, 128), BF),
         pltpu.VMEM((576, 128), F32),
         pltpu.VMEM((576, 128), F32),
         pltpu.VMEM((144, 128), F32),
         pltpu.VMEM((144, 128), F32),
         pltpu.VMEM((576, 128), BF),
-        pltpu.VMEM((96, 128), F32),
         pltpu.VMEM((576, 128), BF),
-        pltpu.VMEM((96, 128), F32),
+        pltpu.VMEM((576, 128), BF),
         pltpu.VMEM((64, 128), F32),
         pltpu.VMEM((256, 128), F32),
         pltpu.VMEM((8, 128), F32),
         pltpu.VMEM((2 * n_gy - 1, 8, 128), F32),
         pltpu.VMEM((128, 128), F32),
+        pltpu.VMEM((128, coarse_inverse.shape[2]), BF),
         pltpu.SemaphoreType.DMA((6, 3)),
         pltpu.SemaphoreType.DMA((6, 3)),
         pltpu.SemaphoreType.DMA,
         pltpu.SemaphoreType.DMA,
-        pltpu.SemaphoreType.DMA((4,)),
-        pltpu.SemaphoreType.DMA((4,)),
+        pltpu.SemaphoreType.DMA,
+        pltpu.SemaphoreType.DMA,
+        pltpu.SemaphoreType.DMA((3,)),
+        pltpu.SemaphoreType.DMA((3,)),
         pltpu.SemaphoreType.DMA((3,)),
         pltpu.SemaphoreType.DMA((len(keys),)),
     ]

time: 58.3 us -> 56.4 us (0.967)
  Pallas kernels: 57.5 us -> 55.6 us
    pallas_call x1, Pallas kernels: 55.9 us -> 53.9 us  [shards(): pl.pallas_call(functools.partial(cycle_kernel, keys, places, n_gx, n_gy),...]
where the time goes in v4:
time: 56.4 us; the launch traced here: 56.2 us
  Pallas kernels  55.6 us (99%)
  between operations  0.64 us (1%)
    pallas_call x1, Pallas kernels, shards(): pl.pallas_call(functools.partial(cycle_kernel, keys, places, n_gx, n_gy),...  53.9 us
    pallas_call x1, Pallas kernels, shards(): pl.pallas_call(hand_over, out_shape=tuple((jax.ShapeDtypeStruct(out.shape...  1.61 us

profile of v4, /device:TPU:1, one launch (start us, length us, event | category | flops | bytes accessed | tf_op | source)
XLA Modules:
  0.0 56.2 jit_solution(7285101223216293309)
XLA Ops:
  0.6 53.9 %shard_map.184 = (f32[16,16,64]{2,1,0:T(8,128)}, f32[8,8,32]{2,1,0:T(8,128)}, f32[2,2,8]{2,1,0:T(2,128)}) custom-call(f32[16,16,64]{2,1,0:T(8,128)} %refs_0_.1, f32[3,2,2,8]{3,2,1,0:T(2,128)} %refs_1_.1, bf16[1,32,512]{2,1,0:T(8,128)(2,1)} %refs_2_.1, f32[544,128]{1,0:T(8,128)} %constant.28.clone.refs_3_, bf16[4096,256]{1,0:T(8,128)(2,1)} %constant.29.clone.refs_4_, ...), custom_call_target="tpu_custom_call" | custom-call | tf_op jit(solution)/shard_map/pallas_call | solution.py:1044
  54.6 1.6 %shard_map.185 = (f32[16,16,64]{2,1,0:T(8,128)}, f32[8,8,32]{2,1,0:T(8,128)}, f32[2,2,8]{2,1,0:T(2,128)}) custom-call(f32[16,16,64]{2,1,0:T(8,128)} %get-tuple-element.6.refs_0_, f32[8,8,32]{2,1,0:T(8,128)} %get-tuple-element.7.refs_1_, f32[2,2,8]{2,1,0:T(2,128)} %get-tuple-element.8.refs_2_), custom_call_target="tpu_custom_call" | custom-call | tf_op jit(solution)/shard_map/pallas_call | solution.py:1056

commit v5 on v4

--- a/solution.py
+++ b/solution.py
@@ -158,7 +158,6 @@
 BLOCK_ROWS = (16,) * 8
 WIDE_ROWS = (80, 80, 80, 64, 64, 80, 64, 64)
 LOW_SIDE = ((-1, 0), (-1, -1), (-1, 1), (0, -1), (0, 1))
-HIGH_SIDE = ((1, 0), (1, -1), (1, 1), (0, -1), (0, 1))
 MESH = pl.DeviceIdType.MESH
 
 
@@ -264,29 +263,27 @@
     a1w = blocks(s7.T, 4) @ ext.reshape(count, 36)
     middle = a1w[:, 10:26]
     beside = {-1: a1w[:, 0:10], 1: a1w[:, 26:36]}
-    for name, group, rows in (("vl", LOW_SIDE, slice(0, 2 * modes)), ("vr", HIGH_SIDE, slice(2 * modes, None))):
-        parts = []
-        for half in range(2):
-            for dx, dy in group:
-                pieces = []
-                for at in range(half, 10, 2):
-                    if dy == 0:
-                        pieces.append(np.kron(beside[dx][rows, at : at + 1], middle))
-                    elif dx == 0:
-                        pieces.append(np.kron(middle[rows], beside[dy][:, at : at + 1]))
-                    else:
-                        pieces.append(np.kron(beside[dx][rows], beside[dy][:, at : at + 1]))
-                piece = np.concatenate(pieces, 1)
-                parts.append(np.pad(piece, ((0, 0), (0, -piece.shape[1] % 16))))
-        plain[name] = (np.concatenate(parts, 1), BF)
-    pair["vo"] = np.kron(middle, middle)
+    near, parts = slice(0, 2 * modes), []
+    for half in range(2):
+        for dx, dy in LOW_SIDE:
+            if dy == 0:
+                pieces = [np.kron(beside[dx][near, at : at + 1], middle) for at in range(half, 10, 2)]
+            elif dx == 0:
+                columns = range(15, 7, -1) if half else range(8)
+                pieces = [np.kron(middle[near][:, columns], beside[dy][:, at : at + 1]) for at in range(10)]
+            else:
+                pieces = [np.kron(beside[dx][near], beside[dy][:, at : at + 1]) for at in range(half, 10, 2)]
+            piece = np.concatenate(pieces, 1)
+            parts.append(np.pad(piece, ((0, 0), (0, -piece.shape[1] % 16))))
+    plain["vl"] = (np.concatenate(parts, 1), BF)
+    pair["vo"] = np.kron(middle[near], middle)
     raw = blocks(inner, 4)
     around = np.array(raw[p : 3 * p])
     for at in (p - 1, 2 * p - 1, 3 * p - 1):
         for row in (at, at + 1):
             if p <= row < 3 * p:
                 around[row - p] = raw[at] + raw[at + 1]
-    pair["vb"] = np.kron(around, around)
+    pair["vb"] = np.kron(around[:, near], around)
 
     def weights(points):
         line = line_weights(points, 2)
@@ -397,6 +394,7 @@
     for x in range(count):
         for y in range(count):
             ex, ey = x // modes + 1, y // modes + 1
+            ex = ex if ex < 3 else 7 - ex
             ld9[x * count + y, ring_row(ex, ey, 0)] = l7[x % modes]
             ld9[x * count + y, ring_row(ex, ey, 1)] = l7[y % modes]
             le9[x * count + y, ring_row(ex, ey, 2)] = 1
@@ -503,7 +501,7 @@
 
 STAGES = (
     ("columns", "vo", "jxy", "jz", "s80", "sl80", "e7", "e3", "e1", "s64", "s32", "s256", "wz7", "chosen", "mask"),
-    ("ld9", "le9", "vl", "vr", "az", "vb", "la", "bzra"),
+    ("ld9", "le9", "vl", "az", "vb", "la", "bzra"),
     ("ld3", "le3", "s48", "sl48", "er"),
     (
         "wmo", "jl", "rj", "bz", "k7", "kz7", "wmn", "azm", "lb", "rb", "left", "bm", "bzm", "select",
@@ -601,7 +599,7 @@
     "fine_f": (768, 128), "mid_f": (192, 128), "low_f": (48, 256), "ring_f": (1728, 128), "inverse3": (576, 128), "wt7": (256, 128), "wt3": (64, 128), "base_mid": (64, 128),
     "base_low": (16, 256), "first_fine": (256, 128), "base_fine": (256, 128),
     "first_mid": (64, 128), "modal3": (576, 128), "base_ring": (576, 128),
-    "ww7": (256, 128), "inverse9": (1600, 128), "corner_f": (432, 128), "modal9": (1600, 128),
+    "ww7": (256, 128), "inverse9": (1600, 128), "corner_f": (432, 128), "modal9": (800, 256),
 }
 
 
@@ -612,7 +610,7 @@
     out_fine, out_mid, out_low = refs[3 + count : 6 + count]
     stores = refs[6 + count : 6 + 2 * count]
     (
-        r_ref, len_ref, inv_ref, rs, fs, hb1, rm, fm, rp, fp, hb2, hs1, hs2, corner, held, gs, gb, cb, invs,
+        r_ref, len_ref, inv_ref, rs, fs, hb1, rm, fm, rp, fp, hb2, hs1, hs2, rb, corner, held, gs, gb, cb, invs,
         send_sem, recv_sem, gsend, grecv, csend, crecv, isend, irecv, in_sem, table_sem,
     ) = refs[6 + 2 * count : -len(KEPT)]
     gx, gy = lax.axis_index("gx"), lax.axis_index("gy")
@@ -731,33 +729,43 @@
 
     at_wide = offsets(WIDE_ROWS)
 
+    def mirrored(values):
+        return jnp.concatenate([values[(15 - x) * 16 : (16 - x) * 16] for x in range(16)], 0)
+
     def wide_halo(field, stage):
+        for x in range(16):
+            rb[x] = field[15 - x]
         for index, (tx, ty) in enumerate(RING):
-            xs, ys = (6, 0)[tx < 0], (6, 0)[ty < 0]
+            source, ys = (rb if tx < 0 else field), (6, 0)[ty < 0]
             if 0 not in (tx, ty):
                 corner[48:64, :] = jnp.zeros((16, 128), F32)
             for pair in range(5):
-                xa, ya = xs + 2 * pair, ys + 2 * pair
+                xa, ya = 6 + 2 * pair, ys + 2 * pair
                 at = at_wide[index] + pair * 16
                 if ty == 0:
-                    layers = field[xa, :, :], field[xa + 1, :, :]
+                    layers = source[xa, :, :], source[xa + 1, :, :]
                     stage[at : at + 16, :] = jnp.concatenate(layers, 1).astype(stage.dtype)
                 elif tx == 0:
-                    layers = field[:, ya, :], field[:, ya + 1, :]
-                    stage[at : at + 16, :] = jnp.concatenate(layers, 1).astype(stage.dtype)
+                    rows = [jnp.concatenate([field[0:8, y, :], rb[0:8, y, :]], 1) for y in (ya, ya + 1)]
+                    stage[at : at + 16, :] = jnp.concatenate(rows, 0).astype(stage.dtype)
                 else:
-                    layers = field[xs : xs + 10, ya, :], field[xs : xs + 10, ya + 1, :]
+                    layers = source[6:16, ya, :], source[6:16, ya + 1, :]
                     corner[pair * 10 : pair * 10 + 10, :] = jnp.concatenate(layers, 1)
             if 0 not in (tx, ty):
                 stage[at_wide[index] : at_wide[index + 1], :] = corner[...].astype(stage.dtype)
 
-    def side_values(buffer, group):
-        pieces = []
-        for direction in group:
-            index = RING.index(direction)
-            pieces.append(buffer[at_wide[index] : at_wide[index + 1], :])
-        turned_back = [pltpu.roll(piece.astype(F32), 64, 1).astype(BF) for piece in pieces]
-        return tall(jnp.concatenate(pieces + turned_back, 0), 768)
+    def side_values(buffer):
+        plain, turned_back = {}, {}
+        for index, direction in enumerate(RING):
+            piece = buffer[at_wide[index] : at_wide[index + 1], :]
+            plain[direction] = piece
+            turned_back[direction] = pltpu.roll(piece.astype(F32), 64, 1).astype(BF)
+        ends, flanks = LOW_SIDE[:3], LOW_SIDE[3:]
+        opposite = [(-dx, dy) for dx, dy in ends]
+        low_part = [plain[d] for d in ends + flanks] + [turned_back[d] for d in ends + flanks]
+        high_part = [plain[d] for d in opposite] + [turned_back[d] for d in flanks]
+        high_part += [turned_back[d] for d in opposite] + [plain[d] for d in flanks]
+        return jnp.concatenate([tall(jnp.concatenate(part, 0), 768) for part in (low_part, high_part)], 1)
 
     def fold(block):
         result = block[0:16]
@@ -822,21 +830,19 @@
     ww7 = keep("ww7", jnp.broadcast_to(columns[:, 9:10], (256, 128)))
     r = wide(r_ref[...].reshape(256, 64))
     f_own = wide(fs[own_f : own_f + 16, :])
-    modal9 = keep("modal9", left3(t["vo"], r))
+    modal9 = keep("modal9", left3(t["vo"], jnp.concatenate([r, mirrored(r)], 1)))
     base_mid = keep("base_mid", right3(left3(t["jxy"], r), t["jz"]))
     fine_f = keep("fine_f", left2(t["e7"], right2(f_own, t["s64"])))
     mid_f = keep("mid_f", left2(t["e3"], right2(f_own, t["s32"])))
     low_f = keep("low_f", left2(t["e1"], right2(f_own, t["s256"])))
 
     def ring_modes(buffer):
-        modal = jnp.concatenate(
-            [
-                modal9[0:800] + dot(t["vl"][...], side_values(buffer, LOW_SIDE)),
-                modal9[800:1600] + dot(t["vr"][...], side_values(buffer, HIGH_SIDE)),
-            ],
-            0,
-        )
-        return right3(modal, t["az"]) * inverse9[...]
+        modal = modal9[...] + dot(t["vl"][...], side_values(buffer))
+        modal = right3(jnp.concatenate([modal[:, 0:128], modal[:, 128:256]], 0), t["az"]) * inverse9[...]
+        return jnp.concatenate([modal[0:800], modal[800:1600]], 1)
+
+    def joined(values):
+        return values[:, 0:128] + mirrored(values[:, 128:256])
 
     ready(1)
     fetch(3)
@@ -845,7 +851,7 @@
     d9 = left3(t["ld9"], right2(ring_l, t["s80"])) + left2(t["le9"], right3(ring_l, t["sl80"]))
     inverse9 = keep("inverse9", jnp.where(d9 > 0.0, 1.0 / d9, 0.0))
     settle(1, recv_sem, hb1, WIDE_ROWS)
-    local = left3(t["vb"], ring_modes(hb1)) * wt7[...]
+    local = joined(left3(t["vb"], ring_modes(hb1))) * wt7[...]
     terms = terms3(t["la"], right3(local, t["bzra"]))
     residual_mid = base_mid[...] - (mid_f[0:64] * terms[0] + mid_f[64:128] * terms[1] + mid_f[128:192] * terms[2])
     rp[128:144, :] = fold(residual_mid)
@@ -980,10 +986,10 @@
     exchange(5, lambda index: hs2.at[pl.ds(at_wide[index], WIDE_ROWS[index])], hb2, WIDE_ROWS)
     mid_result = held[0:64, :] + right3(smoothed, t["bzm"])
     out_mid[...] = mid_result[:, 0:32].reshape(8, 8, 32)
-    modal9 = keep("modal9", dot(t["vo"][0], residual.astype(BF)))
+    modal9 = keep("modal9", dot(t["vo"][0], jnp.concatenate([residual, mirrored(residual)], 1).astype(BF)))
     held[...] = first_fine[...] + right3(left3(t["pxy"], mid_result), t["pz"])
     settle(5, recv_sem, hb2, WIDE_ROWS)
-    local = dot(t["vb"][0], tall(ring_modes(hb2), 1664).astype(BF)) * wt7[...]
+    local = joined(dot(t["vb"][0], tall(ring_modes(hb2), 896).astype(BF))) * wt7[...]
     result = held[...] + right3(local, t["bz"])
     out_fine[...] = result[:, 0:64].reshape(16, 16, 64)
 
@@ -1023,6 +1029,7 @@
         pltpu.VMEM((576, 128), BF),
         pltpu.VMEM((576, 128), BF),
         pltpu.VMEM((576, 128), BF),
+        pltpu.VMEM((16, 16, 64), F32),
         pltpu.VMEM((64, 128), F32),
         pltpu.VMEM((256, 128), F32),
         pltpu.VMEM((8, 128), F32),

time: 56.4 us -> 55.6 us (0.986)
  Pallas kernels: 55.6 us -> 54.8 us
    pallas_call x1, Pallas kernels: 53.9 us -> 53.2 us  [shards(): pl.pallas_call(functools.partial(cycle_kernel, keys, places, n_gx, n_gy),...]
where the time goes in v5:
time: 55.6 us; the launch traced here: 55.5 us
  Pallas kernels  54.8 us (99%)
  between operations  0.64 us (1%)
    pallas_call x1, Pallas kernels, shards(): pl.pallas_call(functools.partial(cycle_kernel, keys, places, n_gx, n_gy),...  53.2 us
    pallas_call x1, Pallas kernels, shards(): pl.pallas_call(hand_over, out_shape=tuple((jax.ShapeDtypeStruct(out.shape...  1.61 us

profile of v5, /device:TPU:1, one launch (start us, length us, event | category | flops | bytes accessed | tf_op | source)
XLA Modules:
  0.0 55.5 jit_solution(4441846094335209878)
XLA Ops:
  0.6 53.2 %shard_map.184 = (f32[16,16,64]{2,1,0:T(8,128)}, f32[8,8,32]{2,1,0:T(8,128)}, f32[2,2,8]{2,1,0:T(2,128)}) custom-call(f32[16,16,64]{2,1,0:T(8,128)} %refs_0_.1, f32[3,2,2,8]{3,2,1,0:T(2,128)} %refs_1_.1, bf16[1,32,512]{2,1,0:T(8,128)(2,1)} %refs_2_.1, f32[544,128]{1,0:T(8,128)} %constant.28.clone.refs_3_, bf16[2496,256]{1,0:T(8,128)(2,1)} %constant.29.clone.refs_4_, ...), custom_call_target="tpu_custom_call" | custom-call | tf_op jit(solution)/shard_map/pallas_call | solution.py:1051
  53.9 1.6 %shard_map.185 = (f32[16,16,64]{2,1,0:T(8,128)}, f32[8,8,32]{2,1,0:T(8,128)}, f32[2,2,8]{2,1,0:T(2,128)}) custom-call(f32[16,16,64]{2,1,0:T(8,128)} %get-tuple-element.6.refs_0_, f32[8,8,32]{2,1,0:T(8,128)} %get-tuple-element.7.refs_1_, f32[2,2,8]{2,1,0:T(2,128)} %get-tuple-element.8.refs_2_), custom_call_target="tpu_custom_call" | custom-call | tf_op jit(solution)/shard_map/pallas_call | solution.py:1063

commit v6 on v5

--- a/solution.py
+++ b/solution.py
@@ -398,10 +398,8 @@
             ld9[x * count + y, ring_row(ex, ey, 0)] = l7[x % modes]
             ld9[x * count + y, ring_row(ex, ey, 1)] = l7[y % modes]
             le9[x * count + y, ring_row(ex, ey, 2)] = 1
-    pair["ld9"] = ld9
-    plain["le9"] = (le9, BF)
-    pair["ld3"] = ld3
-    plain["le3"] = (le3, BF)
+    pair["ld9"] = ld9 + le9
+    pair["ld3"] = ld3 + le3
     plain["s48"] = (spread(m3), BF)
     pair["sl48"] = spread(m3) * np.tile(l3, ez)[None]
     er = np.zeros((3, 9, 2 * q, 2 * q, 144))
@@ -501,8 +499,8 @@
 
 STAGES = (
     ("columns", "vo", "jxy", "jz", "s80", "sl80", "e7", "e3", "e1", "s64", "s32", "s256", "wz7", "chosen", "mask"),
-    ("ld9", "le9", "vl", "az", "vb", "la", "bzra"),
-    ("ld3", "le3", "s48", "sl48", "er"),
+    ("ld9", "vl", "az", "vb", "la", "bzra"),
+    ("ld3", "s48", "sl48", "er"),
     (
         "wmo", "jl", "rj", "bz", "k7", "kz7", "wmn", "azm", "lb", "rb", "left", "bm", "bzm", "select",
         "rk3", "k3", "wl", "ra3", "ev", "ef", "cz", "s16", "jc", "rcj", "rp", "bzrp", "lp", "pxy", "pz",
@@ -628,16 +626,26 @@
             for ahead in columns:
                 greet(ahead, row)
 
-    greet_if(gy + 1, 0, 1, -1)
-    greet_if(gy - 1, 0, 1, -1)
+    def other_row(flips):
+        row = gy
+        for bit in (8, 4, 2, 1):
+            if flips & bit:
+                row = row + bit * (1 - 2 * (gy // bit % 2))
+        return row
+
+    def greet_rows(*several):
+        for flips in several:
+            if flips < n_gy:
+                greet(-1, other_row(flips))
+                if flips:
+                    greet(0, other_row(flips))
+
+    greet_rows(12, 13, 10, 11, 14, 15, 8, 9)
+    greet_if(gy + 1, 1)
+    greet_if(gy - 1, 1)
     greet(1, gy)
-    greet(-1, gy)
     greet(2, gy)
-    for row in range(n_gy):
-        @pl.when((row < gy - 1) | (row > gy + 1))
-        def _():
-            greet(0, row)
-            greet(-1, row)
+    greet_rows(4, 5, 2, 3, 6, 7, 1, 0)
     inputs = [
         pltpu.make_async_copy(source, target, in_sem.at[at])
         for at, (source, target) in enumerate(((len_hbm, len_ref), (r_hbm, r_ref), (inv_hbm, inv_ref)))
@@ -848,7 +856,8 @@
     fetch(3)
     settle(0, recv_sem, fs, BLOCK_ROWS)
     ring_l = wide(fs[...])
-    d9 = left3(t["ld9"], right2(ring_l, t["s80"])) + left2(t["le9"], right3(ring_l, t["sl80"]))
+    kind = lax.broadcasted_iota(jnp.int32, (144, 128), 0) % 16 // 4
+    d9 = left3(t["ld9"], jnp.where(kind == 2, right3(ring_l, t["sl80"]), right2(ring_l, t["s80"])))
     inverse9 = keep("inverse9", jnp.where(d9 > 0.0, 1.0 / d9, 0.0))
     settle(1, recv_sem, hb1, WIDE_ROWS)
     local = joined(left3(t["vb"], ring_modes(hb1))) * wt7[...]
@@ -861,7 +870,7 @@
     ready(2)
     ready(3)
     ring_l = wide(fs[...])
-    d3 = left3(t["ld3"], right2(ring_l, t["s48"])) + left2(t["le3"], right3(ring_l, t["sl48"]))
+    d3 = left3(t["ld3"], jnp.where(kind == 2, right3(ring_l, t["sl48"]), right2(ring_l, t["s48"])))
     inverse3 = keep("inverse3", jnp.where(d3 > 0.0, 1.0 / d3, 0.0))
     own_modal = keep("modal3", left3(t["wmo"], residual_mid))
     base_low = keep("base_low", right3(left3(t["jl"], residual_mid), t["rj"]))
@@ -891,10 +900,7 @@
     gs[...] = message
 
     def send_slab(flips, ahead):
-        row = gy
-        for bit in (8, 4, 2, 1):
-            if flips & bit:
-                row = row + bit * (1 - 2 * (gy // bit % 2))
+        row = other_row(flips)
         pltpu.make_async_remote_copy(
             src_ref=gs,
             dst_ref=gb.at[flips + (n_gy - 1 if ahead else -1)],

time: 55.6 us -> 55.6 us (level)
  no operation moved by 1% of the time
where the time goes in v6:
time: 55.6 us; the launch traced here: 55.4 us
  Pallas kernels  54.8 us (99%)
  between operations  0.64 us (1%)
    pallas_call x1, Pallas kernels, shards(): pl.pallas_call(functools.partial(cycle_kernel, keys, places, n_gx, n_gy),...  53.2 us
    pallas_call x1, Pallas kernels, shards(): pl.pallas_call(hand_over, out_shape=tuple((jax.ShapeDtypeStruct(out.shape...  1.61 us

profile of v6, /device:TPU:1, one launch (start us, length us, event | category | flops | bytes accessed | tf_op | source)
XLA Modules:
  0.0 55.4 jit_solution(3056910987703556719)
XLA Ops:
  0.6 53.2 %shard_map.184 = (f32[16,16,64]{2,1,0:T(8,128)}, f32[8,8,32]{2,1,0:T(8,128)}, f32[2,2,8]{2,1,0:T(2,128)}) custom-call(f32[16,16,64]{2,1,0:T(8,128)} %refs_0_.1, f32[3,2,2,8]{3,2,1,0:T(2,128)} %refs_1_.1, bf16[1,32,512]{2,1,0:T(8,128)(2,1)} %refs_2_.1, f32[544,128]{1,0:T(8,128)} %constant.28.clone.refs_3_, bf16[2496,256]{1,0:T(8,128)(2,1)} %constant.29.clone.refs_4_, ...), custom_call_target="tpu_custom_call" | custom-call | tf_op jit(solution)/shard_map/pallas_call | solution.py:1057
  53.8 1.6 %shard_map.185 = (f32[16,16,64]{2,1,0:T(8,128)}, f32[8,8,32]{2,1,0:T(8,128)}, f32[2,2,8]{2,1,0:T(2,128)}) custom-call(f32[16,16,64]{2,1,0:T(8,128)} %get-tuple-element.6.refs_0_, f32[8,8,32]{2,1,0:T(8,128)} %get-tuple-element.7.refs_1_, f32[2,2,8]{2,1,0:T(2,128)} %get-tuple-element.8.refs_2_), custom_call_target="tpu_custom_call" | custom-call | tf_op jit(solution)/shard_map/pallas_call | solution.py:1069

commit v7 on v6

--- a/solution.py
+++ b/solution.py
@@ -683,7 +683,7 @@
         else:
             pl.when(condition)(action)
 
-    def exchange(phase, source, buffer, rows):
+    def exchange(phase, source, buffer, rows, numbers=(1, 2, 0)):
         at = offsets(rows)
 
         def group(number):
@@ -703,7 +703,7 @@
 
             return action
 
-        for number in (1, 2, 0):
+        for number in numbers:
             guarded(sent[number], group(number))
 
     def settle(phase, sems, buffer, rows):
@@ -802,8 +802,9 @@
     wide_halo(r_ref, hs1)
     near = jnp.minimum(gy + 1, last) - jnp.maximum(gy - 1, 0) + 1
     pl.semaphore_wait(barrier, 2 * n_gy + near)
-    exchange(0, lambda index: fs.at[pl.ds(own_f, 16)], fs, BLOCK_ROWS)
-    exchange(1, lambda index: hs1.at[pl.ds(at_wide[index], WIDE_ROWS[index])], hb1, WIDE_ROWS)
+    for numbers in ((1, 2), (0,)):
+        exchange(1, lambda index: hs1.at[pl.ds(at_wide[index], WIDE_ROWS[index])], hb1, WIDE_ROWS, numbers)
+        exchange(0, lambda index: fs.at[pl.ds(own_f, 16)], fs, BLOCK_ROWS, numbers)
     fetch(1, 2)
     inputs[2].wait()
     invs[32:64, :] = inv_ref[0]

time: 55.6 us -> 56.4 us (1.014)
  Pallas kernels: 54.8 us -> 55.6 us
    pallas_call x1, Pallas kernels: 53.2 us -> 53.9 us  [shards(): pl.pallas_call(functools.partial(cycle_kernel, keys, places, n_gx, n_gy),...]
where the time goes in v7:
time: 56.4 us; the launch traced here: 56.2 us
  Pallas kernels  55.6 us (99%)
  between operations  0.64 us (1%)
    pallas_call x1, Pallas kernels, shards(): pl.pallas_call(functools.partial(cycle_kernel, keys, places, n_gx, n_gy),...  53.9 us
    pallas_call x1, Pallas kernels, shards(): pl.pallas_call(hand_over, out_shape=tuple((jax.ShapeDtypeStruct(out.shape...  1.61 us

profile of v7, /device:TPU:1, one launch (start us, length us, event | category | flops | bytes accessed | tf_op | source)
XLA Modules:
  0.0 56.2 jit_solution(16964035313982742394)
XLA Ops:
  0.6 53.9 %shard_map.184 = (f32[16,16,64]{2,1,0:T(8,128)}, f32[8,8,32]{2,1,0:T(8,128)}, f32[2,2,8]{2,1,0:T(2,128)}) custom-call(f32[16,16,64]{2,1,0:T(8,128)} %refs_0_.1, f32[3,2,2,8]{3,2,1,0:T(2,128)} %refs_1_.1, bf16[1,32,512]{2,1,0:T(8,128)(2,1)} %refs_2_.1, f32[544,128]{1,0:T(8,128)} %constant.28.clone.refs_3_, bf16[2496,256]{1,0:T(8,128)(2,1)} %constant.29.clone.refs_4_, ...), custom_call_target="tpu_custom_call" | custom-call | tf_op jit(solution)/shard_map/pallas_call | solution.py:1058
  54.6 1.6 %shard_map.185 = (f32[16,16,64]{2,1,0:T(8,128)}, f32[8,8,32]{2,1,0:T(8,128)}, f32[2,2,8]{2,1,0:T(2,128)}) custom-call(f32[16,16,64]{2,1,0:T(8,128)} %get-tuple-element.6.refs_0_, f32[8,8,32]{2,1,0:T(8,128)} %get-tuple-element.7.refs_1_, f32[2,2,8]{2,1,0:T(2,128)} %get-tuple-element.8.refs_2_), custom_call_target="tpu_custom_call" | custom-call | tf_op jit(solution)/shard_map/pallas_call | solution.py:1070
